TPU v7x, 32 devices: a whole 2x2x4 slice. The times are simulated.
32 devices in a mesh: layer: 4 (over y, core), phi: 8 (over z, x).
Axes of the slice: x: 2, y: 2, z: 4, core: 2. Of those that a mesh axis runs over, the one named last changes fastest.
Arguments:
- hit_features: bfloat16 [4, 8, 1024, 128], P('layer', 'phi'), may hold values from -6 to 6
- edge_features: bfloat16 [4, 8, 4, 1024, 128], P('layer', 'phi'), may hold values from -6 to 6
- sender_slot: int32 [4, 8, 4, 1024], P('layer', 'phi'), may hold values from 0 to 1023
- receiver_slot: int32 [4, 8, 4, 1024], P('layer', 'phi'), may hold values from 0 to 1023
- edge_count: int32 [4, 8, 4], P('layer', 'phi'), may hold values from 0 to 1024, as said below
- grad_hits: bfloat16 [4, 8, 1024, 128], P('layer', 'phi'), may hold values from -6 to 6
- grad_edges: bfloat16 [4, 8, 4, 1024, 128], P('layer', 'phi'), may hold values from -6 to 6
- w_edge_in: bfloat16 [384, 128], replicated, may hold values from -0.3125 to 0.3125
- w_edge_out: bfloat16 [128, 128], replicated, may hold values from -0.5 to 0.5
- w_node_in: bfloat16 [256, 128], replicated, may hold values from -0.375 to 0.375
- w_node_out: bfloat16 [128, 128], replicated, may hold values from -0.5 to 0.5
Outputs:
- hit_grads: float32 [4, 8, 1024, 128], P('layer', 'phi')
- edge_grads: bfloat16 [4, 8, 4, 1024, 128], P('layer', 'phi')
- edge_in_grad: float32 [384, 128], replicated
- edge_out_grad: float32 [128, 128], replicated
- node_in_grad: float32 [256, 128], replicated
- node_out_grad: float32 [128, 128], replicated
Inputs may be any that keep to these rules, and one draw needn't show every extreme that they name: `edge_count`: live slots come first in each block. Kind 0 edges have their sender in the same shard, kind 1 in the previous layer group, kind 2 in the previous phi sector, kind 3 in the next one (phi closes into a loop). Kind 1 has no live slots in layer group 0. Some block is full in every draw. `sender_slot`: rows of dead slots are arbitrary. `receiver_slot`: rows of dead slots are arbitrary.
All inputs are finite; a program needn't handle non-finite values.
Results may differ from a plain program's by a relative error of at most 0.009.
Values may be sent and summed in bfloat16 or wider, within the bound.
No kernel may reach another device: no remote copies, remote signals or barrier semaphores. Data moves between devices by JAX's collectives and lax.ppermute only.
A program may use at most 64 MiB of HBM per device.

v0:
```python
import functools

import jax
import jax.numpy as jnp
from jax import lax
from jax.experimental import pallas as pl
from jax.experimental.pallas import tpu as pltpu
from jax.sharding import PartitionSpec as P

norm_eps = 1e-05
bf16, f32 = jnp.bfloat16, jnp.float32
TILE = 256
VMEM_BYTES = 56 * 1024 * 1024


def shifted(value, axis, steps, ring):
    count = lax.axis_size(axis)
    if ring:
        route = [(i, (i + steps) % count) for i in range(count)]
    else:
        route = [(i, i + steps) for i in range(count) if 0 <= i + steps < count]
    return lax.ppermute(value, axis, route)


def dot(a, b):
    return jnp.dot(a, b, preferred_element_type=f32)


def dot_nt(a, b):
    return lax.dot_general(a, b, (((1,), (1,)), ((), ())), preferred_element_type=f32)


def dot_tn(a, b):
    return lax.dot_general(a, b, (((0,), (0,)), ((), ())), preferred_element_type=f32)


def halves(x):
    upper = x.astype(bf16)
    return upper, (x - upper.astype(f32)).astype(bf16)


def row_select(idx_row, nodes):
    edges = idx_row.shape[1]
    col = jnp.broadcast_to(idx_row, (128, edges)).T
    lane = lax.broadcasted_iota(jnp.int32, (edges, 128), 1)
    parts = [jnp.where(col == lane + c * 128, 1.0, 0.0).astype(bf16) for c in range(nodes // 128)]
    return jnp.concatenate(parts, axis=1)


def col_select(idx_row, nodes):
    edges = idx_row.shape[1]
    place = lax.broadcasted_iota(jnp.int32, (nodes, edges), 0)
    return jnp.where(place == idx_row, 1.0, 0.0).astype(bf16)


def normed(pre):
    centred = pre - jnp.mean(pre, axis=-1, keepdims=True)
    rstd = lax.rsqrt(jnp.mean(centred * centred, axis=-1, keepdims=True) + norm_eps)
    return centred * rstd, rstd


def gate(u):
    return 1.0 / (1.0 + jnp.exp(-u))


def normed_back(u, rstd, sig, upstream):
    du = upstream * (sig * (1.0 + u * (1.0 - sig)))
    mean_du = jnp.mean(du, axis=-1, keepdims=True)
    mean_duu = jnp.mean(du * u, axis=-1, keepdims=True)
    return rstd * (du - mean_du - u * mean_duu)


def live_rows(offset, count, shape):
    return offset + lax.broadcasted_iota(jnp.int32, shape, 0) < count


def idx_tile(ref, k, offset):
    return ref[k : k + 1, pl.ds(offset, TILE)]


def loop_tiles(count, step):
    def looped(i, carry):
        step(pl.multiple_of(i * TILE, TILE))
        return carry

    lax.fori_loop(0, (count + TILE - 1) // TILE, looped, 0)


def finish_forward(pre, offset, count, recv_row, nodes, u_ref, rs_ref, total_ref):
    u, rstd = normed(pre)
    u_ref[pl.ds(offset, TILE), :] = u
    rs_ref[pl.ds(offset, TILE), :] = jnp.broadcast_to(rstd, u.shape)
    hidden = jnp.where(live_rows(offset, count, u.shape), u * gate(u), 0.0).astype(bf16)
    total_ref[...] += dot(col_select(recv_row, nodes), hidden)


def first_kernel(counts, send, recv, hit, edges, w_in, part, u0, rs0, total):
    nodes, d = hit.shape
    kinds = send.shape[0]
    total[...] = jnp.zeros_like(total)
    for k in range(kinds):

        def step(offset, k=k):
            recv_row = idx_tile(recv, k, offset)
            rows = dot(row_select(recv_row, nodes), hit[...]).astype(bf16)
            pre = dot(rows, w_in[d : 2 * d, :]) + dot(
                edges[k, pl.ds(offset, TILE), :], w_in[2 * d :, :]
            )
            if k == 0:
                rows = dot(row_select(idx_tile(send, k, offset), nodes), hit[...]).astype(bf16)
                pre += dot(rows, w_in[:d, :])
                finish_forward(pre, offset, counts[k], recv_row, nodes, u0, rs0, total)
            else:
                part[k - 1, pl.ds(offset, TILE), :] = pre

        loop_tiles(counts[k], step)


def second_kernel(
    counts, send, recv, hit, src1, src2, src3, edges, grad_hit, grad_edge,
    w_in, w_out, wn_in, wn_out, part, u0, rs0, total0,
    back1, back2, back3, edge_done, hit_done, weights,
    u_s, rs_s, total, recv_sum, send_sum, inc_grad,
):
    nodes, d = hit.shape
    kinds = send.shape[0]
    sources = (hit, src1, src2, src3)
    us = (u0,) + tuple(u_s.at[k] for k in range(kinds - 1))
    rss = (rs0,) + tuple(rs_s.at[k] for k in range(kinds - 1))
    total[...] = total0[...]
    edge_done[...] = grad_edge[...]
    for k in range(1, kinds):

        def step(offset, k=k):
            rows = dot(row_select(idx_tile(send, k, offset), nodes), sources[k][...]).astype(bf16)
            pre = part[k - 1, pl.ds(offset, TILE), :] + dot(rows, w_in[:d, :])
            recv_row = idx_tile(recv, k, offset)
            finish_forward(pre, offset, counts[k], recv_row, nodes, us[k], rss[k], total)

        loop_tiles(counts[k], step)
    upper, lower = halves(total[...])
    incoming = (dot(upper, w_out[...]) + dot(lower, w_out[...])).astype(bf16)
    u, rstd = normed(dot(hit[...], wn_in[:d, :]) + dot(incoming, wn_in[d:, :]))
    sig = gate(u)
    hidden = (u * sig).astype(bf16)
    hidden_grad = dot_nt(grad_hit[...], wn_out[...])
    pre_grad = normed_back(u, rstd, sig, hidden_grad).astype(bf16)
    weights[6 * d : 7 * d, :] = dot_tn(hidden, grad_hit[...])
    weights[4 * d : 5 * d, :] = dot_tn(hit[...], pre_grad)
    weights[5 * d : 6 * d, :] = dot_tn(incoming, pre_grad)
    hit_done[...] = grad_hit[...].astype(f32) + dot_nt(pre_grad, wn_in[:d, :])
    upper, lower = halves(dot_nt(pre_grad, wn_in[d:, :]))
    inc_grad[:, :d] = upper
    inc_grad[:, d:] = lower
    recv_sum[...] = jnp.zeros_like(recv_sum)
    weights[: 4 * d, :] = jnp.zeros((4 * d, d), f32)
    for k in (*range(1, kinds), 0):
        send_sum[...] = jnp.zeros_like(send_sum)

        def step(offset, k=k):
            recv_row = idx_tile(recv, k, offset)
            picked = dot(row_select(recv_row, nodes), inc_grad[...])
            picked = picked[:, :d] + picked[:, d:]
            grad_rows = grad_edge[k, pl.ds(offset, TILE), :].astype(f32)
            live = live_rows(offset, counts[k], grad_rows.shape)
            message_grad = jnp.where(live, grad_rows + picked, 0.0).astype(bf16)
            hidden_grad = dot_nt(message_grad, w_out[...])
            u = us[k][pl.ds(offset, TILE), :]
            rstd = rss[k][pl.ds(offset, TILE), :]
            sig = gate(u)
            hidden = (u * sig).astype(bf16)
            pre_grad = normed_back(u, rstd, sig, hidden_grad).astype(bf16)
            edge_done[k, pl.ds(offset, TILE), :] = (
                grad_rows + dot_nt(pre_grad, w_in[2 * d :, :])
            ).astype(bf16)
            weights[2 * d : 3 * d, :] += dot_tn(edges[k, pl.ds(offset, TILE), :], pre_grad)
            weights[3 * d : 4 * d, :] += dot_tn(hidden, message_grad)
            recv_sum[...] += dot(col_select(recv_row, nodes), pre_grad)
            send_sum[...] += dot(col_select(idx_tile(send, k, offset), nodes), pre_grad)

        loop_tiles(counts[k], step)
        upper, lower = halves(send_sum[...])
        weights[:d, :] += dot_tn(sources[k][...], upper) + dot_tn(sources[k][...], lower)
        back = dot_nt(upper, w_in[:d, :]) + dot_nt(lower, w_in[:d, :])
        if k == 0:
            hit_done[...] += back
        else:
            (back1, back2, back3)[k - 1][...] = back.astype(bf16)
    upper, lower = halves(recv_sum[...])
    weights[d : 2 * d, :] = dot_tn(hit[...], upper) + dot_tn(hit[...], lower)
    hit_done[...] += dot_nt(upper, w_in[d : 2 * d, :]) + dot_nt(lower, w_in[d : 2 * d, :])


def on_device(kernel, outs, scratch, operands, flops):
    in_specs = [pl.BlockSpec(memory_space=pltpu.SMEM)]
    in_specs += [pl.BlockSpec(memory_space=pltpu.VMEM)] * (len(operands) - 1)
    return pl.pallas_call(
        kernel,
        out_shape=outs,
        in_specs=in_specs,
        out_specs=[pl.BlockSpec(memory_space=pltpu.VMEM)] * len(outs),
        scratch_shapes=scratch,
        compiler_params=pltpu.CompilerParams(vmem_limit_bytes=VMEM_BYTES),
        cost_estimate=pl.CostEstimate(flops=flops, bytes_accessed=4 << 20, transcendentals=1 << 20),
    )(*operands)


def all_summed(part, layers, sectors):
    axes = ("layer", "phi")
    total = layers * sectors
    if total & (total - 1) or layers < 2:
        return lax.psum(part, axes)

    def swap(value, mask):
        return lax.ppermute(value, axes, [(i, i ^ mask) for i in range(total)])

    rows, d = part.shape
    me = lax.axis_index("layer") % 2
    both = part.reshape(2, rows // 2, d)
    mine = lax.dynamic_index_in_dim(both, me, 0, False)
    other = lax.dynamic_index_in_dim(both, 1 - me, 0, False)
    mine = mine + swap(other.astype(bf16), sectors).astype(f32)
    bits = [1 << b for b in range(total.bit_length() - 1) if 1 << b != sectors]
    near = [1] + [b for b in bits if b > sectors]
    far = [b for b in bits if b not in near]
    ordered = far + near if len(far) % 2 == 0 else near + far
    for at in range(0, len(ordered), 2):
        pair = ordered[at : at + 2]
        masks = pair + [pair[0] ^ pair[1]] if len(pair) == 2 else pair
        sent = mine.astype(bf16)
        mine = sum((swap(sent, m).astype(f32) for m in masks), sent.astype(f32))
    mine = mine.astype(bf16)
    theirs = swap(mine, sectors)
    pair = jnp.where(me == 0, jnp.stack([mine, theirs]), jnp.stack([theirs, mine]))
    return pair.reshape(rows, d).astype(f32)


def body(
    hit_features, edge_features, sender_slot, receiver_slot, edge_count, grad_hits, grad_edges,
    w_edge_in, w_edge_out, w_node_in, w_node_out,
):
    hit = hit_features[0, 0]
    nodes, d = hit.shape
    edges, grad_edge = edge_features[0, 0], grad_edges[0, 0]
    send, recv, counts = sender_slot[0, 0], receiver_slot[0, 0], edge_count[0, 0]
    grad_hit = grad_hits[0, 0]
    kinds, cap = send.shape
    src1 = shifted(hit, "layer", 1, False)
    src2 = shifted(hit, "phi", 1, True)
    src3 = shifted(hit, "phi", -1, True)
    wide = jax.ShapeDtypeStruct((cap, d), f32)
    node_wide = jax.ShapeDtypeStruct((nodes, d), f32)
    part, u0, rs0, total0 = on_device(
        first_kernel,
        [jax.ShapeDtypeStruct((kinds - 1, cap, d), f32), wide, wide, node_wide],
        [],
        (counts, send, recv, hit, edges, w_edge_in),
        4 * 10**9,
    )
    back = jax.ShapeDtypeStruct((nodes, d), bf16)
    back1, back2, back3, edge_done, hit_done, weights = on_device(
        second_kernel,
        [
            back, back, back,
            jax.ShapeDtypeStruct(edges.shape, bf16),
            node_wide,
            jax.ShapeDtypeStruct((7 * d, d), f32),
        ],
        [
            pltpu.VMEM((kinds - 1, cap, d), f32),
            pltpu.VMEM((kinds - 1, cap, d), f32),
            pltpu.VMEM((nodes, d), f32),
            pltpu.VMEM((nodes, d), f32),
            pltpu.VMEM((nodes, d), f32),
            pltpu.VMEM((nodes, 2 * d), bf16),
        ],
        (counts, send, recv, hit, src1, src2, src3, edges, grad_hit, grad_edge,
         w_edge_in, w_edge_out, w_node_in, w_node_out, part, u0, rs0, total0),
        8 * 10**9,
    )
    layers, sectors = lax.axis_size("layer"), lax.axis_size("phi")
    from_upper = shifted(back1, "layer", -1, False).astype(f32)
    from_next = shifted(back2, "phi", -1, True).astype(f32)
    from_prev = shifted(back3, "phi", 1, True).astype(f32)
    summed = all_summed(weights, layers, sectors) / (layers * sectors)
    hit_total = hit_done + from_upper + (from_next + from_prev)
    return (
        hit_total[None, None],
        edge_done[None, None],
        summed[: 3 * d],
        summed[3 * d : 4 * d],
        summed[4 * d : 6 * d],
        summed[6 * d :],
    )


def solution(mesh):
    placed = (
        P("layer", "phi", None, None),
        P("layer", "phi", None, None, None),
        P("layer", "phi", None, None),
        P("layer", "phi", None, None),
        P("layer", "phi", None),
        P("layer", "phi", None, None),
        P("layer", "phi", None, None, None),
        P(),
        P(),
        P(),
        P(),
    )
    return jax.shard_map(
        body,
        mesh=mesh,
        in_specs=placed,
        out_specs=(
            P("layer", "phi", None, None),
            P("layer", "phi", None, None, None),
            P(),
            P(),
            P(),
            P(),
        ),
        check_vma=False,
    )
```

profile of v0, /device:TPU:0, one launch (start us, length us, event | category | flops | bytes accessed | tf_op | source)
XLA Modules:
  0.0 90.3 jit_solution(8760403897707910637)
XLA Ops:
  0.6 2.4 %collective-permute-start = (bf16[1024,128]{1,0:T(8,128)(2,1)}, bf16[1024,128]{1,0:T(8,128)(2,1)S(1)}, u32[]{:S(2)}, u32[]{:S(2)}) collective-permute-start(bf16[1024,128]{1,0:T(8,128)(2,1)} %bitcast.30), channel_id=1, source_target_pairs={{0,8},{8,16},{16,24},{1,9},{9,17},{17,25},{2,10},{10,18},{18,26},{... | collective-permute-start | bytes 786440 | tf_op jit(solution)/shard_map/ppermute | solution.py:22
  3.0 2.4 %collective-permute-start.1 = (bf16[1024,128]{1,0:T(8,128)(2,1)}, bf16[1024,128]{1,0:T(8,128)(2,1)S(1)}, u32[]{:S(2)}, u32[]{:S(2)}) collective-permute-start(bf16[1024,128]{1,0:T(8,128)(2,1)} %bitcast.31), channel_id=1, source_target_pairs={{0,1},{1,2},{2,3},{3,4},{4,5},{5,6},{6,7},{7,0},{8,9},{9,10},{10,1... | collective-permute-start | bytes 786440 | tf_op jit(solution)/shard_map/ppermute | solution.py:22
  5.4 3.1 %collective-permute-start.2 = (bf16[1024,128]{1,0:T(8,128)(2,1)}, bf16[1024,128]{1,0:T(8,128)(2,1)S(1)}, u32[]{:S(2)}, u32[]{:S(2)}) collective-permute-start(bf16[1024,128]{1,0:T(8,128)(2,1)} %bitcast.32), channel_id=1, source_target_pairs={{0,7},{1,0},{2,1},{3,2},{4,3},{5,4},{6,5},{7,6},{8,15},{9,8},{10,9... | collective-permute-start | bytes 786440 | tf_op jit(solution)/shard_map/ppermute | solution.py:22
  8.5 11.1 %shard_map.154 = (f32[3,1024,128]{2,1,0:T(8,128)}, f32[1024,128]{1,0:T(8,128)}, f32[1024,128]{1,0:T(8,128)}, f32[1024,128]{1,0:T(8,128)}) custom-call(s32[4]{0:T(128)} %bitcast.40, s32[4,1024]{1,0:T(4,128)} %bitcast.36, s32[4,1024]{1,0:T(4,128)} %bitcast.38, bf16[1024,128]{1,0:T(8,128)(2,1)} %bitcast.33, bf16[4,1024,128]{2,1,0:T(8,128)(2,1)} %bitcast.27, ...), custom_call_target="tpu_custom_call" | custom-call | flops 4000000000 | bytes 4194304 | tf_op jit(solution)/shard_map/pallas_call | solution.py:197
  20.6 24.9 %shard_map.155 = (bf16[1024,128]{1,0:T(8,128)(2,1)}, bf16[1024,128]{1,0:T(8,128)(2,1)}, bf16[1024,128]{1,0:T(8,128)(2,1)}, bf16[4,1024,128]{2,1,0:T(8,128)(2,1)}...) custom-call(s32[4]{0:T(128)} %bitcast.41, s32[4,1024]{1,0:T(4,128)} %bitcast.37, s32[4,1024]{1,0:T(4,128)} %bitcast.39, ...), custom_call_target="tpu_custom_call" | custom-call | flops 8000000000 | bytes 4194304 | tf_op jit(solution)/shard_map/pallas_call | solution.py:197
  45.6 1.0 %fusion.1 = bf16[448,128]{1,0:T(8,128)(2,1)S(1)} fusion(f32[2,448,128]{2,1,0:T(8,128)} %bitcast.24, s32[]{:T(128)S(6)} %select_n.27), kind=kLoop, calls=%fused_computation.8 | loop fusion | bytes 229380 | tf_op jit(solution)/shard_map/convert_element_type | solution.py:222
  46.7 1.3 %collective-permute-done.6 = bf16[448,128]{1,0:T(8,128)(2,1)S(1)} collective-permute-done((bf16[448,128]{1,0:T(8,128)(2,1)S(1)}, bf16[448,128]{1,0:T(8,128)(2,1)S(1)}, u32[]{:S(2)}, u32[]{:S(2)}) %collective-permute-start.6) | collective-permute-done | bytes 114720 | tf_op jit(solution)/shard_map/ppermute | solution.py:215
  48.0 1.0 %fusion = bf16[448,128]{1,0:T(8,128)(2,1)S(1)} fusion(bf16[448,128]{1,0:T(8,128)(2,1)S(1)} %collective-permute-done.6, f32[2,448,128]{2,1,0:T(8,128)} %bitcast.25, s32[]{:T(128)S(6)} %select_n.26), kind=kLoop, calls=%fused_computation.4 | loop fusion | flops 172032 | bytes 458756 | tf_op jit(solution)/shard_map/convert_element_type | solution.py:230
  48.9 6.2 %collective-permute-start.9 = (bf16[448,128]{1,0:T(8,128)(2,1)S(1)}, bf16[448,128]{1,0:T(8,128)(2,1)S(1)}, u32[]{:S(2)}, u32[]{:S(2)}) collective-permute-start(bf16[448,128]{1,0:T(8,128)(2,1)S(1)} %fusion), channel_id=1, source_target_pairs={{0,6},{1,7},{2,4},{3,5},{4,2},{5,3},{6,0},{7,1},{8,14},{9,15},{10,... | collective-permute-start | bytes 344072 | tf_op jit(solution)/shard_map/ppermute | solution.py:215
  55.1 0.6 collective-permute-start.7
  55.8 3.4 %collective-permute-done.9 = bf16[448,128]{1,0:T(8,128)(2,1)S(1)} collective-permute-done((bf16[448,128]{1,0:T(8,128)(2,1)S(1)}, bf16[448,128]{1,0:T(8,128)(2,1)S(1)}, u32[]{:S(2)}, u32[]{:S(2)}) %collective-permute-start.9) | collective-permute-done | bytes 114720 | tf_op jit(solution)/shard_map/ppermute | solution.py:215
  59.2 6.1 %collective-permute-done.8 = bf16[448,128]{1,0:T(8,128)(2,1)S(1)} collective-permute-done((bf16[448,128]{1,0:T(8,128)(2,1)S(1)}, bf16[448,128]{1,0:T(8,128)(2,1)S(1)}, u32[]{:S(2)}, u32[]{:S(2)}) %collective-permute-start.8) | collective-permute-done | bytes 114720 | tf_op jit(solution)/shard_map/ppermute | solution.py:215
  65.4 4.9 %collective-permute-start.11 = (bf16[448,128]{1,0:T(8,128)(2,1)S(1)}, bf16[448,128]{1,0:T(8,128)(2,1)S(1)}, u32[]{:S(2)}, u32[]{:S(2)}) collective-permute-start(bf16[448,128]{1,0:T(8,128)(2,1)S(1)} %add_convert_fusion.1), channel_id=1, source_target_pairs={{0,16},{1,17},{2,18},{3,19},{4,20},{5,21},{6,22},{7,23},{8,24},{9,... | collective-permute-start | bytes 344072 | tf_op jit(solution)/shard_map/ppermute | solution.py:215
  70.3 0.9 collective-permute-start.10
  71.2 1.1 %collective-permute-start.5 = (bf16[1024,128]{1,0:T(8,128)(2,1)}, bf16[1024,128]{1,0:T(8,128)(2,1)S(1)}, u32[]{:S(2)}, u32[]{:S(2)}) collective-permute-start(bf16[1024,128]{1,0:T(8,128)(2,1)} %get-tuple-element.23), channel_id=1, source_target_pairs={{0,1},{1,2},{2,3},{3,4},{4,5},{5,6},{6,7},{7,0},{8,9},{9,10},{10,1... | collective-permute-start | bytes 786440 | tf_op jit(solution)/shard_map/ppermute | solution.py:22
  72.3 3.6 %collective-permute-start.4 = (bf16[1024,128]{1,0:T(8,128)(2,1)}, bf16[1024,128]{1,0:T(8,128)(2,1)S(1)}, u32[]{:S(2)}, u32[]{:S(2)}) collective-permute-start(bf16[1024,128]{1,0:T(8,128)(2,1)} %get-tuple-element.22), channel_id=1, source_target_pairs={{0,7},{1,0},{2,1},{3,2},{4,3},{5,4},{6,5},{7,6},{8,15},{9,8},{10,9... | collective-permute-start | bytes 786440 | tf_op jit(solution)/shard_map/ppermute | solution.py:22
  75.9 1.3 %collective-permute-start.3 = (bf16[1024,128]{1,0:T(8,128)(2,1)}, bf16[1024,128]{1,0:T(8,128)(2,1)S(1)}, u32[]{:S(2)}, u32[]{:S(2)}) collective-permute-start(bf16[1024,128]{1,0:T(8,128)(2,1)} %get-tuple-element.21), channel_id=1, source_target_pairs={{8,0},{16,8},{24,16},{9,1},{17,9},{25,17},{10,2},{18,10},{26,18},{... | collective-permute-start | bytes 786440 | tf_op jit(solution)/shard_map/ppermute | solution.py:22
  77.2 5.9 %collective-permute-done.10 = bf16[448,128]{1,0:T(8,128)(2,1)S(1)} collective-permute-done((bf16[448,128]{1,0:T(8,128)(2,1)S(1)}, bf16[448,128]{1,0:T(8,128)(2,1)S(1)}, u32[]{:S(2)}, u32[]{:S(2)}) %collective-permute-start.10) | collective-permute-done | bytes 114720 | tf_op jit(solution)/shard_map/ppermute | solution.py:215
  83.3 1.1 %collective-permute-done.5 = bf16[1024,128]{1,0:T(8,128)(2,1)S(1)} collective-permute-done((bf16[1024,128]{1,0:T(8,128)(2,1)}, bf16[1024,128]{1,0:T(8,128)(2,1)S(1)}, u32[]{:S(2)}, u32[]{:S(2)}) %collective-permute-start.5) | collective-permute-done | bytes 262176 | tf_op jit(solution)/shard_map/ppermute | solution.py:22
  84.4 2.9 %collective-permute-done.4 = bf16[1024,128]{1,0:T(8,128)(2,1)S(1)} collective-permute-done((bf16[1024,128]{1,0:T(8,128)(2,1)}, bf16[1024,128]{1,0:T(8,128)(2,1)S(1)}, u32[]{:S(2)}, u32[]{:S(2)}) %collective-permute-start.4) | collective-permute-done | bytes 262176 | tf_op jit(solution)/shard_map/ppermute | solution.py:22
  87.3 0.9 add_bitcast_fusion
  88.2 0.7 slice.16
  88.9 0.7 fusion.2
  89.6 0.7 slice.18
  (23 shorter events, 1.4 us)
Async XLA Ops:
  0.6 19.0 %collective-permute-start = (bf16[1024,128]{1,0:T(8,128)(2,1)}, bf16[1024,128]{1,0:T(8,128)(2,1)S(1)}, u32[]{:S(2)}, u32[]{:S(2)}) collective-permute-start(bf16[1024,128]{1,0:T(8,128)(2,1)} %bitcast.30), channel_id=1, source_target_pairs={{0,8},{8,16},{16,24},{1,9},{9,17},{17,25},{2,10},{10,18},{18,26},{... | collective-permute-start | bytes 786440 | tf_op jit(solution)/shard_map/ppermute | solution.py:22
  3.0 16.6 %collective-permute-start.1 = (bf16[1024,128]{1,0:T(8,128)(2,1)}, bf16[1024,128]{1,0:T(8,128)(2,1)S(1)}, u32[]{:S(2)}, u32[]{:S(2)}) collective-permute-start(bf16[1024,128]{1,0:T(8,128)(2,1)} %bitcast.31), channel_id=1, source_target_pairs={{0,1},{1,2},{2,3},{3,4},{4,5},{5,6},{6,7},{7,0},{8,9},{9,10},{10,1... | collective-permute-start | bytes 786440 | tf_op jit(solution)/shard_map/ppermute | solution.py:22
  5.4 14.5 %collective-permute-start.2 = (bf16[1024,128]{1,0:T(8,128)(2,1)}, bf16[1024,128]{1,0:T(8,128)(2,1)S(1)}, u32[]{:S(2)}, u32[]{:S(2)}) collective-permute-start(bf16[1024,128]{1,0:T(8,128)(2,1)} %bitcast.32), channel_id=1, source_target_pairs={{0,7},{1,0},{2,1},{3,2},{4,3},{5,4},{6,5},{7,6},{8,15},{9,8},{10,9... | collective-permute-start | bytes 786440 | tf_op jit(solution)/shard_map/ppermute | solution.py:22
  19.6 0.7 copy-start.1
  19.6 0.8 copy-start.2
  19.9 0.7 copy-start.3
  45.6 41.7 %copy-start = (f32[1024,128]{1,0:T(8,128)S(1)}, f32[1024,128]{1,0:T(8,128)}, u32[]{:S(2)}) copy-start(f32[1024,128]{1,0:T(8,128)} %get-tuple-element.20) | copy-start | bytes 1572868
  46.6 1.4 %collective-permute-start.6 = (bf16[448,128]{1,0:T(8,128)(2,1)S(1)}, bf16[448,128]{1,0:T(8,128)(2,1)S(1)}, u32[]{:S(2)}, u32[]{:S(2)}) collective-permute-start(bf16[448,128]{1,0:T(8,128)(2,1)S(1)} %fusion.1), channel_id=1, source_target_pairs={{0,8},{1,9},{2,10},{3,11},{4,12},{5,13},{6,14},{7,15},{8,0},{9,1},... | collective-permute-start | bytes 344072 | tf_op jit(solution)/shard_map/ppermute | solution.py:215
  48.9 10.3 %collective-permute-start.9 = (bf16[448,128]{1,0:T(8,128)(2,1)S(1)}, bf16[448,128]{1,0:T(8,128)(2,1)S(1)}, u32[]{:S(2)}, u32[]{:S(2)}) collective-permute-start(bf16[448,128]{1,0:T(8,128)(2,1)S(1)} %fusion), channel_id=1, source_target_pairs={{0,6},{1,7},{2,4},{3,5},{4,2},{5,3},{6,0},{7,1},{8,14},{9,15},{10,... | collective-permute-start | bytes 344072 | tf_op jit(solution)/shard_map/ppermute | solution.py:215
  55.1 10.1 %collective-permute-start.8 = (bf16[448,128]{1,0:T(8,128)(2,1)S(1)}, bf16[448,128]{1,0:T(8,128)(2,1)S(1)}, u32[]{:S(2)}, u32[]{:S(2)}) collective-permute-start(bf16[448,128]{1,0:T(8,128)(2,1)S(1)} %fusion), channel_id=1, source_target_pairs={{0,4},{1,5},{2,6},{3,7},{4,0},{5,1},{6,2},{7,3},{8,12},{9,13},{10,... | collective-permute-start | bytes 344072 | tf_op jit(solution)/shard_map/ppermute | solution.py:215
  55.1 10.1 %collective-permute-start.7 = (bf16[448,128]{1,0:T(8,128)(2,1)S(1)}, bf16[448,128]{1,0:T(8,128)(2,1)S(1)}, u32[]{:S(2)}, u32[]{:S(2)}) collective-permute-start(bf16[448,128]{1,0:T(8,128)(2,1)S(1)} %fusion), channel_id=1, source_target_pairs={{0,2},{1,3},{2,0},{3,1},{4,6},{5,7},{6,4},{7,5},{8,10},{9,11},{10,... | collective-permute-start | bytes 344072 | tf_op jit(solution)/shard_map/ppermute | solution.py:215
  65.3 10.6 %collective-permute-start.12 = (bf16[448,128]{1,0:T(8,128)(2,1)S(1)}, bf16[448,128]{1,0:T(8,128)(2,1)S(1)}, u32[]{:S(2)}, u32[]{:S(2)}) collective-permute-start(bf16[448,128]{1,0:T(8,128)(2,1)S(1)} %add_convert_fusion.1), channel_id=1, source_target_pairs={{0,17},{1,16},{2,19},{3,18},{4,21},{5,20},{6,23},{7,22},{8,25},{9,... | collective-permute-start | bytes 344072 | tf_op jit(solution)/shard_map/ppermute | solution.py:215
  65.4 11.8 %collective-permute-start.11 = (bf16[448,128]{1,0:T(8,128)(2,1)S(1)}, bf16[448,128]{1,0:T(8,128)(2,1)S(1)}, u32[]{:S(2)}, u32[]{:S(2)}) collective-permute-start(bf16[448,128]{1,0:T(8,128)(2,1)S(1)} %add_convert_fusion.1), channel_id=1, source_target_pairs={{0,16},{1,17},{2,18},{3,19},{4,20},{5,21},{6,22},{7,23},{8,24},{9,... | collective-permute-start | bytes 344072 | tf_op jit(solution)/shard_map/ppermute | solution.py:215
  70.3 12.8 %collective-permute-start.10 = (bf16[448,128]{1,0:T(8,128)(2,1)S(1)}, bf16[448,128]{1,0:T(8,128)(2,1)S(1)}, u32[]{:S(2)}, u32[]{:S(2)}) collective-permute-start(bf16[448,128]{1,0:T(8,128)(2,1)S(1)} %add_convert_fusion.1), channel_id=1, source_target_pairs={{0,1},{1,0},{2,3},{3,2},{4,5},{5,4},{6,7},{7,6},{8,9},{9,8},{10,11... | collective-permute-start | bytes 344072 | tf_op jit(solution)/shard_map/ppermute | solution.py:215
  71.2 13.2 %collective-permute-start.5 = (bf16[1024,128]{1,0:T(8,128)(2,1)}, bf16[1024,128]{1,0:T(8,128)(2,1)S(1)}, u32[]{:S(2)}, u32[]{:S(2)}) collective-permute-start(bf16[1024,128]{1,0:T(8,128)(2,1)} %get-tuple-element.23), channel_id=1, source_target_pairs={{0,1},{1,2},{2,3},{3,4},{4,5},{5,6},{6,7},{7,0},{8,9},{9,10},{10,1... | collective-permute-start | bytes 786440 | tf_op jit(solution)/shard_map/ppermute | solution.py:22
  72.3 15.0 %collective-permute-start.4 = (bf16[1024,128]{1,0:T(8,128)(2,1)}, bf16[1024,128]{1,0:T(8,128)(2,1)S(1)}, u32[]{:S(2)}, u32[]{:S(2)}) collective-permute-start(bf16[1024,128]{1,0:T(8,128)(2,1)} %get-tuple-element.22), channel_id=1, source_target_pairs={{0,7},{1,0},{2,1},{3,2},{4,3},{5,4},{6,5},{7,6},{8,15},{9,8},{10,9... | collective-permute-start | bytes 786440 | tf_op jit(solution)/shard_map/ppermute | solution.py:22
  75.9 11.4 %collective-permute-start.3 = (bf16[1024,128]{1,0:T(8,128)(2,1)}, bf16[1024,128]{1,0:T(8,128)(2,1)S(1)}, u32[]{:S(2)}, u32[]{:S(2)}) collective-permute-start(bf16[1024,128]{1,0:T(8,128)(2,1)} %get-tuple-element.21), channel_id=1, source_target_pairs={{8,0},{16,8},{24,16},{9,1},{17,9},{25,17},{10,2},{18,10},{26,18},{... | collective-permute-start | bytes 786440 | tf_op jit(solution)/shard_map/ppermute | solution.py:22
  83.2 5.0 %collective-permute-start.13 = (bf16[448,128]{1,0:T(8,128)(2,1)S(1)}, bf16[448,128]{1,0:T(8,128)(2,1)S(1)}, u32[]{:S(2)}, u32[]{:S(2)}) collective-permute-start(bf16[448,128]{1,0:T(8,128)(2,1)S(1)} %add_convert_fusion), channel_id=1, source_target_pairs={{0,8},{1,9},{2,10},{3,11},{4,12},{5,13},{6,14},{7,15},{8,0},{9,1},... | collective-permute-start | bytes 344072 | tf_op jit(solution)/shard_map/ppermute | solution.py:215
where the time goes:
time: 90.3 us
  Pallas kernels  36 us (40%)
  starting transfers between devices  26.7 us (30%)
  waiting for transfers between devices  21 us (23%)
  local copies, waits for them, and re-layouts  3.73 us (4%)
  other arithmetic  2.04 us (2%)
    pallas_call x2, Pallas kernels, on_device(): pl.pallas_call(kernel, out_shape=outs, in_specs=in_specs, out_specs=[pl.B...  36 us
    ppermute x8, waiting for transfers between devices, swap(): return lax.ppermute(value, axes, [(i, i ^ mask) for i in range(total)])  16.8 us
    ppermute x6, starting transfers between devices, shifted(): return lax.ppermute(value, axis, route)  13.9 us
    ppermute x8, starting transfers between devices, swap(): return lax.ppermute(value, axes, [(i, i ^ mask) for i in range(total)])  12.8 us
    ppermute x6, waiting for transfers between devices, shifted(): return lax.ppermute(value, axis, route)  4.29 us
  transfers between devices with their start and end apart: 14, of which 7 were waited for; matrix products, arithmetic and copies ran while one was open for 1% of the time, Pallas kernels for 12%

commit v1 on v0

v1 whole, which is shorter than its diff:
```python
import functools

import jax
import jax.numpy as jnp
from jax import lax
from jax.experimental import pallas as pl
from jax.experimental.pallas import tpu as pltpu
from jax.sharding import PartitionSpec as P

norm_eps = 1e-05
bf16, f32 = jnp.bfloat16, jnp.float32
SPAN = 256
VMEM_BYTES = 16 * 1024 * 1024


def shifted(value, axis, steps, ring):
    count = lax.axis_size(axis)
    if ring:
        route = [(i, (i + steps) % count) for i in range(count)]
    else:
        route = [(i, i + steps) for i in range(count) if 0 <= i + steps < count]
    return lax.ppermute(value, axis, route)


def dot(a, b):
    return jnp.dot(a, b, preferred_element_type=f32)


def dot_nt(a, b):
    return lax.dot_general(a, b, (((1,), (1,)), ((), ())), preferred_element_type=f32)


def dot_tn(a, b):
    return lax.dot_general(a, b, (((0,), (0,)), ((), ())), preferred_element_type=f32)


def halves(x):
    upper = x.astype(bf16)
    return upper, (x - upper.astype(f32)).astype(bf16)


def row_select(idx_row, nodes):
    edges = idx_row.shape[1]
    col = jnp.broadcast_to(idx_row, (128, edges)).T
    lane = lax.broadcasted_iota(jnp.int32, (edges, 128), 1)
    parts = [jnp.where(col == lane + c * 128, 1.0, 0.0).astype(bf16) for c in range(nodes // 128)]
    return jnp.concatenate(parts, axis=1)


def normed(pre):
    centred = pre - jnp.mean(pre, axis=-1, keepdims=True)
    rstd = lax.rsqrt(jnp.mean(centred * centred, axis=-1, keepdims=True) + norm_eps)
    return centred * rstd, rstd


def gate(u):
    return 1.0 / (1.0 + jnp.exp(-u))


def normed_back(u, rstd, sig, upstream):
    du = upstream * (sig * (1.0 + u * (1.0 - sig)))
    mean_du = jnp.mean(du, axis=-1, keepdims=True)
    mean_duu = jnp.mean(du * u, axis=-1, keepdims=True)
    return rstd * (du - mean_du - u * mean_duu)


class Tiles:
    def __init__(self, counts, kinds, cap, first, held):
        self.kinds, self.cap, self.first, self.held = kinds, cap, first, held
        self.counts = [counts[k] for k in kinds]
        self.ends = []
        end = jnp.int32(0)
        for count in self.counts:
            end = end + (count + SPAN - 1) // SPAN
            self.ends.append(end)

    def place(self, t):
        kind, at, start, count = self.kinds[0], jnp.int32(0), jnp.int32(0), self.counts[0]
        for i in range(1, len(self.kinds)):
            past = t >= self.ends[i - 1]
            kind = jnp.where(past, self.kinds[i], kind)
            at = jnp.where(past, i, at)
            start = jnp.where(past, self.ends[i - 1], start)
            count = jnp.where(past, self.counts[i], count)
        real = t < self.ends[-1]
        offset = jnp.where(real, (t - start) * SPAN, 0)
        rest = jnp.where(real, count - offset, 0)
        row = kind * self.cap + offset
        store = jnp.where(real, row - self.first * self.cap, self.held * self.cap)
        return Place(kind, at, offset, rest, row, store)

    def run(self, step):
        def looped(i, carry):
            step([self.place(2 * i), self.place(2 * i + 1)])
            return carry

        lax.fori_loop(0, (self.ends[-1] + 1) // 2, looped, 0)


class Place:
    def __init__(self, kind, at, offset, rest, row, store):
        self.kind, self.at, self.rest = kind, at, rest
        self.offset = pl.multiple_of(offset, SPAN)
        self.rows = pl.ds(pl.multiple_of(row, SPAN), SPAN)
        self.stored = pl.ds(pl.multiple_of(store, SPAN), SPAN)
        self.tile = store // SPAN

    def slots(self, ref):
        return ref[pl.ds(self.kind, 1), pl.ds(self.offset, SPAN)]


def rows_of(ref, places):
    return jnp.concatenate([ref[p.rows, :] for p in places], axis=0)


def slots_of(ref, places):
    return jnp.concatenate([p.slots(ref) for p in places], axis=1)


def live_of(places, d):
    place = lax.broadcasted_iota(jnp.int32, (SPAN, d), 0)
    return jnp.concatenate([place < p.rest for p in places], axis=0)


def store_rows(ref, places, value):
    for i, p in enumerate(places):
        ref[p.stored, :] = value[i * SPAN : (i + 1) * SPAN]


def receiver_forward(tiles, recv, hit, edges, w_in, part):
    nodes, d = hit.shape

    def step(places):
        picked = dot(row_select(slots_of(recv, places), nodes), hit[...]).astype(bf16)
        pre = dot(picked, w_in[d : 2 * d, :]) + dot(rows_of(edges, places), w_in[2 * d :, :])
        store_rows(part, places, pre)

    tiles.run(step)


def sender_part(places, send, source, w_in):
    nodes, d = source.shape[1:]
    picked = [dot(row_select(p.slots(send), nodes), source[p.at]) for p in places]
    return dot(jnp.concatenate(picked, axis=0).astype(bf16), w_in[:d, :])


def forward(tiles, send, recv, source, w_in, part, u_all, rs_all, hidden_all, total):
    d, nodes = total.shape

    def step(places):
        pre = rows_of(part, places)
        if source is not None:
            pre += sender_part(places, send, source, w_in)
        u, rstd = normed(pre)
        store_rows(u_all, places, u)
        store_rows(rs_all, places, jnp.broadcast_to(rstd, u.shape))
        hidden = jnp.where(live_of(places, d), u * gate(u), 0.0).T.astype(bf16)
        for i, p in enumerate(places):
            hidden_all[p.tile] = hidden[:, i * SPAN : (i + 1) * SPAN]
        total[...] += dot(hidden, row_select(slots_of(recv, places), nodes))

    tiles.run(step)


def local_kernel(
    counts_far, send_far, recv_far, hit_far, edges_far, w_in_far,
    part,
    counts, send, recv, hit, edges, w_in, arrived,
):
    far = (counts_far, send_far, recv_far, hit_far, edges_far, w_in_far)
    near = (counts, send, recv, hit.at[0], edges, w_in)
    copies = [pltpu.make_async_copy(f, n, arrived.at[i]) for i, (f, n) in enumerate(zip(far, near))]
    for copy in copies:
        copy.start()
    for copy in copies:
        copy.wait()
    kinds, cap = send.shape
    tiles = Tiles(counts, tuple(range(kinds)), cap, 0, kinds)
    receiver_forward(tiles, recv, hit.at[0], edges, w_in, part)

    def step(places):
        store_rows(part, places, rows_of(part, places) + sender_part(places, send, hit, w_in))

    Tiles(counts, (0,), cap, 0, kinds).run(step)


def early_kernel(
    counts, send, recv, src1, src2, w_in, part,
    u_all, rs_all, hidden_all, total,
    source,
):
    total[...] = jnp.zeros_like(total)
    source[0] = src1[...]
    source[1] = src2[...]
    cap = send.shape[1]
    results = (u_all, rs_all, hidden_all, total)
    forward(Tiles(counts, (0,), cap, 0, 3), send, recv, None, w_in, part, *results)
    forward(Tiles(counts, (1, 2), cap, 0, 3), send, recv, source, w_in, part, *results)


def both_halves(x, axis):
    return jnp.concatenate(halves(x), axis=axis)


def late_kernel(
    counts, send, recv, hit, src1, src2, src3, edges, grad_hit, grad_edge,
    w_in, w_out, wn_in, wn_out, part, u0, rs0, hidden0, total_in, me,
    back1, back2, back3, edge_back, recv_sum, send0, node_back, mine, other,
    source, send_sum, inc_grad, turned, weights, u_all, rs_all, hidden_all, total, moved,
):
    nodes, d = hit.shape
    kinds, cap = send.shape
    near, whole = cap // SPAN, 3 * cap // SPAN
    parts = (
        (u0.at[: 3 * cap], u_all.at[: 3 * cap]),
        (rs0.at[: 3 * cap], rs_all.at[: 3 * cap]),
        (hidden0.at[:whole], hidden_all.at[:whole]),
    )
    moves = [pltpu.make_async_copy(a, b, moved.at[i]) for i, (a, b) in enumerate(parts)]
    for move in moves:
        move.start()
    hidden_all[kinds * near] = jnp.zeros(hidden_all.shape[1:], bf16)
    total[...] = total_in[...]
    source[0] = src3[...]
    tiles = Tiles(counts, (3,), cap, 0, kinds)
    forward(tiles, send, recv, source, w_in, part, u_all, rs_all, hidden_all, total)
    for move in moves:
        move.wait()
    upper, lower = halves(total[...].T)
    incoming = (dot(upper, w_out[...]) + dot(lower, w_out[...])).astype(bf16)
    u, rstd = normed(dot(hit[...], wn_in[:d, :]) + dot(incoming, wn_in[d:, :]))
    sig = gate(u)
    hidden = (u * sig).astype(bf16)
    hidden_grad = dot_nt(grad_hit[...], wn_out[...])
    pre_grad = normed_back(u, rstd, sig, hidden_grad).astype(bf16)
    node_back[...] = pre_grad
    inc_grad[...] = both_halves(dot_nt(pre_grad, wn_in[d:, :]), 1)
    weights[6 * d : 7 * d, :] = dot_tn(hidden, grad_hit[...])
    weights[4 * d : 5 * d, :] = dot_tn(hit[...], pre_grad)
    weights[5 * d : 6 * d, :] = dot_tn(incoming, pre_grad)
    weights[3 * d : 4 * d, :] = jnp.zeros((d, d), f32)
    turned[...] = jnp.zeros_like(turned)
    recv_sum[...] = jnp.zeros_like(recv_sum)
    send_sum[...] = jnp.zeros_like(send_sum)

    def step(places):
        recv_hot = row_select(slots_of(recv, places), nodes)
        picked = dot(recv_hot, inc_grad[...])
        picked = picked[:, :d] + picked[:, d:]
        live = live_of(places, d)
        grad_rows = rows_of(grad_edge, places).astype(f32)
        message_grad = jnp.where(live, grad_rows + picked, 0.0).astype(bf16)
        hidden_grad = dot_nt(message_grad, w_out[...])
        u = rows_of(u_all, places)
        pre_grad = normed_back(u, rows_of(rs_all, places), gate(u), hidden_grad)
        pre_grad = jnp.where(live, pre_grad, 0.0)
        store_rows(edge_back, places, pre_grad.astype(bf16))
        pre_grad = pre_grad.T.astype(bf16)
        recv_sum[...] += dot(pre_grad, recv_hot)
        turned[...] += dot(pre_grad, rows_of(edges, places))
        hidden = jnp.concatenate([hidden_all[p.tile] for p in places], axis=1)
        weights[3 * d : 4 * d, :] += dot(hidden, message_grad)
        for i, p in enumerate(places):
            part_grad = pre_grad[:, i * SPAN : (i + 1) * SPAN]
            send_sum[p.kind] += dot(part_grad, row_select(p.slots(send), nodes))

    Tiles(counts, tuple(range(kinds)), cap, 0, kinds).run(step)
    weights[2 * d : 3 * d, :] = turned[...].T
    sources = (hit, src1, src2, src3)
    w_send = jnp.concatenate([w_in[:d, :], w_in[:d, :]], axis=1)
    send_turned = jnp.zeros((2 * d, d), f32)
    for k in range(kinds):
        both = both_halves(send_sum[k], 0)
        send_turned += dot(both, sources[k][...])
        if k > 0:
            (back1, back2, back3)[k - 1][...] = dot(w_send, both).T.astype(bf16)
    weights[:d, :] = (send_turned[:d] + send_turned[d:]).T
    recv_turned = dot(both_halves(recv_sum[...], 0), hit[...])
    weights[d : 2 * d, :] = (recv_turned[:d] + recv_turned[d:]).T
    send0[...] = send_sum[0]
    half = mine.shape[0]
    mine[...] = weights[pl.ds(pl.multiple_of(me[0] * half, half), half), :]
    other[...] = weights[pl.ds(pl.multiple_of((1 - me[0]) * half, half), half), :].astype(bf16)


def edge_kernel(
    counts, grad_hit, grad_edge, w_in, wn_in, edge_back, recv_sum, send0, node_back,
    edge_done, hit_done,
):
    d = w_in.shape[1]
    kinds, cap = edge_done.shape[:2]
    for k in range(kinds):
        rows = slice(k * cap, (k + 1) * cap)
        through = dot_nt(edge_back[rows, :], w_in[2 * d :, :])
        live = lax.broadcasted_iota(jnp.int32, through.shape, 0) < counts[k]
        edge_done[k] = (grad_edge[rows, :].astype(f32) + jnp.where(live, through, 0.0)).astype(bf16)
    ends = jnp.concatenate([w_in[d : 2 * d, :]] * 2 + [w_in[:d, :]] * 2, axis=1)
    sums = jnp.concatenate([both_halves(recv_sum[...], 0), both_halves(send0[...], 0)], axis=0)
    hit_done[...] = (
        grad_hit[...].astype(f32) + dot_nt(node_back[...], wn_in[:d, :]) + dot(ends, sums).T
    )


def closing_kernel(scale, me, mine, theirs, *outs):
    half = mine.shape[0]

    def put(block, start):
        row = 0
        for out in outs:
            low, high = max(row, start), min(row + out.shape[0], start + half)
            if low < high:
                out[low - row : high - row, :] = block[low - start : high - start, :].astype(f32) * scale
            row += out.shape[0]

    @pl.when(me[0] == 0)
    def _():
        put(mine, 0)
        put(theirs, half)

    @pl.when(me[0] != 0)
    def _():
        put(theirs, 0)
        put(mine, half)


def on_device(kernel, outs, operands, flops, scratch=(), scalars=(0,), hbm=False, free=()):
    vmem_spec = pl.BlockSpec(memory_space=pltpu.VMEM)
    smem_spec = pl.BlockSpec(memory_space=pltpu.SMEM)
    in_specs = [smem_spec if i in scalars else vmem_spec for i in range(len(operands))]
    if hbm:
        in_specs = [pl.BlockSpec(memory_space=pltpu.HBM)] * len(operands)
        operands = [pltpu.with_memory_space_constraint(x, pltpu.HBM) for x in operands]
    for i in free:
        in_specs[i] = pl.BlockSpec(memory_space=pl.ANY)
    return pl.pallas_call(
        kernel,
        out_shape=outs,
        in_specs=in_specs,
        out_specs=[vmem_spec] * len(outs),
        scratch_shapes=list(scratch),
        compiler_params=pltpu.CompilerParams(vmem_limit_bytes=VMEM_BYTES),
        cost_estimate=pl.CostEstimate(flops=flops, bytes_accessed=0, transcendentals=0),
    )(*operands)


def summed_over_chips(mine, total, sectors):
    axes = ("layer", "phi")

    def swap(value, mask):
        return lax.ppermute(value, axes, [(i, i ^ mask) for i in range(total)])

    bits = [1 << b for b in range(total.bit_length() - 1) if 1 << b != sectors]
    near = [1] + [b for b in bits if b > sectors]
    far = [b for b in bits if b not in near]
    ordered = far + near if len(far) % 2 == 0 else near + far
    for at in range(0, len(ordered), 2):
        pair = ordered[at : at + 2]
        masks = pair + [pair[0] ^ pair[1]] if len(pair) == 2 else pair
        sent = mine.astype(bf16)
        mine = sum((swap(sent, m).astype(f32) for m in masks), sent.astype(f32))
    mine = mine.astype(bf16)
    return mine, swap(mine, sectors)


def body(
    hit_features, edge_features, sender_slot, receiver_slot, edge_count, grad_hits, grad_edges,
    w_edge_in, w_edge_out, w_node_in, w_node_out,
):
    hit = hit_features[0, 0]
    nodes, d = hit.shape
    kinds, cap = sender_slot.shape[2:]
    edges, grad_edge = edge_features.reshape(kinds * cap, d), grad_edges.reshape(kinds * cap, d)
    send, recv, counts = sender_slot[0, 0], receiver_slot[0, 0], edge_count[0, 0]
    grad_hit = grad_hits[0, 0]
    layers, sectors = lax.axis_size("layer"), lax.axis_size("phi")
    devices = layers * sectors
    me = (lax.axis_index("layer") % 2).astype(jnp.int32).reshape(1)
    src2 = shifted(hit, "phi", 1, True)
    src3 = shifted(hit, "phi", -1, True)
    src1 = shifted(hit, "layer", 1, False)

    def shape(*dims, dtype=f32):
        return jax.ShapeDtypeStruct(dims, dtype)

    def rows(count):
        return shape(count * cap + SPAN, d)

    def tiles(count):
        return shape(count * cap // SPAN + 1, d, SPAN, dtype=bf16)

    turned = shape(d, nodes)
    node_half = shape(nodes, d, dtype=bf16)
    (part,) = on_device(
        local_kernel,
        [rows(kinds)],
        (counts, send, recv, hit, edges, w_edge_in),
        4 * 10**9,
        scratch=[
            pltpu.SMEM(counts.shape, jnp.int32),
            pltpu.VMEM(send.shape, jnp.int32),
            pltpu.VMEM(recv.shape, jnp.int32),
            pltpu.VMEM((1, nodes, d), bf16),
            pltpu.VMEM(edges.shape, bf16),
            pltpu.VMEM(w_edge_in.shape, bf16),
            pltpu.SemaphoreType.DMA((6,)),
        ],
        hbm=True,
    )
    u0, rs0, hidden0, total = on_device(
        early_kernel,
        [rows(3), rows(3), tiles(3), turned],
        (counts, send, recv, src1, src2, w_edge_in, part),
        2 * 10**9,
        scratch=[pltpu.VMEM((2, nodes, d), bf16)],
    )
    spare = kinds * cap + SPAN
    back1, back2, back3, edge_back, recv_sum, send0, node_back, mine, other = on_device(
        late_kernel,
        [
            node_half, node_half, node_half, shape(spare, d, dtype=bf16),
            turned, turned, node_half, shape(7 * d // 2, d), shape(7 * d // 2, d, dtype=bf16),
        ],
        (counts, send, recv, hit, src1, src2, src3, edges, grad_hit, grad_edge,
         w_edge_in, w_edge_out, w_node_in, w_node_out,
         part, u0, rs0, hidden0, total, me),
        8 * 10**9,
        scratch=[
            pltpu.VMEM((1, nodes, d), bf16),
            pltpu.VMEM((kinds, d, nodes), f32),
            pltpu.VMEM((nodes, 2 * d), bf16),
            pltpu.VMEM((d, d), f32),
            pltpu.VMEM((7 * d, d), f32),
            pltpu.VMEM((spare, d), f32),
            pltpu.VMEM((spare, d), f32),
            pltpu.VMEM((spare // SPAN, d, SPAN), bf16),
            pltpu.VMEM((d, nodes), f32),
            pltpu.SemaphoreType.DMA((3,)),
        ],
        scalars=(0, 19),
    )
    from_next = shifted(back2, "phi", -1, True)
    from_prev = shifted(back3, "phi", 1, True)
    from_upper = shifted(back1, "layer", -1, False)
    mine = mine + lax.ppermute(other, "layer", [(i, i ^ 1) for i in range(layers)]).astype(f32)
    edge_done, hit_done = on_device(
        edge_kernel,
        [shape(kinds, cap, d, dtype=bf16), shape(nodes, d)],
        (counts, grad_hit, grad_edge, w_edge_in, w_node_in,
         edge_back, recv_sum, send0, node_back),
        10**6,
    )
    mine, theirs = summed_over_chips(mine, devices, sectors)
    summed = on_device(
        functools.partial(closing_kernel, 1.0 / devices),
        [shape(3 * d, d), shape(d, d), shape(2 * d, d), shape(d, d)],
        (me, mine, theirs),
        10**6,
    )
    hit_total = hit_done + from_upper.astype(f32) + (from_next.astype(f32) + from_prev.astype(f32))
    return (hit_total[None, None], edge_done[None, None], *summed)


def solution(mesh):
    placed = (
        P("layer", "phi", None, None),
        P("layer", "phi", None, None, None),
        P("layer", "phi", None, None),
        P("layer", "phi", None, None),
        P("layer", "phi", None),
        P("layer", "phi", None, None),
        P("layer", "phi", None, None, None),
        P(),
        P(),
        P(),
        P(),
    )
    return jax.shard_map(
        body,
        mesh=mesh,
        in_specs=placed,
        out_specs=(
            P("layer", "phi", None, None),
            P("layer", "phi", None, None, None),
            P(),
            P(),
            P(),
            P(),
        ),
        check_vma=False,
    )
```

time: 90.3 us -> 73 us (0.81); the launches traced: 90.3 us -> 71.8 us
  Pallas kernels: 36 us -> 23.4 us
  local copies, waits for them, and re-layouts: 3.73 us -> 0.06 us
  starting transfers between devices: 26.7 us -> 23.2 us
  waiting for transfers between devices: 21 us -> 23.2 us
  other arithmetic: 2.04 us -> 1.07 us
    pallas_call x2 -> x5, Pallas kernels: 36 us -> 23.4 us  [on_device(): pl.pallas_call(kernel, out_shape=outs, in_specs=in_specs, out_specs=[vmem...]
    ppermute x6, waiting for transfers between devices: 4.29 us -> 13.1 us  [shifted(): return lax.ppermute(value, axis, route)]
    ppermute x8 -> x7, waiting for transfers between devices: 16.8 us -> 9.09 us  [swap(): return lax.ppermute(value, axes, [(i, i ^ mask) for i in range(total)])]
    ppermute x8 -> x7, starting transfers between devices: 12.8 us -> 8.78 us  [swap(): return lax.ppermute(value, axes, [(i, i ^ mask) for i in range(total)])]
    ppermute x0 -> x1, starting transfers between devices: none -> 2.91 us  [body(): lax.ppermute(other, 'layer', [(i, i ^ 1) for i in range(layers)])]
    ppermute x6, starting transfers between devices: 13.9 us -> 11.6 us  [shifted(): return lax.ppermute(value, axis, route)]
    slice x3 -> x0, local copies, waits for them, and re-layouts: 2.01 us -> none  [the longest x1 0.69 us: body(): summed[:3 * d]]
    convert_element_type x1 -> x0, local copies, waits for them, and re-layouts: 1.01 us -> none  [all_summed(): mine = mine + swap(other.astype(bf16), sectors).astype(f32)]
  transfers between devices with their start and end apart: 14 -> 14, of which waited for: 7 -> 5; matrix products, arithmetic and copies ran while one was open for 1% -> 1% of each run, Pallas kernels for 12% -> 13%
where the time goes in v1:
time: 73 us; the launch traced here: 71.8 us
  Pallas kernels  23.4 us (32%)
  starting transfers between devices  23.2 us (32%)
  waiting for transfers between devices  23.2 us (32%)
  other arithmetic  1.07 us (1%)
  between operations  0.88 us (1%)
    pallas_call x5, Pallas kernels, on_device(): pl.pallas_call(kernel, out_shape=outs, in_specs=in_specs, out_specs=[vmem...  23.4 us
    ppermute x6, waiting for transfers between devices, shifted(): return lax.ppermute(value, axis, route)  13.1 us
    ppermute x6, starting transfers between devices, shifted(): return lax.ppermute(value, axis, route)  11.6 us
    ppermute x7, waiting for transfers between devices, swap(): return lax.ppermute(value, axes, [(i, i ^ mask) for i in range(total)])  9.09 us
    ppermute x7, starting transfers between devices, swap(): return lax.ppermute(value, axes, [(i, i ^ mask) for i in range(total)])  8.78 us
    ppermute x1, starting transfers between devices, body(): lax.ppermute(other, 'layer', [(i, i ^ 1) for i in range(layers)])  2.91 us
  transfers between devices with their start and end apart: 14, of which 5 were waited for; matrix products, arithmetic and copies ran while one was open for 1% of the time, Pallas kernels for 13%

profile of v1, /device:TPU:0, one launch (start us, length us, event | category | flops | bytes accessed | tf_op | source)
XLA Modules:
  0.0 71.8 jit_solution(13500414903942249681)
XLA Ops:
  0.6 6.0 %collective-permute-start.2 = (bf16[1024,128]{1,0:T(8,128)(2,1)}, bf16[1024,128]{1,0:T(8,128)(2,1)S(1)}, u32[]{:S(2)}, u32[]{:S(2)}) collective-permute-start(bf16[1024,128]{1,0:T(8,128)(2,1)} %bitcast.21), channel_id=1, source_target_pairs={{0,7},{1,0},{2,1},{3,2},{4,3},{5,4},{6,5},{7,6},{8,15},{9,8},{10,9... | collective-permute-start | bytes 786440 | tf_op jit(solution)/shard_map/ppermute | solution.py:22
  6.7 1.5 %collective-permute-start = (bf16[1024,128]{1,0:T(8,128)(2,1)}, bf16[1024,128]{1,0:T(8,128)(2,1)S(1)}, u32[]{:S(2)}, u32[]{:S(2)}) collective-permute-start(bf16[1024,128]{1,0:T(8,128)(2,1)} %bitcast.23), channel_id=1, source_target_pairs={{0,8},{8,16},{16,24},{1,9},{9,17},{17,25},{2,10},{10,18},{18,26},{... | collective-permute-start | bytes 786440 | tf_op jit(solution)/shard_map/ppermute | solution.py:22
  8.2 4.8 %shard_map.154.part = f32[4352,128]{1,0:T(8,128)S(1)} custom-call(s32[4]{0:T(128)} %bitcast.15, s32[4,1024]{1,0:T(4,128)} %bitcast.26, s32[4,1024]{1,0:T(4,128)} %bitcast.29, bf16[1024,128]{1,0:T(8,128)(2,1)} %bitcast.24, bf16[4096,128]{1,0:T(8,128)(2,1)} %bitcast.19, bf16[384,128]{1,0:T(8,128)(2,1)} %w_in.5), custom_call_target="tpu_custom_call" | custom-call | flops 4000000000 | tf_op jit(solution)/shard_map/pallas_call | solution.py:335
  13.1 4.2 %collective-permute-done.1.src2 = bf16[1024,128]{1,0:T(8,128)(2,1)S(1)} collective-permute-done((bf16[1024,128]{1,0:T(8,128)(2,1)}, bf16[1024,128]{1,0:T(8,128)(2,1)S(1)}, u32[]{:S(2)}, u32[]{:S(2)}) %collective-permute-start.1) | collective-permute-done | bytes 262176 | tf_op jit(solution)/shard_map/ppermute | solution.py:22
  17.4 2.6 %shard_map.155 = (f32[3328,128]{1,0:T(8,128)S(1)}, f32[3328,128]{1,0:T(8,128)S(1)}, bf16[13,128,256]{2,1,0:T(8,128)(2,1)S(1)}, f32[128,1024]{1,0:T(8,128)S(1)}) custom-call(s32[4]{0:T(128)S(1)} %bitcast.16, s32[4,1024]{1,0:T(4,128)S(1)} %bitcast.27, s32[4,1024]{1,0:T(4,128)S(1)} %bitcast.30, bf16[1024,128]{1,0:T(8,128)(2,1)S(1)} %collective-permute-done.src1, ...), custom_call_target="tpu_custom_call" | custom-call | flops 2000000000 | tf_op jit(solution)/shard_map/pallas_call | solution.py:335
  20.0 13.0 %shard_map.156 = (bf16[1024,128]{1,0:T(8,128)(2,1)S(1)}, bf16[1024,128]{1,0:T(8,128)(2,1)S(1)}, bf16[1024,128]{1,0:T(8,128)(2,1)S(1)}, bf16[4352,128]{1,0:T(8,12...) custom-call(s32[4]{0:T(128)S(1)} %bitcast.17, ...), custom_call_target="tpu_custom_call" | custom-call | flops 8000000000 | tf_op jit(solution)/shard_map/pallas_call | solution.py:335
  33.1 2.9 %collective-permute-start.6 = (bf16[448,128]{1,0:T(8,128)(2,1)S(1)}, bf16[448,128]{1,0:T(8,128)(2,1)S(1)}, u32[]{:S(2)}, u32[]{:S(2)}) collective-permute-start(bf16[448,128]{1,0:T(8,128)(2,1)S(1)} %get-tuple-element.39), channel_id=1, source_target_pairs={{0,8},{8,0},{16,24},{24,16},{1,9},{9,1},{17,25},{25,17},{2,10},{10... | collective-permute-start | bytes 344072 | tf_op jit(solution)/shard_map/ppermute | solution.py:444
  36.0 1.0 %collective-permute-done.6 = bf16[448,128]{1,0:T(8,128)(2,1)S(1)} collective-permute-done((bf16[448,128]{1,0:T(8,128)(2,1)S(1)}, bf16[448,128]{1,0:T(8,128)(2,1)S(1)}, u32[]{:S(2)}, u32[]{:S(2)}) %collective-permute-start.6) | collective-permute-done | bytes 114720 | tf_op jit(solution)/shard_map/ppermute | solution.py:444
  37.0 3.5 %collective-permute-start.9 = (bf16[448,128]{1,0:T(8,128)(2,1)S(1)}, bf16[448,128]{1,0:T(8,128)(2,1)S(1)}, u32[]{:S(2)}, u32[]{:S(2)}) collective-permute-start(bf16[448,128]{1,0:T(8,128)(2,1)S(1)} %add_convert_fusion.2), channel_id=1, source_target_pairs={{0,6},{1,7},{2,4},{3,5},{4,2},{5,3},{6,0},{7,1},{8,14},{9,15},{10,... | collective-permute-start | bytes 344072 | tf_op jit(solution)/shard_map/ppermute | solution.py:350
  40.5 0.9 %collective-permute-start.7 = (bf16[448,128]{1,0:T(8,128)(2,1)S(1)}, bf16[448,128]{1,0:T(8,128)(2,1)S(1)}, u32[]{:S(2)}, u32[]{:S(2)}) collective-permute-start(bf16[448,128]{1,0:T(8,128)(2,1)S(1)} %add_convert_fusion.2), channel_id=1, source_target_pairs={{0,2},{1,3},{2,0},{3,1},{4,6},{5,7},{6,4},{7,5},{8,10},{9,11},{10,... | collective-permute-start | bytes 344072 | tf_op jit(solution)/shard_map/ppermute | solution.py:350
  41.4 3.5 %collective-permute-done.9 = bf16[448,128]{1,0:T(8,128)(2,1)S(1)} collective-permute-done((bf16[448,128]{1,0:T(8,128)(2,1)S(1)}, bf16[448,128]{1,0:T(8,128)(2,1)S(1)}, u32[]{:S(2)}, u32[]{:S(2)}) %collective-permute-start.9) | collective-permute-done | bytes 114720 | tf_op jit(solution)/shard_map/ppermute | solution.py:350
  44.9 5.6 %collective-permute-done.8 = bf16[448,128]{1,0:T(8,128)(2,1)S(1)} collective-permute-done((bf16[448,128]{1,0:T(8,128)(2,1)S(1)}, bf16[448,128]{1,0:T(8,128)(2,1)S(1)}, u32[]{:S(2)}, u32[]{:S(2)}) %collective-permute-start.8) | collective-permute-done | bytes 114720 | tf_op jit(solution)/shard_map/ppermute | solution.py:350
  50.5 0.1 add_convert_fusion.1
  50.6 2.0 %collective-permute-start.12 = (bf16[448,128]{1,0:T(8,128)(2,1)S(1)}, bf16[448,128]{1,0:T(8,128)(2,1)S(1)}, u32[]{:S(2)}, u32[]{:S(2)}) collective-permute-start(bf16[448,128]{1,0:T(8,128)(2,1)S(1)} %add_convert_fusion.1), channel_id=1, source_target_pairs={{0,17},{1,16},{2,19},{3,18},{4,21},{5,20},{6,23},{7,22},{8,25},{9,... | collective-permute-start | bytes 344072 | tf_op jit(solution)/shard_map/ppermute | solution.py:350
  52.6 0.5 collective-permute-start.11
  53.1 1.1 %collective-permute-start.10 = (bf16[448,128]{1,0:T(8,128)(2,1)S(1)}, bf16[448,128]{1,0:T(8,128)(2,1)S(1)}, u32[]{:S(2)}, u32[]{:S(2)}) collective-permute-start(bf16[448,128]{1,0:T(8,128)(2,1)S(1)} %add_convert_fusion.1), channel_id=1, source_target_pairs={{0,1},{1,0},{2,3},{3,2},{4,5},{5,4},{6,7},{7,6},{8,9},{9,8},{10,11... | collective-permute-start | bytes 344072 | tf_op jit(solution)/shard_map/ppermute | solution.py:350
  54.1 1.3 %collective-permute-start.3 = (bf16[1024,128]{1,0:T(8,128)(2,1)S(1)}, bf16[1024,128]{1,0:T(8,128)(2,1)S(1)}, u32[]{:S(2)}, u32[]{:S(2)}) collective-permute-start(bf16[1024,128]{1,0:T(8,128)(2,1)S(1)} %get-tuple-element.34), channel_id=1, source_target_pairs={{8,0},{16,8},{24,16},{9,1},{17,9},{25,17},{10,2},{18,10},{26,18},{... | collective-permute-start | bytes 786440 | tf_op jit(solution)/shard_map/ppermute | solution.py:22
  55.4 2.6 %collective-permute-start.4 = (bf16[1024,128]{1,0:T(8,128)(2,1)S(1)}, bf16[1024,128]{1,0:T(8,128)(2,1)S(1)}, u32[]{:S(2)}, u32[]{:S(2)}) collective-permute-start(bf16[1024,128]{1,0:T(8,128)(2,1)S(1)} %get-tuple-element.35), channel_id=1, source_target_pairs={{0,7},{1,0},{2,1},{3,2},{4,3},{5,4},{6,5},{7,6},{8,15},{9,8},{10,9... | collective-permute-start | bytes 786440 | tf_op jit(solution)/shard_map/ppermute | solution.py:22
  58.1 0.2 collective-permute-start.5
  58.2 2.2 %shard_map.157 = (bf16[4,1024,128]{2,1,0:T(8,128)(2,1)}, f32[1024,128]{1,0:T(8,128)S(1)}) custom-call(s32[4]{0:T(128)S(1)} %bitcast.18, bf16[1024,128]{1,0:T(8,128)(2,1)S(1)} %bitcast.14, bf16[4096,128]{1,0:T(8,128)(2,1)S(1)} %bitcast.12, bf16[384,128]{1,0:T(8,128)(2,1)S(1)} %copy-done.2, bf16[256,128]{1,0:T(8,128)(2,1)S(1)} %copy-done.3, ...), custom_call_target="tpu_custom_call" | custom-call | flops 1000000 | tf_op jit(solution)/shard_map/pallas_call | solution.py:335
  60.5 0.8 %collective-permute-start.13 = (bf16[448,128]{1,0:T(8,128)(2,1)S(1)}, bf16[448,128]{1,0:T(8,128)(2,1)S(1)}, u32[]{:S(2)}, u32[]{:S(2)}) collective-permute-start(bf16[448,128]{1,0:T(8,128)(2,1)S(1)} %add_convert_fusion.mine), channel_id=1, source_target_pairs={{0,8},{1,9},{2,10},{3,11},{4,12},{5,13},{6,14},{7,15},{8,0},{9,1},... | collective-permute-start | bytes 344072 | tf_op jit(solution)/shard_map/ppermute | solution.py:350
  61.2 8.9 %collective-permute-done.4 = bf16[1024,128]{1,0:T(8,128)(2,1)S(1)} collective-permute-done((bf16[1024,128]{1,0:T(8,128)(2,1)S(1)}, bf16[1024,128]{1,0:T(8,128)(2,1)S(1)}, u32[]{:S(2)}, u32[]{:S(2)}) %collective-permute-start.4) | collective-permute-done | bytes 262176 | tf_op jit(solution)/shard_map/ppermute | solution.py:22
  70.1 0.9 %add_bitcast_fusion = f32[1,1,1024,128]{3,2,1,0:T(8,128)} fusion(bf16[1024,128]{1,0:T(8,128)(2,1)S(1)} %collective-permute-done.5, bf16[1024,128]{1,0:T(8,128)(2,1)S(1)} %collective-permute-done.4, f32[1024,128]{1,0:T(8,128)S(1)} %get-tuple-element.33, bf16[1024,128]{1,0:T(8,128)(2,1)S(1)} %collective-permute-done.3), kind=kLoop, calls=%fused_computation | loop fusion | flops 786432 | bytes 1835008 | tf_op jit(solution)/shard_map/broadcast_in_dim | solution.py:460
  71.0 0.8 %shard_map.158 = (f32[384,128]{1,0:T(8,128)}, f32[128,128]{1,0:T(8,128)}, f32[256,128]{1,0:T(8,128)}, f32[128,128]{1,0:T(8,128)}) custom-call(s32[1]{0:T(128)} %bitcast.7.me, bf16[448,128]{1,0:T(8,128)(2,1)S(1)} %add_convert_fusion.mine, bf16[448,128]{1,0:T(8,128)(2,1)S(1)} %collective-permute-done.13.theirs), custom_call_target="tpu_custom_call" | custom-call | flops 1000000 | tf_op jit(solution)/shard_map/pallas_call | solution.py:335
  (35 shorter events, 0.2 us)
Async XLA Ops:
  0.6 19.3 %collective-permute-start.2 = (bf16[1024,128]{1,0:T(8,128)(2,1)}, bf16[1024,128]{1,0:T(8,128)(2,1)S(1)}, u32[]{:S(2)}, u32[]{:S(2)}) collective-permute-start(bf16[1024,128]{1,0:T(8,128)(2,1)} %bitcast.21), channel_id=1, source_target_pairs={{0,7},{1,0},{2,1},{3,2},{4,3},{5,4},{6,5},{7,6},{8,15},{9,8},{10,9... | collective-permute-start | bytes 786440 | tf_op jit(solution)/shard_map/ppermute | solution.py:22
  6.7 10.7 %collective-permute-start.1 = (bf16[1024,128]{1,0:T(8,128)(2,1)}, bf16[1024,128]{1,0:T(8,128)(2,1)S(1)}, u32[]{:S(2)}, u32[]{:S(2)}) collective-permute-start(bf16[1024,128]{1,0:T(8,128)(2,1)} %bitcast.22), channel_id=1, source_target_pairs={{0,1},{1,2},{2,3},{3,4},{4,5},{5,6},{6,7},{7,0},{8,9},{9,10},{10,1... | collective-permute-start | bytes 786440 | tf_op jit(solution)/shard_map/ppermute | solution.py:22
  6.7 10.7 %collective-permute-start = (bf16[1024,128]{1,0:T(8,128)(2,1)}, bf16[1024,128]{1,0:T(8,128)(2,1)S(1)}, u32[]{:S(2)}, u32[]{:S(2)}) collective-permute-start(bf16[1024,128]{1,0:T(8,128)(2,1)} %bitcast.23), channel_id=1, source_target_pairs={{0,8},{8,16},{16,24},{1,9},{9,17},{17,25},{2,10},{10,18},{18,26},{... | collective-permute-start | bytes 786440 | tf_op jit(solution)/shard_map/ppermute | solution.py:22
  8.1 9.2 %copy-start.2 = (bf16[384,128]{1,0:T(8,128)(2,1)S(1)}, bf16[384,128]{1,0:T(8,128)(2,1)}, u32[]{:S(2)}) copy-start(bf16[384,128]{1,0:T(8,128)(2,1)} %w_in.5) | copy-start | bytes 294916
  8.1 9.2 %copy-start.4 = (s32[1,1,4]{2,1,0:T(1,128)S(1)}, s32[1,1,4]{2,1,0:T(1,128)}, u32[]{:S(2)}) copy-start(s32[1,1,4]{2,1,0:T(1,128)} %param.15) | copy-start | bytes 52
  8.2 9.2 %copy-start.9 = (s32[1,1,4,1024]{3,2,1,0:T(4,128)S(1)}, s32[1,1,4,1024]{3,2,1,0:T(4,128)}, u32[]{:S(2)}) copy-start(s32[1,1,4,1024]{3,2,1,0:T(4,128)} %param.13) | copy-start | bytes 49156
  8.2 9.2 %copy-start.10 = (s32[1,1,4,1024]{3,2,1,0:T(4,128)S(1)}, s32[1,1,4,1024]{3,2,1,0:T(4,128)}, u32[]{:S(2)}) copy-start(s32[1,1,4,1024]{3,2,1,0:T(4,128)} %param.14) | copy-start | bytes 49156
  13.0 6.9 %copy-start = (bf16[1,1,4,1024,128]{4,3,2,1,0:T(8,128)(2,1)S(1)}, bf16[1,1,4,1024,128]{4,3,2,1,0:T(8,128)(2,1)}, u32[]{:S(2)}) copy-start(bf16[1,1,4,1024,128]{4,3,2,1,0:T(8,128)(2,1)} %param.17) | copy-start | bytes 3145732
  13.0 6.9 %copy-start.1 = (bf16[1,1,1024,128]{3,2,1,0:T(8,128)(2,1)S(1)}, bf16[1,1,1024,128]{3,2,1,0:T(8,128)(2,1)}, u32[]{:S(2)}) copy-start(bf16[1,1,1024,128]{3,2,1,0:T(8,128)(2,1)} %param.16) | copy-start | bytes 786436
  13.0 6.9 %copy-start.3 = (bf16[256,128]{1,0:T(8,128)(2,1)S(1)}, bf16[256,128]{1,0:T(8,128)(2,1)}, u32[]{:S(2)}) copy-start(bf16[256,128]{1,0:T(8,128)(2,1)} %wn_in.3) | copy-start | bytes 196612
  13.1 6.9 %copy-start.5 = (bf16[1,1,4,1024,128]{4,3,2,1,0:T(8,128)(2,1)S(1)}, bf16[1,1,4,1024,128]{4,3,2,1,0:T(8,128)(2,1)}, u32[]{:S(2)}) copy-start(bf16[1,1,4,1024,128]{4,3,2,1,0:T(8,128)(2,1)} %param.12) | copy-start | bytes 3145732
  13.1 6.9 %copy-start.6 = (bf16[1,1,1024,128]{3,2,1,0:T(8,128)(2,1)S(1)}, bf16[1,1,1024,128]{3,2,1,0:T(8,128)(2,1)}, u32[]{:S(2)}) copy-start(bf16[1,1,1024,128]{3,2,1,0:T(8,128)(2,1)} %param.11) | copy-start | bytes 786436
  13.1 6.9 %copy-start.7 = (bf16[128,128]{1,0:T(8,128)(2,1)S(1)}, bf16[128,128]{1,0:T(8,128)(2,1)}, u32[]{:S(2)}) copy-start(bf16[128,128]{1,0:T(8,128)(2,1)} %w_out.1) | copy-start | bytes 98308
  33.1 3.9 %collective-permute-start.6 = (bf16[448,128]{1,0:T(8,128)(2,1)S(1)}, bf16[448,128]{1,0:T(8,128)(2,1)S(1)}, u32[]{:S(2)}, u32[]{:S(2)}) collective-permute-start(bf16[448,128]{1,0:T(8,128)(2,1)S(1)} %get-tuple-element.39), channel_id=1, source_target_pairs={{0,8},{8,0},{16,24},{24,16},{1,9},{9,1},{17,25},{25,17},{2,10},{10... | collective-permute-start | bytes 344072 | tf_op jit(solution)/shard_map/ppermute | solution.py:444
  37.0 7.9 %collective-permute-start.9 = (bf16[448,128]{1,0:T(8,128)(2,1)S(1)}, bf16[448,128]{1,0:T(8,128)(2,1)S(1)}, u32[]{:S(2)}, u32[]{:S(2)}) collective-permute-start(bf16[448,128]{1,0:T(8,128)(2,1)S(1)} %add_convert_fusion.2), channel_id=1, source_target_pairs={{0,6},{1,7},{2,4},{3,5},{4,2},{5,3},{6,0},{7,1},{8,14},{9,15},{10,... | collective-permute-start | bytes 344072 | tf_op jit(solution)/shard_map/ppermute | solution.py:350
  40.5 10.0 %collective-permute-start.8 = (bf16[448,128]{1,0:T(8,128)(2,1)S(1)}, bf16[448,128]{1,0:T(8,128)(2,1)S(1)}, u32[]{:S(2)}, u32[]{:S(2)}) collective-permute-start(bf16[448,128]{1,0:T(8,128)(2,1)S(1)} %add_convert_fusion.2), channel_id=1, source_target_pairs={{0,4},{1,5},{2,6},{3,7},{4,0},{5,1},{6,2},{7,3},{8,12},{9,13},{10,... | collective-permute-start | bytes 344072 | tf_op jit(solution)/shard_map/ppermute | solution.py:350
  40.5 10.0 %collective-permute-start.7 = (bf16[448,128]{1,0:T(8,128)(2,1)S(1)}, bf16[448,128]{1,0:T(8,128)(2,1)S(1)}, u32[]{:S(2)}, u32[]{:S(2)}) collective-permute-start(bf16[448,128]{1,0:T(8,128)(2,1)S(1)} %add_convert_fusion.2), channel_id=1, source_target_pairs={{0,2},{1,3},{2,0},{3,1},{4,6},{5,7},{6,4},{7,5},{8,10},{9,11},{10,... | collective-permute-start | bytes 344072 | tf_op jit(solution)/shard_map/ppermute | solution.py:350
  50.6 7.5 %collective-permute-start.12 = (bf16[448,128]{1,0:T(8,128)(2,1)S(1)}, bf16[448,128]{1,0:T(8,128)(2,1)S(1)}, u32[]{:S(2)}, u32[]{:S(2)}) collective-permute-start(bf16[448,128]{1,0:T(8,128)(2,1)S(1)} %add_convert_fusion.1), channel_id=1, source_target_pairs={{0,17},{1,16},{2,19},{3,18},{4,21},{5,20},{6,23},{7,22},{8,25},{9,... | collective-permute-start | bytes 344072 | tf_op jit(solution)/shard_map/ppermute | solution.py:350
  52.6 7.8 %collective-permute-start.11 = (bf16[448,128]{1,0:T(8,128)(2,1)S(1)}, bf16[448,128]{1,0:T(8,128)(2,1)S(1)}, u32[]{:S(2)}, u32[]{:S(2)}) collective-permute-start(bf16[448,128]{1,0:T(8,128)(2,1)S(1)} %add_convert_fusion.1), channel_id=1, source_target_pairs={{0,16},{1,17},{2,18},{3,19},{4,20},{5,21},{6,22},{7,23},{8,24},{9,... | collective-permute-start | bytes 344072 | tf_op jit(solution)/shard_map/ppermute | solution.py:350
  53.1 7.3 %collective-permute-start.10 = (bf16[448,128]{1,0:T(8,128)(2,1)S(1)}, bf16[448,128]{1,0:T(8,128)(2,1)S(1)}, u32[]{:S(2)}, u32[]{:S(2)}) collective-permute-start(bf16[448,128]{1,0:T(8,128)(2,1)S(1)} %add_convert_fusion.1), channel_id=1, source_target_pairs={{0,1},{1,0},{2,3},{3,2},{4,5},{5,4},{6,7},{7,6},{8,9},{9,8},{10,11... | collective-permute-start | bytes 344072 | tf_op jit(solution)/shard_map/ppermute | solution.py:350
  54.1 7.1 %collective-permute-start.3 = (bf16[1024,128]{1,0:T(8,128)(2,1)S(1)}, bf16[1024,128]{1,0:T(8,128)(2,1)S(1)}, u32[]{:S(2)}, u32[]{:S(2)}) collective-permute-start(bf16[1024,128]{1,0:T(8,128)(2,1)S(1)} %get-tuple-element.34), channel_id=1, source_target_pairs={{8,0},{16,8},{24,16},{9,1},{17,9},{25,17},{10,2},{18,10},{26,18},{... | collective-permute-start | bytes 786440 | tf_op jit(solution)/shard_map/ppermute | solution.py:22
  55.4 14.7 %collective-permute-start.4 = (bf16[1024,128]{1,0:T(8,128)(2,1)S(1)}, bf16[1024,128]{1,0:T(8,128)(2,1)S(1)}, u32[]{:S(2)}, u32[]{:S(2)}) collective-permute-start(bf16[1024,128]{1,0:T(8,128)(2,1)S(1)} %get-tuple-element.35), channel_id=1, source_target_pairs={{0,7},{1,0},{2,1},{3,2},{4,3},{5,4},{6,5},{7,6},{8,15},{9,8},{10,9... | collective-permute-start | bytes 786440 | tf_op jit(solution)/shard_map/ppermute | solution.py:22
  58.1 12.1 %collective-permute-start.5 = (bf16[1024,128]{1,0:T(8,128)(2,1)S(1)}, bf16[1024,128]{1,0:T(8,128)(2,1)S(1)}, u32[]{:S(2)}, u32[]{:S(2)}) collective-permute-start(bf16[1024,128]{1,0:T(8,128)(2,1)S(1)} %get-tuple-element.36), channel_id=1, source_target_pairs={{0,1},{1,2},{2,3},{3,4},{4,5},{5,6},{6,7},{7,0},{8,9},{9,10},{10,1... | collective-permute-start | bytes 786440 | tf_op jit(solution)/shard_map/ppermute | solution.py:22
  60.5 10.6 %collective-permute-start.13 = (bf16[448,128]{1,0:T(8,128)(2,1)S(1)}, bf16[448,128]{1,0:T(8,128)(2,1)S(1)}, u32[]{:S(2)}, u32[]{:S(2)}) collective-permute-start(bf16[448,128]{1,0:T(8,128)(2,1)S(1)} %add_convert_fusion.mine), channel_id=1, source_target_pairs={{0,8},{1,9},{2,10},{3,11},{4,12},{5,13},{6,14},{7,15},{8,0},{9,1},... | collective-permute-start | bytes 344072 | tf_op jit(solution)/shard_map/ppermute | solution.py:350
  (1 other events, 6.9 us)

commit v2 on v1

--- a/solution.py
+++ b/solution.py
@@ -87,21 +87,22 @@
         rest = jnp.where(real, count - offset, 0)
         row = kind * self.cap + offset
         store = jnp.where(real, row - self.first * self.cap, self.held * self.cap)
-        return Place(kind, at, offset, rest, row, store)
-
-    def run(self, step):
+        return Place(kind, at, offset, rest, row, row - self.first * self.cap, store)
+
+    def run(self, step, group=2):
         def looped(i, carry):
-            step([self.place(2 * i), self.place(2 * i + 1)])
+            step([self.place(group * i + j) for j in range(group)])
             return carry
 
-        lax.fori_loop(0, (self.ends[-1] + 1) // 2, looped, 0)
+        lax.fori_loop(0, (self.ends[-1] + group - 1) // group, looped, 0)
 
 
 class Place:
-    def __init__(self, kind, at, offset, rest, row, store):
+    def __init__(self, kind, at, offset, rest, row, own, store):
         self.kind, self.at, self.rest = kind, at, rest
         self.offset = pl.multiple_of(offset, SPAN)
         self.rows = pl.ds(pl.multiple_of(row, SPAN), SPAN)
+        self.own = pl.ds(pl.multiple_of(own, SPAN), SPAN)
         self.stored = pl.ds(pl.multiple_of(store, SPAN), SPAN)
         self.tile = store // SPAN
 
@@ -111,6 +112,10 @@
 
 def rows_of(ref, places):
     return jnp.concatenate([ref[p.rows, :] for p in places], axis=0)
+
+
+def own_rows_of(ref, places):
+    return jnp.concatenate([ref[p.own, :] for p in places], axis=0)
 
 
 def slots_of(ref, places):
@@ -135,7 +140,7 @@
         pre = dot(picked, w_in[d : 2 * d, :]) + dot(rows_of(edges, places), w_in[2 * d :, :])
         store_rows(part, places, pre)
 
-    tiles.run(step)
+    tiles.run(step, 4)
 
 
 def sender_part(places, send, source, w_in):
@@ -144,7 +149,7 @@
     return dot(jnp.concatenate(picked, axis=0).astype(bf16), w_in[:d, :])
 
 
-def forward(tiles, send, recv, source, w_in, part, u_all, rs_all, hidden_all, total):
+def forward(tiles, group, send, recv, source, w_in, part, u_all, rs_all, hidden_all, total):
     d, nodes = total.shape
 
     def step(places):
@@ -159,7 +164,7 @@
             hidden_all[p.tile] = hidden[:, i * SPAN : (i + 1) * SPAN]
         total[...] += dot(hidden, row_select(slots_of(recv, places), nodes))
 
-    tiles.run(step)
+    tiles.run(step, group)
 
 
 def local_kernel(
@@ -181,7 +186,7 @@
     def step(places):
         store_rows(part, places, rows_of(part, places) + sender_part(places, send, hit, w_in))
 
-    Tiles(counts, (0,), cap, 0, kinds).run(step)
+    Tiles(counts, (0,), cap, 0, kinds).run(step, 4)
 
 
 def early_kernel(
@@ -190,42 +195,84 @@
     source,
 ):
     total[...] = jnp.zeros_like(total)
+    hidden_all[hidden_all.shape[0] - 1] = jnp.zeros(hidden_all.shape[1:], bf16)
     source[0] = src1[...]
     source[1] = src2[...]
     cap = send.shape[1]
     results = (u_all, rs_all, hidden_all, total)
-    forward(Tiles(counts, (0,), cap, 0, 3), send, recv, None, w_in, part, *results)
-    forward(Tiles(counts, (1, 2), cap, 0, 3), send, recv, source, w_in, part, *results)
+    forward(Tiles(counts, (0,), cap, 0, 3), 4, send, recv, None, w_in, part, *results)
+    forward(Tiles(counts, (1, 2), cap, 0, 3), 4, send, recv, source, w_in, part, *results)
 
 
 def both_halves(x, axis):
     return jnp.concatenate(halves(x), axis=axis)
 
 
-def late_kernel(
-    counts, send, recv, hit, src1, src2, src3, edges, grad_hit, grad_edge,
+def backward(
+    tiles, send, recv, edges, grad_edge, w_out, inc_grad, u_all, rs_all, hidden_all,
+    edge_back, recv_sum, send_sum, edge_turned, out_sum,
+):
+    nodes = inc_grad.shape[0]
+    d = w_out.shape[0]
+
+    def step(places):
+        recv_hot = row_select(slots_of(recv, places), nodes)
+        picked = dot(recv_hot, inc_grad[...])
+        live = live_of(places, d)
+        grad_rows = rows_of(grad_edge, places).astype(f32)
+        message_grad = jnp.where(live, grad_rows + picked, 0.0).astype(bf16)
+        hidden_grad = dot_nt(message_grad, w_out[...])
+        u = own_rows_of(u_all, places)
+        pre_grad = normed_back(u, own_rows_of(rs_all, places), gate(u), hidden_grad)
+        pre_grad = jnp.where(live, pre_grad, 0.0)
+        store_rows(edge_back, places, pre_grad.astype(bf16))
+        pre_grad = pre_grad.T.astype(bf16)
+        recv_sum[...] += dot(pre_grad, recv_hot)
+        edge_turned[...] += dot(pre_grad, rows_of(edges, places))
+        hidden = jnp.concatenate([hidden_all[p.tile] for p in places], axis=1)
+        out_sum[...] += dot(hidden, message_grad)
+        for i, p in enumerate(places):
+            part_grad = pre_grad[:, i * SPAN : (i + 1) * SPAN]
+            send_sum[p.at] += dot(part_grad, row_select(p.slots(send), nodes))
+
+    tiles.run(step)
+
+
+def senders_back(send_sum, w_in):
+    d = w_in.shape[1]
+    w_send = jnp.concatenate([w_in[:d, :], w_in[:d, :]], axis=1)
+    return dot(w_send, both_halves(send_sum, 0)).T.astype(bf16)
+
+
+def turned_product(sums, table):
+    both = dot(both_halves(sums, 0), table)
+    d = table.shape[1]
+    return both[:d] + both[d:]
+
+
+def node_kernel(
+    counts, send, recv, hit, src2, src3, edges, grad_hit, grad_edge,
     w_in, w_out, wn_in, wn_out, part, u0, rs0, hidden0, total_in, me,
-    back1, back2, back3, edge_back, recv_sum, send0, node_back, mine, other,
-    source, send_sum, inc_grad, turned, weights, u_all, rs_all, hidden_all, total, moved,
+    far_back, near_back, edge_back, recv_sum, node_back, inc_grad, partial,
+    source, send_sum, u_all, rs_all, hidden_all, total, moved,
 ):
     nodes, d = hit.shape
-    kinds, cap = send.shape
-    near, whole = cap // SPAN, 3 * cap // SPAN
+    cap = send.shape[1]
+    near = cap // SPAN
+    second = slice(2 * cap, 3 * cap)
     parts = (
-        (u0.at[: 3 * cap], u_all.at[: 3 * cap]),
-        (rs0.at[: 3 * cap], rs_all.at[: 3 * cap]),
-        (hidden0.at[:whole], hidden_all.at[:whole]),
+        (u0.at[second], u_all.at[:cap]),
+        (rs0.at[second], rs_all.at[:cap]),
+        (hidden0.at[2 * near : 3 * near], hidden_all.at[:near]),
     )
     moves = [pltpu.make_async_copy(a, b, moved.at[i]) for i, (a, b) in enumerate(parts)]
     for move in moves:
         move.start()
-    hidden_all[kinds * near] = jnp.zeros(hidden_all.shape[1:], bf16)
+    hidden_all[2 * near] = jnp.zeros(hidden_all.shape[1:], bf16)
     total[...] = total_in[...]
     source[0] = src3[...]
-    tiles = Tiles(counts, (3,), cap, 0, kinds)
-    forward(tiles, send, recv, source, w_in, part, u_all, rs_all, hidden_all, total)
-    for move in moves:
-        move.wait()
+    results = (u_all, rs_all, hidden_all, total)
+    forward(Tiles(counts, (3,), cap, 2, 2), 2, send, recv, source, w_in, part, *results)
     upper, lower = halves(total[...].T)
     incoming = (dot(upper, w_out[...]) + dot(lower, w_out[...])).astype(bf16)
     u, rstd = normed(dot(hit[...], wn_in[:d, :]) + dot(incoming, wn_in[d:, :]))
@@ -234,49 +281,45 @@
     hidden_grad = dot_nt(grad_hit[...], wn_out[...])
     pre_grad = normed_back(u, rstd, sig, hidden_grad).astype(bf16)
     node_back[...] = pre_grad
-    inc_grad[...] = both_halves(dot_nt(pre_grad, wn_in[d:, :]), 1)
-    weights[6 * d : 7 * d, :] = dot_tn(hidden, grad_hit[...])
-    weights[4 * d : 5 * d, :] = dot_tn(hit[...], pre_grad)
-    weights[5 * d : 6 * d, :] = dot_tn(incoming, pre_grad)
-    weights[3 * d : 4 * d, :] = jnp.zeros((d, d), f32)
-    turned[...] = jnp.zeros_like(turned)
+    inc_grad[...] = dot_nt(pre_grad, wn_in[d:, :]).astype(bf16)
+    partial[6 * d : 7 * d, :] = dot_tn(hidden, grad_hit[...])
+    partial[4 * d : 5 * d, :] = dot_tn(hit[...], pre_grad)
+    partial[5 * d : 6 * d, :] = dot_tn(incoming, pre_grad)
+    partial[2 * d : 4 * d, :] = jnp.zeros((2 * d, d), f32)
     recv_sum[...] = jnp.zeros_like(recv_sum)
     send_sum[...] = jnp.zeros_like(send_sum)
-
-    def step(places):
-        recv_hot = row_select(slots_of(recv, places), nodes)
-        picked = dot(recv_hot, inc_grad[...])
-        picked = picked[:, :d] + picked[:, d:]
-        live = live_of(places, d)
-        grad_rows = rows_of(grad_edge, places).astype(f32)
-        message_grad = jnp.where(live, grad_rows + picked, 0.0).astype(bf16)
-        hidden_grad = dot_nt(message_grad, w_out[...])
-        u = rows_of(u_all, places)
-        pre_grad = normed_back(u, rows_of(rs_all, places), gate(u), hidden_grad)
-        pre_grad = jnp.where(live, pre_grad, 0.0)
-        store_rows(edge_back, places, pre_grad.astype(bf16))
-        pre_grad = pre_grad.T.astype(bf16)
-        recv_sum[...] += dot(pre_grad, recv_hot)
-        turned[...] += dot(pre_grad, rows_of(edges, places))
-        hidden = jnp.concatenate([hidden_all[p.tile] for p in places], axis=1)
-        weights[3 * d : 4 * d, :] += dot(hidden, message_grad)
-        for i, p in enumerate(places):
-            part_grad = pre_grad[:, i * SPAN : (i + 1) * SPAN]
-            send_sum[p.kind] += dot(part_grad, row_select(p.slots(send), nodes))
-
-    Tiles(counts, tuple(range(kinds)), cap, 0, kinds).run(step)
-    weights[2 * d : 3 * d, :] = turned[...].T
-    sources = (hit, src1, src2, src3)
-    w_send = jnp.concatenate([w_in[:d, :], w_in[:d, :]], axis=1)
-    send_turned = jnp.zeros((2 * d, d), f32)
-    for k in range(kinds):
-        both = both_halves(send_sum[k], 0)
-        send_turned += dot(both, sources[k][...])
-        if k > 0:
-            (back1, back2, back3)[k - 1][...] = dot(w_send, both).T.astype(bf16)
-    weights[:d, :] = (send_turned[:d] + send_turned[d:]).T
-    recv_turned = dot(both_halves(recv_sum[...], 0), hit[...])
-    weights[d : 2 * d, :] = (recv_turned[:d] + recv_turned[d:]).T
+    for move in moves:
+        move.wait()
+    backward(
+        Tiles(counts, (2, 3), cap, 2, 2), send, recv, edges, grad_edge, w_out, inc_grad,
+        u_all, rs_all, hidden_all, edge_back, recv_sum, send_sum,
+        partial.at[2 * d : 3 * d], partial.at[3 * d : 4 * d],
+    )
+    partial[:d, :] = turned_product(send_sum[0], src2[...]) + turned_product(send_sum[1], src3[...])
+    far_back[...] = senders_back(send_sum[me[1]], w_in)
+    near_back[...] = senders_back(send_sum[1 - me[1]], w_in)
+
+
+def last_kernel(
+    counts, send, recv, hit, src1, edges, grad_edge, w_in, w_out,
+    u0, rs0, hidden0, recv_in, inc_grad, partial, me,
+    back1, edge_back, recv_sum, send0, mine, other,
+    send_sum, weights,
+):
+    cap, d = send.shape[1], hit.shape[1]
+    weights[...] = partial[...]
+    recv_sum[...] = recv_in[...]
+    send_sum[...] = jnp.zeros_like(send_sum)
+    backward(
+        Tiles(counts, (0, 1), cap, 0, 3), send, recv, edges, grad_edge, w_out, inc_grad,
+        u0, rs0, hidden0, edge_back, recv_sum, send_sum,
+        weights.at[2 * d : 3 * d], weights.at[3 * d : 4 * d],
+    )
+    turned = turned_product(send_sum[0], hit[...]) + turned_product(send_sum[1], src1[...])
+    weights[:d, :] = (weights[:d, :] + turned).T
+    weights[d : 2 * d, :] = turned_product(recv_sum[...], hit[...]).T
+    weights[2 * d : 3 * d, :] = weights[2 * d : 3 * d, :].T
+    back1[...] = senders_back(send_sum[1], w_in)
     send0[...] = send_sum[0]
     half = mine.shape[0]
     mine[...] = weights[pl.ds(pl.multiple_of(me[0] * half, half), half), :]
@@ -284,16 +327,17 @@
 
 
 def edge_kernel(
-    counts, grad_hit, grad_edge, w_in, wn_in, edge_back, recv_sum, send0, node_back,
+    counts, grad_hit, grad_edge, w_in, wn_in, first_back, second_back, recv_sum, send0, node_back,
     edge_done, hit_done,
 ):
     d = w_in.shape[1]
     kinds, cap = edge_done.shape[:2]
     for k in range(kinds):
-        rows = slice(k * cap, (k + 1) * cap)
-        through = dot_nt(edge_back[rows, :], w_in[2 * d :, :])
+        back = (first_back, second_back)[k // 2][k % 2 * cap : (k % 2 + 1) * cap, :]
+        through = dot_nt(back, w_in[2 * d :, :])
         live = lax.broadcasted_iota(jnp.int32, through.shape, 0) < counts[k]
-        edge_done[k] = (grad_edge[rows, :].astype(f32) + jnp.where(live, through, 0.0)).astype(bf16)
+        grad_rows = grad_edge[k * cap : (k + 1) * cap, :].astype(f32)
+        edge_done[k] = (grad_rows + jnp.where(live, through, 0.0)).astype(bf16)
     ends = jnp.concatenate([w_in[d : 2 * d, :]] * 2 + [w_in[:d, :]] * 2, axis=1)
     sums = jnp.concatenate([both_halves(recv_sum[...], 0), both_halves(send0[...], 0)], axis=0)
     hit_done[...] = (
@@ -343,7 +387,7 @@
     )(*operands)
 
 
-def summed_over_chips(mine, total, sectors):
+def summed_over_chips(mine, total, sectors, beside):
     axes = ("layer", "phi")
 
     def swap(value, mask):
@@ -358,8 +402,10 @@
         masks = pair + [pair[0] ^ pair[1]] if len(pair) == 2 else pair
         sent = mine.astype(bf16)
         mine = sum((swap(sent, m).astype(f32) for m in masks), sent.astype(f32))
+        if at == 0:
+            mine, beside = lax.optimization_barrier((mine, beside))
     mine = mine.astype(bf16)
-    return mine, swap(mine, sectors)
+    return mine, swap(mine, sectors), beside
 
 
 def body(
@@ -374,7 +420,7 @@
     grad_hit = grad_hits[0, 0]
     layers, sectors = lax.axis_size("layer"), lax.axis_size("phi")
     devices = layers * sectors
-    me = (lax.axis_index("layer") % 2).astype(jnp.int32).reshape(1)
+    me = jnp.stack([lax.axis_index("layer") % 2, lax.axis_index("phi") % 2]).astype(jnp.int32)
     src2 = shifted(hit, "phi", 1, True)
     src3 = shifted(hit, "phi", -1, True)
     src1 = shifted(hit, "layer", 1, False)
@@ -413,50 +459,64 @@
         2 * 10**9,
         scratch=[pltpu.VMEM((2, nodes, d), bf16)],
     )
-    spare = kinds * cap + SPAN
-    back1, back2, back3, edge_back, recv_sum, send0, node_back, mine, other = on_device(
-        late_kernel,
+    partial = shape(7 * d, d)
+    far_back, near_back, second_back, recv_sum, node_back, inc_grad, partial = on_device(
+        node_kernel,
         [
-            node_half, node_half, node_half, shape(spare, d, dtype=bf16),
-            turned, turned, node_half, shape(7 * d // 2, d), shape(7 * d // 2, d, dtype=bf16),
+            node_half, node_half, shape(2 * cap + SPAN, d, dtype=bf16),
+            turned, node_half, node_half, partial,
         ],
-        (counts, send, recv, hit, src1, src2, src3, edges, grad_hit, grad_edge,
-         w_edge_in, w_edge_out, w_node_in, w_node_out,
-         part, u0, rs0, hidden0, total, me),
+        (counts, send, recv, hit, src2, src3, edges, grad_hit, grad_edge,
+         w_edge_in, w_edge_out, w_node_in, w_node_out, part, u0, rs0, hidden0, total, me),
         8 * 10**9,
         scratch=[
             pltpu.VMEM((1, nodes, d), bf16),
-            pltpu.VMEM((kinds, d, nodes), f32),
-            pltpu.VMEM((nodes, 2 * d), bf16),
-            pltpu.VMEM((d, d), f32),
-            pltpu.VMEM((7 * d, d), f32),
-            pltpu.VMEM((spare, d), f32),
-            pltpu.VMEM((spare, d), f32),
-            pltpu.VMEM((spare // SPAN, d, SPAN), bf16),
+            pltpu.VMEM((2, d, nodes), f32),
+            pltpu.VMEM((2 * cap + SPAN, d), f32),
+            pltpu.VMEM((2 * cap + SPAN, d), f32),
+            pltpu.VMEM((2 * cap // SPAN + 1, d, SPAN), bf16),
             pltpu.VMEM((d, nodes), f32),
             pltpu.SemaphoreType.DMA((3,)),
         ],
-        scalars=(0, 19),
-    )
-    from_next = shifted(back2, "phi", -1, True)
-    from_prev = shifted(back3, "phi", 1, True)
+        scalars=(0, 18),
+    )
+    route = [(i, (i + (2 if i % 2 else -2)) % sectors) for i in range(sectors)]
+    relayed = lax.ppermute(far_back, "phi", route)
+    back1, first_back, recv_sum, send0, mine, other = on_device(
+        last_kernel,
+        [
+            node_half, shape(3 * cap + SPAN, d, dtype=bf16), turned, turned,
+            shape(7 * d // 2, d), shape(7 * d // 2, d, dtype=bf16),
+        ],
+        (counts, send, recv, hit, src1, edges, grad_edge, w_edge_in, w_edge_out,
+         u0, rs0, hidden0, recv_sum, inc_grad, partial, me),
+        8 * 10**9,
+        scratch=[pltpu.VMEM((2, d, nodes), f32), pltpu.VMEM((7 * d, d), f32)],
+        scalars=(0, 15),
+    )
     from_upper = shifted(back1, "layer", -1, False)
+    other, relayed = lax.optimization_barrier((other, relayed))
+    from_beside = lax.ppermute(
+        (near_back.astype(f32) + relayed.astype(f32)).astype(bf16),
+        "phi",
+        [(i, i ^ 1) for i in range(sectors)],
+    )
     mine = mine + lax.ppermute(other, "layer", [(i, i ^ 1) for i in range(layers)]).astype(f32)
     edge_done, hit_done = on_device(
         edge_kernel,
         [shape(kinds, cap, d, dtype=bf16), shape(nodes, d)],
         (counts, grad_hit, grad_edge, w_edge_in, w_node_in,
-         edge_back, recv_sum, send0, node_back),
+         first_back, second_back, recv_sum, send0, node_back),
         10**6,
     )
-    mine, theirs = summed_over_chips(mine, devices, sectors)
+    hit_total = hit_done + from_upper.astype(f32) + from_beside.astype(f32)
+    mine, theirs, hit_total = summed_over_chips(mine, devices, sectors, hit_total)
     summed = on_device(
         functools.partial(closing_kernel, 1.0 / devices),
         [shape(3 * d, d), shape(d, d), shape(2 * d, d), shape(d, d)],
         (me, mine, theirs),
         10**6,
     )
-    hit_total = hit_done + from_upper.astype(f32) + (from_next.astype(f32) + from_prev.astype(f32))
     return (hit_total[None, None], edge_done[None, None], *summed)
 
 

time: 73 us -> 67.5 us (0.925); the launches traced: 71.8 us -> 67.5 us
  waiting for transfers between devices: 23.2 us -> 19.7 us
  starting transfers between devices: 23.2 us -> 21.9 us
    ppermute x6 -> x4, waiting for transfers between devices: 13.1 us -> 4.58 us  [shifted(): return lax.ppermute(value, axis, route)]
    ppermute x0 -> x2, waiting for transfers between devices: none -> 4.97 us  [the longest x1 3.58 us: body(): relayed = lax.ppermute(far_back, 'phi', route)]
    ppermute x0 -> x2, starting transfers between devices: none -> 3.51 us  [the longest x1 3.45 us: body(): lax.ppermute((near_back.astype(f32) + relayed.astype(f32)).astype(bf16),...]
    ppermute x1, starting transfers between devices: 2.91 us -> 0.01 us  [body(): lax.ppermute(other, 'layer', [(i, i ^ 1) for i in range(layers)])]
    ppermute x6 -> x4, starting transfers between devices: 11.6 us -> 8.78 us  [shifted(): return lax.ppermute(value, axis, route)]
    ppermute x7, waiting for transfers between devices: 9.09 us -> 10.1 us  [swap(): return lax.ppermute(value, axes, [(i, i ^ mask) for i in range(total)])]
    add x0 -> x2, other arithmetic: none -> 0.95 us  [the longest x1 0.89 us: body(): hit_total = hit_done + from_upper.astype(f32) + from_beside.astype(f32)]
    ppermute x1, waiting for transfers between devices: 0.97 us -> 0.03 us  [body(): lax.ppermute(other, 'layer', [(i, i ^ 1) for i in range(layers)])]
  transfers between devices with their start and end apart: 14 -> 14, of which waited for: 5 -> 8; matrix products, arithmetic and copies ran while one was open for 1% -> 0% of each run, Pallas kernels for 13% -> 19%
where the time goes in v2:
time: 67.5 us
  Pallas kernels  23.8 us (35%)
  starting transfers between devices  21.9 us (32%)
  waiting for transfers between devices  19.7 us (29%)
  other arithmetic  1.19 us (2%)
  between operations  0.89 us (1%)
    pallas_call x6, Pallas kernels, on_device(): pl.pallas_call(kernel, out_shape=outs, in_specs=in_specs, out_specs=[vmem...  23.8 us
    ppermute x7, waiting for transfers between devices, swap(): return lax.ppermute(value, axes, [(i, i ^ mask) for i in range(total)])  10.1 us
    ppermute x7, starting transfers between devices, swap(): return lax.ppermute(value, axes, [(i, i ^ mask) for i in range(total)])  9.63 us
    ppermute x4, starting transfers between devices, shifted(): return lax.ppermute(value, axis, route)  8.78 us
    ppermute x4, waiting for transfers between devices, shifted(): return lax.ppermute(value, axis, route)  4.58 us
    ppermute x1, waiting for transfers between devices, body(): relayed = lax.ppermute(far_back, 'phi', route)  3.58 us
    ppermute x1, starting transfers between devices, body(): lax.ppermute((near_back.astype(f32) + relayed.astype(f32)).astype(bf16),...  3.45 us
    ppermute x1, waiting for transfers between devices, body(): lax.ppermute((near_back.astype(f32) + relayed.astype(f32)).astype(bf16),...  1.38 us
  transfers between devices with their start and end apart: 14, of which 8 were waited for; matrix products, arithmetic and copies ran while one was open for 0% of the time, Pallas kernels for 19%

profile of v2, /device:TPU:0, one launch (start us, length us, event | category | flops | bytes accessed | tf_op | source)
XLA Modules:
  0.0 67.5 jit_solution(16659665716087577499)
XLA Ops:
  0.6 6.0 %collective-permute-start.2 = (bf16[1024,128]{1,0:T(8,128)(2,1)}, bf16[1024,128]{1,0:T(8,128)(2,1)S(1)}, u32[]{:S(2)}, u32[]{:S(2)}) collective-permute-start(bf16[1024,128]{1,0:T(8,128)(2,1)} %bitcast.24), channel_id=1, source_target_pairs={{0,7},{1,0},{2,1},{3,2},{4,3},{5,4},{6,5},{7,6},{8,15},{9,8},{10,9... | collective-permute-start | bytes 786440 | tf_op jit(solution)/shard_map/ppermute | solution.py:22
  6.7 1.5 %collective-permute-start = (bf16[1024,128]{1,0:T(8,128)(2,1)}, bf16[1024,128]{1,0:T(8,128)(2,1)S(1)}, u32[]{:S(2)}, u32[]{:S(2)}) collective-permute-start(bf16[1024,128]{1,0:T(8,128)(2,1)} %bitcast.26), channel_id=1, source_target_pairs={{0,8},{8,16},{16,24},{1,9},{9,17},{17,25},{2,10},{10,18},{18,26},{... | collective-permute-start | bytes 786440 | tf_op jit(solution)/shard_map/ppermute | solution.py:22
  8.2 4.4 %shard_map.154.part = f32[4352,128]{1,0:T(8,128)S(1)} custom-call(s32[4]{0:T(128)} %bitcast.16, s32[4,1024]{1,0:T(4,128)} %bitcast.30, s32[4,1024]{1,0:T(4,128)} %bitcast.34, bf16[1024,128]{1,0:T(8,128)(2,1)} %bitcast.27, bf16[4096,128]{1,0:T(8,128)(2,1)} %bitcast.21, bf16[384,128]{1,0:T(8,128)(2,1)} %w_in.7), custom_call_target="tpu_custom_call" | custom-call | flops 4000000000 | tf_op jit(solution)/shard_map/pallas_call | solution.py:379
  12.6 0.1 pad_add_fusion.me
  12.8 4.6 %collective-permute-done.1.src2 = bf16[1024,128]{1,0:T(8,128)(2,1)S(1)} collective-permute-done((bf16[1024,128]{1,0:T(8,128)(2,1)}, bf16[1024,128]{1,0:T(8,128)(2,1)S(1)}, u32[]{:S(2)}, u32[]{:S(2)}) %collective-permute-start.1) | collective-permute-done | bytes 262176 | tf_op jit(solution)/shard_map/ppermute | solution.py:22
  17.4 3.6 %shard_map.155 = (f32[3328,128]{1,0:T(8,128)S(1)}, f32[3328,128]{1,0:T(8,128)S(1)}, bf16[13,128,256]{2,1,0:T(8,128)(2,1)S(1)}, f32[128,1024]{1,0:T(8,128)S(1)}) custom-call(s32[4]{0:T(128)S(1)} %bitcast.17, s32[4,1024]{1,0:T(4,128)S(1)} %bitcast.31, s32[4,1024]{1,0:T(4,128)S(1)} %bitcast.35, bf16[1024,128]{1,0:T(8,128)(2,1)S(1)} %collective-permute-done.src1, ...), custom_call_target="tpu_custom_call" | custom-call | flops 2000000000 | tf_op jit(solution)/shard_map/pallas_call | solution.py:379
  21.0 9.5 %shard_map.156 = (bf16[1024,128]{1,0:T(8,128)(2,1)S(1)}, bf16[1024,128]{1,0:T(8,128)(2,1)S(1)}, bf16[2304,128]{1,0:T(8,128)(2,1)S(1)}, f32[128,1024]{1,0:T(8,128...) custom-call(s32[4]{0:T(128)S(1)} %bitcast.18, ...), custom_call_target="tpu_custom_call" | custom-call | flops 8000000000 | tf_op jit(solution)/shard_map/pallas_call | solution.py:379
  30.6 2.8 %shard_map.157 = (bf16[1024,128]{1,0:T(8,128)(2,1)S(1)}, bf16[3328,128]{1,0:T(8,128)(2,1)S(1)}, f32[128,1024]{1,0:T(8,128)S(1)}, f32[128,1024]{1,0:T(8,128)S(1)}...) custom-call(s32[4]{0:T(128)S(1)} %bitcast.19, s32[4,1024]{1,0:T(4,128)S(1)} %bitcast.33, s32[4,1024]{1,0:T(4,128)S(1)} %bitcast.37, ...), custom_call_target="tpu_custom_call" | custom-call | flops 8000000000 | tf_op jit(solution)/shard_map/pallas_call | solution.py:379
  33.4 3.6 %collective-permute-done.3 = bf16[1024,128]{1,0:T(8,128)(2,1)S(1)} collective-permute-done((bf16[1024,128]{1,0:T(8,128)(2,1)S(1)}, bf16[1024,128]{1,0:T(8,128)(2,1)S(1)}, u32[]{:S(2)}, u32[]{:S(2)}) %collective-permute-start.3) | collective-permute-done | bytes 262176 | tf_op jit(solution)/shard_map/ppermute | solution.py:484
  37.0 1.3 %collective-permute-start.8 = (bf16[1024,128]{1,0:T(8,128)(2,1)S(1)}, bf16[1024,128]{1,0:T(8,128)(2,1)S(1)}, u32[]{:S(2)}, u32[]{:S(2)}) collective-permute-start(bf16[1024,128]{1,0:T(8,128)(2,1)S(1)} %get-tuple-element.50), channel_id=1, source_target_pairs={{8,0},{16,8},{24,16},{9,1},{17,9},{25,17},{10,2},{18,10},{26,18},{... | collective-permute-start | bytes 786440 | tf_op jit(solution)/shard_map/ppermute | solution.py:22
  38.3 3.4 %collective-permute-start.7 = (bf16[448,128]{1,0:T(8,128)(2,1)S(1)}, bf16[448,128]{1,0:T(8,128)(2,1)S(1)}, u32[]{:S(2)}, u32[]{:S(2)}) collective-permute-start(bf16[448,128]{1,0:T(8,128)(2,1)S(1)} %add_convert_fusion.2), channel_id=1, source_target_pairs={{0,6},{1,7},{2,4},{3,5},{4,2},{5,3},{6,0},{7,1},{8,14},{9,15},{10,... | collective-permute-start | bytes 344072 | tf_op jit(solution)/shard_map/ppermute | solution.py:394
  41.7 1.0 %collective-permute-start.5 = (bf16[448,128]{1,0:T(8,128)(2,1)S(1)}, bf16[448,128]{1,0:T(8,128)(2,1)S(1)}, u32[]{:S(2)}, u32[]{:S(2)}) collective-permute-start(bf16[448,128]{1,0:T(8,128)(2,1)S(1)} %add_convert_fusion.2), channel_id=1, source_target_pairs={{0,2},{1,3},{2,0},{3,1},{4,6},{5,7},{6,4},{7,5},{8,10},{9,11},{10,... | collective-permute-start | bytes 344072 | tf_op jit(solution)/shard_map/ppermute | solution.py:394
  42.8 3.5 %collective-permute-start.9 = (bf16[1024,128]{1,0:T(8,128)(2,1)S(1)}, bf16[1024,128]{1,0:T(8,128)(2,1)S(1)}, u32[]{:S(2)}, u32[]{:S(2)}) collective-permute-start(bf16[1024,128]{1,0:T(8,128)(2,1)S(1)} %add_convert_fusion), channel_id=1, source_target_pairs={{0,1},{1,0},{2,3},{3,2},{4,5},{5,4},{6,7},{7,6},{8,9},{9,8},{10,11... | collective-permute-start | bytes 786440 | tf_op jit(solution)/shard_map/ppermute | solution.py:499
  46.3 2.2 %shard_map.158 = (bf16[4,1024,128]{2,1,0:T(8,128)(2,1)}, f32[1024,128]{1,0:T(8,128)S(1)}) custom-call(s32[4]{0:T(128)S(1)} %bitcast.20, bf16[1024,128]{1,0:T(8,128)(2,1)S(1)} %bitcast.15, bf16[4096,128]{1,0:T(8,128)(2,1)S(1)} %bitcast.13, bf16[384,128]{1,0:T(8,128)(2,1)S(1)} %copy-done.2, bf16[256,128]{1,0:T(8,128)(2,1)S(1)} %copy-done.3, ...), custom_call_target="tpu_custom_call" | custom-call | flops 1000000 | tf_op jit(solution)/shard_map/pallas_call | solution.py:379
  48.5 3.1 %collective-permute-done.6 = bf16[448,128]{1,0:T(8,128)(2,1)S(1)} collective-permute-done((bf16[448,128]{1,0:T(8,128)(2,1)S(1)}, bf16[448,128]{1,0:T(8,128)(2,1)S(1)}, u32[]{:S(2)}, u32[]{:S(2)}) %collective-permute-start.6) | collective-permute-done | bytes 114720 | tf_op jit(solution)/shard_map/ppermute | solution.py:394
  51.7 1.4 %collective-permute-done.9 = bf16[1024,128]{1,0:T(8,128)(2,1)S(1)} collective-permute-done((bf16[1024,128]{1,0:T(8,128)(2,1)S(1)}, bf16[1024,128]{1,0:T(8,128)(2,1)S(1)}, u32[]{:S(2)}, u32[]{:S(2)}) %collective-permute-start.9) | collective-permute-done | bytes 262176 | tf_op jit(solution)/shard_map/ppermute | solution.py:499
  53.0 0.9 %convert_add_fusion = f32[1024,128]{1,0:T(8,128)} fusion(bf16[1024,128]{1,0:T(8,128)(2,1)S(1)} %collective-permute-done.9, f32[1024,128]{1,0:T(8,128)S(1)} %get-tuple-element.49, bf16[1024,128]{1,0:T(8,128)(2,1)S(1)} %collective-permute-done.8), kind=kLoop, calls=%fused_computation | loop fusion | flops 524288 | bytes 1572864 | tf_op jit(solution)/shard_map/add | solution.py:512
  53.9 2.9 %collective-permute-start.11 = (bf16[448,128]{1,0:T(8,128)(2,1)S(1)}, bf16[448,128]{1,0:T(8,128)(2,1)S(1)}, u32[]{:S(2)}, u32[]{:S(2)}) collective-permute-start(bf16[448,128]{1,0:T(8,128)(2,1)S(1)} %convert_add_fusion.1), channel_id=1, source_target_pairs={{0,16},{1,17},{2,18},{3,19},{4,20},{5,21},{6,22},{7,23},{8,24},{9,... | collective-permute-start | bytes 344072 | tf_op jit(solution)/shard_map/ppermute | solution.py:394
  56.8 2.2 %collective-permute-start.10 = (bf16[448,128]{1,0:T(8,128)(2,1)S(1)}, bf16[448,128]{1,0:T(8,128)(2,1)S(1)}, u32[]{:S(2)}, u32[]{:S(2)}) collective-permute-start(bf16[448,128]{1,0:T(8,128)(2,1)S(1)} %convert_add_fusion.1), channel_id=1, source_target_pairs={{0,1},{1,0},{2,3},{3,2},{4,5},{5,4},{6,7},{7,6},{8,9},{9,8},{10,11... | collective-permute-start | bytes 344072 | tf_op jit(solution)/shard_map/ppermute | solution.py:394
  59.0 0.6 collective-permute-done.11
  59.6 3.4 %collective-permute-done.10 = bf16[448,128]{1,0:T(8,128)(2,1)S(1)} collective-permute-done((bf16[448,128]{1,0:T(8,128)(2,1)S(1)}, bf16[448,128]{1,0:T(8,128)(2,1)S(1)}, u32[]{:S(2)}, u32[]{:S(2)}) %collective-permute-start.10) | collective-permute-done | bytes 114720 | tf_op jit(solution)/shard_map/ppermute | solution.py:394
  63.0 1.7 %collective-permute-done.12 = bf16[448,128]{1,0:T(8,128)(2,1)S(1)} collective-permute-done((bf16[448,128]{1,0:T(8,128)(2,1)S(1)}, bf16[448,128]{1,0:T(8,128)(2,1)S(1)}, u32[]{:S(2)}, u32[]{:S(2)}) %collective-permute-start.12) | collective-permute-done | bytes 114720 | tf_op jit(solution)/shard_map/ppermute | solution.py:394
  64.9 1.3 %collective-permute-done.13.theirs = bf16[448,128]{1,0:T(8,128)(2,1)S(1)} collective-permute-done((bf16[448,128]{1,0:T(8,128)(2,1)S(1)}, bf16[448,128]{1,0:T(8,128)(2,1)S(1)}, u32[]{:S(2)}, u32[]{:S(2)}) %collective-permute-start.13) | collective-permute-done | bytes 114720 | tf_op jit(solution)/shard_map/ppermute | solution.py:394
  66.2 1.3 %shard_map.159 = (f32[384,128]{1,0:T(8,128)}, f32[128,128]{1,0:T(8,128)}, f32[256,128]{1,0:T(8,128)}, f32[128,128]{1,0:T(8,128)}) custom-call(s32[2]{0:T(128)S(1)} %pad_add_fusion.me, bf16[448,128]{1,0:T(8,128)(2,1)S(1)} %add_convert_fusion.1.mine, bf16[448,128]{1,0:T(8,128)(2,1)S(1)} %collective-permute-done.13.theirs), custom_call_target="tpu_custom_call" | custom-call | flops 1000000 | tf_op jit(solution)/shard_map/pallas_call | solution.py:379
  (38 shorter events, 0.5 us)
Async XLA Ops:
  0.6 20.3 %collective-permute-start.2 = (bf16[1024,128]{1,0:T(8,128)(2,1)}, bf16[1024,128]{1,0:T(8,128)(2,1)S(1)}, u32[]{:S(2)}, u32[]{:S(2)}) collective-permute-start(bf16[1024,128]{1,0:T(8,128)(2,1)} %bitcast.24), channel_id=1, source_target_pairs={{0,7},{1,0},{2,1},{3,2},{4,3},{5,4},{6,5},{7,6},{8,15},{9,8},{10,9... | collective-permute-start | bytes 786440 | tf_op jit(solution)/shard_map/ppermute | solution.py:22
  6.7 10.7 %collective-permute-start.1 = (bf16[1024,128]{1,0:T(8,128)(2,1)}, bf16[1024,128]{1,0:T(8,128)(2,1)S(1)}, u32[]{:S(2)}, u32[]{:S(2)}) collective-permute-start(bf16[1024,128]{1,0:T(8,128)(2,1)} %bitcast.25), channel_id=1, source_target_pairs={{0,1},{1,2},{2,3},{3,4},{4,5},{5,6},{6,7},{7,0},{8,9},{9,10},{10,1... | collective-permute-start | bytes 786440 | tf_op jit(solution)/shard_map/ppermute | solution.py:22
  6.7 10.7 %collective-permute-start = (bf16[1024,128]{1,0:T(8,128)(2,1)}, bf16[1024,128]{1,0:T(8,128)(2,1)S(1)}, u32[]{:S(2)}, u32[]{:S(2)}) collective-permute-start(bf16[1024,128]{1,0:T(8,128)(2,1)} %bitcast.26), channel_id=1, source_target_pairs={{0,8},{8,16},{16,24},{1,9},{9,17},{17,25},{2,10},{10,18},{18,26},{... | collective-permute-start | bytes 786440 | tf_op jit(solution)/shard_map/ppermute | solution.py:22
  8.1 9.2 %copy-start.2 = (bf16[384,128]{1,0:T(8,128)(2,1)S(1)}, bf16[384,128]{1,0:T(8,128)(2,1)}, u32[]{:S(2)}) copy-start(bf16[384,128]{1,0:T(8,128)(2,1)} %w_in.7) | copy-start | bytes 294916
  8.1 9.2 %copy-start.4 = (s32[1,1,4]{2,1,0:T(1,128)S(1)}, s32[1,1,4]{2,1,0:T(1,128)}, u32[]{:S(2)}) copy-start(s32[1,1,4]{2,1,0:T(1,128)} %param.15) | copy-start | bytes 52
  8.2 9.2 %copy-start.9 = (s32[1,1,4,1024]{3,2,1,0:T(4,128)S(1)}, s32[1,1,4,1024]{3,2,1,0:T(4,128)}, u32[]{:S(2)}) copy-start(s32[1,1,4,1024]{3,2,1,0:T(4,128)} %param.13) | copy-start | bytes 49156
  8.2 9.2 %copy-start.10 = (s32[1,1,4,1024]{3,2,1,0:T(4,128)S(1)}, s32[1,1,4,1024]{3,2,1,0:T(4,128)}, u32[]{:S(2)}) copy-start(s32[1,1,4,1024]{3,2,1,0:T(4,128)} %param.14) | copy-start | bytes 49156
  12.7 8.3 %copy-start.1 = (bf16[1,1,1024,128]{3,2,1,0:T(8,128)(2,1)S(1)}, bf16[1,1,1024,128]{3,2,1,0:T(8,128)(2,1)}, u32[]{:S(2)}) copy-start(bf16[1,1,1024,128]{3,2,1,0:T(8,128)(2,1)} %param.16) | copy-start | bytes 786436
  12.7 8.3 %copy-start.3 = (bf16[256,128]{1,0:T(8,128)(2,1)S(1)}, bf16[256,128]{1,0:T(8,128)(2,1)}, u32[]{:S(2)}) copy-start(bf16[256,128]{1,0:T(8,128)(2,1)} %wn_in.3) | copy-start | bytes 196612
  12.7 8.3 %copy-start.5 = (bf16[1,1,4,1024,128]{4,3,2,1,0:T(8,128)(2,1)S(1)}, bf16[1,1,4,1024,128]{4,3,2,1,0:T(8,128)(2,1)}, u32[]{:S(2)}) copy-start(bf16[1,1,4,1024,128]{4,3,2,1,0:T(8,128)(2,1)} %param.12) | copy-start | bytes 3145732
  12.7 8.3 %copy-start.6 = (bf16[1,1,1024,128]{3,2,1,0:T(8,128)(2,1)S(1)}, bf16[1,1,1024,128]{3,2,1,0:T(8,128)(2,1)}, u32[]{:S(2)}) copy-start(bf16[1,1,1024,128]{3,2,1,0:T(8,128)(2,1)} %param.11) | copy-start | bytes 786436
  12.7 8.3 %copy-start.7 = (bf16[128,128]{1,0:T(8,128)(2,1)S(1)}, bf16[128,128]{1,0:T(8,128)(2,1)}, u32[]{:S(2)}) copy-start(bf16[128,128]{1,0:T(8,128)(2,1)} %wn_out.1) | copy-start | bytes 98308
  12.7 8.3 %copy-start.8 = (bf16[128,128]{1,0:T(8,128)(2,1)S(1)}, bf16[128,128]{1,0:T(8,128)(2,1)}, u32[]{:S(2)}) copy-start(bf16[128,128]{1,0:T(8,128)(2,1)} %w_out.3) | copy-start | bytes 98308
  30.5 6.4 %collective-permute-start.3 = (bf16[1024,128]{1,0:T(8,128)(2,1)S(1)}, bf16[1024,128]{1,0:T(8,128)(2,1)S(1)}, u32[]{:S(2)}, u32[]{:S(2)}) collective-permute-start(bf16[1024,128]{1,0:T(8,128)(2,1)S(1)} %get-tuple-element.42), channel_id=1, source_target_pairs={{0,6},{1,3},{2,0},{3,5},{4,2},{5,7},{6,4},{7,1},{8,14},{9,11},{10,... | collective-permute-start | bytes 786440 | tf_op jit(solution)/shard_map/ppermute | solution.py:484
  37.0 1.3 %collective-permute-start.4 = (bf16[448,128]{1,0:T(8,128)(2,1)S(1)}, bf16[448,128]{1,0:T(8,128)(2,1)S(1)}, u32[]{:S(2)}, u32[]{:S(2)}) collective-permute-start(bf16[448,128]{1,0:T(8,128)(2,1)S(1)} %get-tuple-element.43), channel_id=1, source_target_pairs={{0,8},{8,0},{16,24},{24,16},{1,9},{9,1},{17,25},{25,17},{2,10},{10... | collective-permute-start | bytes 344072 | tf_op jit(solution)/shard_map/ppermute | solution.py:504
  37.0 14.7 %collective-permute-start.8 = (bf16[1024,128]{1,0:T(8,128)(2,1)S(1)}, bf16[1024,128]{1,0:T(8,128)(2,1)S(1)}, u32[]{:S(2)}, u32[]{:S(2)}) collective-permute-start(bf16[1024,128]{1,0:T(8,128)(2,1)S(1)} %get-tuple-element.50), channel_id=1, source_target_pairs={{8,0},{16,8},{24,16},{9,1},{17,9},{25,17},{10,2},{18,10},{26,18},{... | collective-permute-start | bytes 786440 | tf_op jit(solution)/shard_map/ppermute | solution.py:22
  38.3 10.1 %collective-permute-start.7 = (bf16[448,128]{1,0:T(8,128)(2,1)S(1)}, bf16[448,128]{1,0:T(8,128)(2,1)S(1)}, u32[]{:S(2)}, u32[]{:S(2)}) collective-permute-start(bf16[448,128]{1,0:T(8,128)(2,1)S(1)} %add_convert_fusion.2), channel_id=1, source_target_pairs={{0,6},{1,7},{2,4},{3,5},{4,2},{5,3},{6,0},{7,1},{8,14},{9,15},{10,... | collective-permute-start | bytes 344072 | tf_op jit(solution)/shard_map/ppermute | solution.py:394
  41.7 9.9 %collective-permute-start.6 = (bf16[448,128]{1,0:T(8,128)(2,1)S(1)}, bf16[448,128]{1,0:T(8,128)(2,1)S(1)}, u32[]{:S(2)}, u32[]{:S(2)}) collective-permute-start(bf16[448,128]{1,0:T(8,128)(2,1)S(1)} %add_convert_fusion.2), channel_id=1, source_target_pairs={{0,4},{1,5},{2,6},{3,7},{4,0},{5,1},{6,2},{7,3},{8,12},{9,13},{10,... | collective-permute-start | bytes 344072 | tf_op jit(solution)/shard_map/ppermute | solution.py:394
  41.7 9.9 %collective-permute-start.5 = (bf16[448,128]{1,0:T(8,128)(2,1)S(1)}, bf16[448,128]{1,0:T(8,128)(2,1)S(1)}, u32[]{:S(2)}, u32[]{:S(2)}) collective-permute-start(bf16[448,128]{1,0:T(8,128)(2,1)S(1)} %add_convert_fusion.2), channel_id=1, source_target_pairs={{0,2},{1,3},{2,0},{3,1},{4,6},{5,7},{6,4},{7,5},{8,10},{9,11},{10,... | collective-permute-start | bytes 344072 | tf_op jit(solution)/shard_map/ppermute | solution.py:394
  42.8 10.2 %collective-permute-start.9 = (bf16[1024,128]{1,0:T(8,128)(2,1)S(1)}, bf16[1024,128]{1,0:T(8,128)(2,1)S(1)}, u32[]{:S(2)}, u32[]{:S(2)}) collective-permute-start(bf16[1024,128]{1,0:T(8,128)(2,1)S(1)} %add_convert_fusion), channel_id=1, source_target_pairs={{0,1},{1,0},{2,3},{3,2},{4,5},{5,4},{6,7},{7,6},{8,9},{9,8},{10,11... | collective-permute-start | bytes 786440 | tf_op jit(solution)/shard_map/ppermute | solution.py:499
  53.9 5.7 %collective-permute-start.11 = (bf16[448,128]{1,0:T(8,128)(2,1)S(1)}, bf16[448,128]{1,0:T(8,128)(2,1)S(1)}, u32[]{:S(2)}, u32[]{:S(2)}) collective-permute-start(bf16[448,128]{1,0:T(8,128)(2,1)S(1)} %convert_add_fusion.1), channel_id=1, source_target_pairs={{0,16},{1,17},{2,18},{3,19},{4,20},{5,21},{6,22},{7,23},{8,24},{9,... | collective-permute-start | bytes 344072 | tf_op jit(solution)/shard_map/ppermute | solution.py:394
  56.8 6.2 %collective-permute-start.10 = (bf16[448,128]{1,0:T(8,128)(2,1)S(1)}, bf16[448,128]{1,0:T(8,128)(2,1)S(1)}, u32[]{:S(2)}, u32[]{:S(2)}) collective-permute-start(bf16[448,128]{1,0:T(8,128)(2,1)S(1)} %convert_add_fusion.1), channel_id=1, source_target_pairs={{0,1},{1,0},{2,3},{3,2},{4,5},{5,4},{6,7},{7,6},{8,9},{9,8},{10,11... | collective-permute-start | bytes 344072 | tf_op jit(solution)/shard_map/ppermute | solution.py:394
  59.0 5.7 %collective-permute-start.12 = (bf16[448,128]{1,0:T(8,128)(2,1)S(1)}, bf16[448,128]{1,0:T(8,128)(2,1)S(1)}, u32[]{:S(2)}, u32[]{:S(2)}) collective-permute-start(bf16[448,128]{1,0:T(8,128)(2,1)S(1)} %convert_add_fusion.1), channel_id=1, source_target_pairs={{0,17},{1,16},{2,19},{3,18},{4,21},{5,20},{6,23},{7,22},{8,25},{9,... | collective-permute-start | bytes 344072 | tf_op jit(solution)/shard_map/ppermute | solution.py:394
  64.8 1.4 %collective-permute-start.13 = (bf16[448,128]{1,0:T(8,128)(2,1)S(1)}, bf16[448,128]{1,0:T(8,128)(2,1)S(1)}, u32[]{:S(2)}, u32[]{:S(2)}) collective-permute-start(bf16[448,128]{1,0:T(8,128)(2,1)S(1)} %add_convert_fusion.1.mine), channel_id=1, source_target_pairs={{0,8},{1,9},{2,10},{3,11},{4,12},{5,13},{6,14},{7,15},{8,0},{9,1},... | collective-permute-start | bytes 344072 | tf_op jit(solution)/shard_map/ppermute | solution.py:394
  (1 other events, 8.2 us)

commit v3 on v2

--- a/solution.py
+++ b/solution.py
@@ -10,6 +10,9 @@
 norm_eps = 1e-05
 bf16, f32 = jnp.bfloat16, jnp.float32
 SPAN = 256
+FOLD = 4
+FORWARD = 2
+BACKWARD = 2
 VMEM_BYTES = 16 * 1024 * 1024
 
 
@@ -39,12 +42,42 @@
     return upper, (x - upper.astype(f32)).astype(bf16)
 
 
-def row_select(idx_row, nodes):
-    edges = idx_row.shape[1]
-    col = jnp.broadcast_to(idx_row, (128, edges)).T
-    lane = lax.broadcasted_iota(jnp.int32, (edges, 128), 1)
-    parts = [jnp.where(col == lane + c * 128, 1.0, 0.0).astype(bf16) for c in range(nodes // 128)]
-    return jnp.concatenate(parts, axis=1)
+def folded(table):
+    width = table.shape[0] // FOLD
+    return jnp.concatenate([table[f * width : (f + 1) * width] for f in range(FOLD)], axis=1)
+
+
+def unfolded_sums(sums):
+    d = sums.shape[0] // FOLD
+    return jnp.concatenate([sums[f * d : (f + 1) * d] for f in range(FOLD)], axis=1)
+
+
+class Slots:
+    def __init__(self, idx_row, nodes):
+        edges = idx_row.shape[1]
+        chunks = nodes // FOLD // 128
+        block = idx_row >> 7
+        self.part = block // chunks
+        low = jnp.broadcast_to((idx_row & 127).astype(f32).astype(bf16), (128, edges)).T
+        chunk = (block - self.part * chunks).astype(f32).astype(bf16)
+        chunk = jnp.broadcast_to(chunk, (128, edges)).T
+        self.part_rows = jnp.broadcast_to(self.part.astype(f32), (128, edges)).T
+        lane = lax.broadcasted_iota(jnp.int32, (edges, 128), 1).astype(f32).astype(bf16)
+        one = jnp.where(low == lane, bf16(1), bf16(0))
+        hots = [jnp.where(chunk == bf16(c), one, bf16(0)) for c in range(chunks)]
+        self.hot = jnp.concatenate(hots, axis=1)
+
+    def rows(self, table):
+        wide = dot(self.hot, table)
+        d = wide.shape[1] // FOLD
+        out = wide[:, :d]
+        for f in range(1, FOLD):
+            out = jnp.where(self.part_rows == f, wide[:, f * d : (f + 1) * d], out)
+        return out
+
+    def sums(self, turned):
+        parts = [jnp.where(self.part == f, turned, 0.0).astype(bf16) for f in range(FOLD)]
+        return dot(jnp.concatenate(parts, axis=0), self.hot)
 
 
 def normed(pre):
@@ -89,6 +122,23 @@
         store = jnp.where(real, row - self.first * self.cap, self.held * self.cap)
         return Place(kind, at, offset, rest, row, row - self.first * self.cap, store)
 
+    def pipelined(self, front, back, held, group):
+        steps = (self.ends[-1] + group - 1) // group
+
+        def places(i):
+            return [self.place(group * i + j) for j in range(group)]
+
+        def looped(i, carry):
+            back(places(i - 1), held[...])
+            held[...] = front(places(i))
+            return carry
+
+        @pl.when(steps > 0)
+        def _():
+            held[...] = front(places(0))
+            lax.fori_loop(1, steps, looped, 0)
+            back(places(steps - 1), held[...])
+
     def run(self, step, group=2):
         def looped(i, carry):
             step([self.place(group * i + j) for j in range(group)])
@@ -132,11 +182,11 @@
         ref[p.stored, :] = value[i * SPAN : (i + 1) * SPAN]
 
 
-def receiver_forward(tiles, recv, hit, edges, w_in, part):
-    nodes, d = hit.shape
+def receiver_forward(tiles, recv, table, edges, w_in, part):
+    nodes, d = table.shape[0] * FOLD, w_in.shape[1]
 
     def step(places):
-        picked = dot(row_select(slots_of(recv, places), nodes), hit[...]).astype(bf16)
+        picked = Slots(slots_of(recv, places), nodes).rows(table[...]).astype(bf16)
         pre = dot(picked, w_in[d : 2 * d, :]) + dot(rows_of(edges, places), w_in[2 * d :, :])
         store_rows(part, places, pre)
 
@@ -144,64 +194,68 @@
 
 
 def sender_part(places, send, source, w_in):
-    nodes, d = source.shape[1:]
-    picked = [dot(row_select(p.slots(send), nodes), source[p.at]) for p in places]
+    nodes, d = source.shape[1] * FOLD, w_in.shape[1]
+    picked = [Slots(p.slots(send), nodes).rows(source[p.at]) for p in places]
     return dot(jnp.concatenate(picked, axis=0).astype(bf16), w_in[:d, :])
 
 
-def forward(tiles, group, send, recv, source, w_in, part, u_all, rs_all, hidden_all, total):
-    d, nodes = total.shape
-
-    def step(places):
+def forward(tiles, send, recv, source, w_in, part, held, u_all, rs_all, hidden_all, total):
+    d = w_in.shape[1]
+    nodes = total.shape[1] * FOLD
+
+    def front(places):
         pre = rows_of(part, places)
         if source is not None:
             pre += sender_part(places, send, source, w_in)
         u, rstd = normed(pre)
         store_rows(u_all, places, u)
         store_rows(rs_all, places, jnp.broadcast_to(rstd, u.shape))
-        hidden = jnp.where(live_of(places, d), u * gate(u), 0.0).T.astype(bf16)
+        hidden = jnp.where(live_of(places, d), u * gate(u), 0.0).T
         for i, p in enumerate(places):
-            hidden_all[p.tile] = hidden[:, i * SPAN : (i + 1) * SPAN]
-        total[...] += dot(hidden, row_select(slots_of(recv, places), nodes))
-
-    tiles.run(step, group)
+            hidden_all[p.tile] = hidden[:, i * SPAN : (i + 1) * SPAN].astype(bf16)
+        return hidden
+
+    def back(places, hidden):
+        total[...] += Slots(slots_of(recv, places), nodes).sums(hidden)
+
+    tiles.pipelined(front, back, held, FORWARD)
 
 
 def local_kernel(
     counts_far, send_far, recv_far, hit_far, edges_far, w_in_far,
     part,
-    counts, send, recv, hit, edges, w_in, arrived,
+    counts, send, recv, hit, edges, w_in, table, arrived,
 ):
     far = (counts_far, send_far, recv_far, hit_far, edges_far, w_in_far)
-    near = (counts, send, recv, hit.at[0], edges, w_in)
+    near = (counts, send, recv, hit, edges, w_in)
     copies = [pltpu.make_async_copy(f, n, arrived.at[i]) for i, (f, n) in enumerate(zip(far, near))]
     for copy in copies:
         copy.start()
     for copy in copies:
         copy.wait()
+    table[0] = folded(hit[...])
     kinds, cap = send.shape
     tiles = Tiles(counts, tuple(range(kinds)), cap, 0, kinds)
-    receiver_forward(tiles, recv, hit.at[0], edges, w_in, part)
+    receiver_forward(tiles, recv, table.at[0], edges, w_in, part)
 
     def step(places):
-        store_rows(part, places, rows_of(part, places) + sender_part(places, send, hit, w_in))
+        store_rows(part, places, rows_of(part, places) + sender_part(places, send, table, w_in))
 
     Tiles(counts, (0,), cap, 0, kinds).run(step, 4)
 
 
 def early_kernel(
-    counts, send, recv, src1, src2, w_in, part,
+    counts, send, recv, src1, w_in, part,
     u_all, rs_all, hidden_all, total,
-    source,
+    source, held,
 ):
     total[...] = jnp.zeros_like(total)
     hidden_all[hidden_all.shape[0] - 1] = jnp.zeros(hidden_all.shape[1:], bf16)
-    source[0] = src1[...]
-    source[1] = src2[...]
+    source[0] = folded(src1[...])
     cap = send.shape[1]
     results = (u_all, rs_all, hidden_all, total)
-    forward(Tiles(counts, (0,), cap, 0, 3), 4, send, recv, None, w_in, part, *results)
-    forward(Tiles(counts, (1, 2), cap, 0, 3), 4, send, recv, source, w_in, part, *results)
+    forward(Tiles(counts, (0,), cap, 0, 2), send, recv, None, w_in, part, held, *results)
+    forward(Tiles(counts, (1,), cap, 0, 2), send, recv, source, w_in, part, held, *results)
 
 
 def both_halves(x, axis):
@@ -210,14 +264,13 @@
 
 def backward(
     tiles, send, recv, edges, grad_edge, w_out, inc_grad, u_all, rs_all, hidden_all,
-    edge_back, recv_sum, send_sum, edge_turned, out_sum,
+    held, edge_back, recv_sum, send_sum, edge_turned, out_sum,
 ):
-    nodes = inc_grad.shape[0]
+    nodes = inc_grad.shape[0] * FOLD
     d = w_out.shape[0]
 
-    def step(places):
-        recv_hot = row_select(slots_of(recv, places), nodes)
-        picked = dot(recv_hot, inc_grad[...])
+    def front(places):
+        picked = Slots(slots_of(recv, places), nodes).rows(inc_grad[...])
         live = live_of(places, d)
         grad_rows = rows_of(grad_edge, places).astype(f32)
         message_grad = jnp.where(live, grad_rows + picked, 0.0).astype(bf16)
@@ -226,54 +279,48 @@
         pre_grad = normed_back(u, own_rows_of(rs_all, places), gate(u), hidden_grad)
         pre_grad = jnp.where(live, pre_grad, 0.0)
         store_rows(edge_back, places, pre_grad.astype(bf16))
-        pre_grad = pre_grad.T.astype(bf16)
-        recv_sum[...] += dot(pre_grad, recv_hot)
-        edge_turned[...] += dot(pre_grad, rows_of(edges, places))
         hidden = jnp.concatenate([hidden_all[p.tile] for p in places], axis=1)
         out_sum[...] += dot(hidden, message_grad)
+        return pre_grad.T
+
+    def back(places, pre_grad):
+        recv_sum[...] += Slots(slots_of(recv, places), nodes).sums(pre_grad)
+        edge_turned[...] += dot(pre_grad.astype(bf16), rows_of(edges, places))
         for i, p in enumerate(places):
             part_grad = pre_grad[:, i * SPAN : (i + 1) * SPAN]
-            send_sum[p.at] += dot(part_grad, row_select(p.slots(send), nodes))
-
-    tiles.run(step)
+            send_sum[p.at] += Slots(p.slots(send), nodes).sums(part_grad)
+
+    tiles.pipelined(front, back, held, BACKWARD)
 
 
 def senders_back(send_sum, w_in):
     d = w_in.shape[1]
     w_send = jnp.concatenate([w_in[:d, :], w_in[:d, :]], axis=1)
-    return dot(w_send, both_halves(send_sum, 0)).T.astype(bf16)
+    return dot(w_send, both_halves(unfolded_sums(send_sum), 0)).T.astype(bf16)
 
 
 def turned_product(sums, table):
-    both = dot(both_halves(sums, 0), table)
+    both = dot(both_halves(unfolded_sums(sums), 0), table)
     d = table.shape[1]
     return both[:d] + both[d:]
 
 
 def node_kernel(
     counts, send, recv, hit, src2, src3, edges, grad_hit, grad_edge,
-    w_in, w_out, wn_in, wn_out, part, u0, rs0, hidden0, total_in, me,
+    w_in, w_out, wn_in, wn_out, part, total_in, odd,
     far_back, near_back, edge_back, recv_sum, node_back, inc_grad, partial,
-    source, send_sum, u_all, rs_all, hidden_all, total, moved,
+    source, send_sum, u_all, rs_all, hidden_all, total, held, held_back,
 ):
     nodes, d = hit.shape
     cap = send.shape[1]
     near = cap // SPAN
-    second = slice(2 * cap, 3 * cap)
-    parts = (
-        (u0.at[second], u_all.at[:cap]),
-        (rs0.at[second], rs_all.at[:cap]),
-        (hidden0.at[2 * near : 3 * near], hidden_all.at[:near]),
-    )
-    moves = [pltpu.make_async_copy(a, b, moved.at[i]) for i, (a, b) in enumerate(parts)]
-    for move in moves:
-        move.start()
     hidden_all[2 * near] = jnp.zeros(hidden_all.shape[1:], bf16)
     total[...] = total_in[...]
-    source[0] = src3[...]
+    source[0] = folded(src2[...])
+    source[1] = folded(src3[...])
     results = (u_all, rs_all, hidden_all, total)
-    forward(Tiles(counts, (3,), cap, 2, 2), 2, send, recv, source, w_in, part, *results)
-    upper, lower = halves(total[...].T)
+    forward(Tiles(counts, (2, 3), cap, 2, 2), send, recv, source, w_in, part, held, *results)
+    upper, lower = halves(unfolded_sums(total[...]).T)
     incoming = (dot(upper, w_out[...]) + dot(lower, w_out[...])).astype(bf16)
     u, rstd = normed(dot(hit[...], wn_in[:d, :]) + dot(incoming, wn_in[d:, :]))
     sig = gate(u)
@@ -281,38 +328,36 @@
     hidden_grad = dot_nt(grad_hit[...], wn_out[...])
     pre_grad = normed_back(u, rstd, sig, hidden_grad).astype(bf16)
     node_back[...] = pre_grad
-    inc_grad[...] = dot_nt(pre_grad, wn_in[d:, :]).astype(bf16)
+    inc_grad[...] = folded(dot_nt(pre_grad, wn_in[d:, :]).astype(bf16))
     partial[6 * d : 7 * d, :] = dot_tn(hidden, grad_hit[...])
     partial[4 * d : 5 * d, :] = dot_tn(hit[...], pre_grad)
     partial[5 * d : 6 * d, :] = dot_tn(incoming, pre_grad)
     partial[2 * d : 4 * d, :] = jnp.zeros((2 * d, d), f32)
     recv_sum[...] = jnp.zeros_like(recv_sum)
     send_sum[...] = jnp.zeros_like(send_sum)
-    for move in moves:
-        move.wait()
     backward(
         Tiles(counts, (2, 3), cap, 2, 2), send, recv, edges, grad_edge, w_out, inc_grad,
-        u_all, rs_all, hidden_all, edge_back, recv_sum, send_sum,
+        u_all, rs_all, hidden_all, held_back, edge_back, recv_sum, send_sum,
         partial.at[2 * d : 3 * d], partial.at[3 * d : 4 * d],
     )
     partial[:d, :] = turned_product(send_sum[0], src2[...]) + turned_product(send_sum[1], src3[...])
-    far_back[...] = senders_back(send_sum[me[1]], w_in)
-    near_back[...] = senders_back(send_sum[1 - me[1]], w_in)
+    far_back[...] = senders_back(send_sum[odd[0]], w_in)
+    near_back[...] = senders_back(send_sum[1 - odd[0]], w_in)
 
 
 def last_kernel(
     counts, send, recv, hit, src1, edges, grad_edge, w_in, w_out,
     u0, rs0, hidden0, recv_in, inc_grad, partial, me,
     back1, edge_back, recv_sum, send0, mine, other,
-    send_sum, weights,
+    send_sum, weights, held,
 ):
     cap, d = send.shape[1], hit.shape[1]
     weights[...] = partial[...]
     recv_sum[...] = recv_in[...]
     send_sum[...] = jnp.zeros_like(send_sum)
     backward(
-        Tiles(counts, (0, 1), cap, 0, 3), send, recv, edges, grad_edge, w_out, inc_grad,
-        u0, rs0, hidden0, edge_back, recv_sum, send_sum,
+        Tiles(counts, (0, 1), cap, 0, 2), send, recv, edges, grad_edge, w_out, inc_grad,
+        u0, rs0, hidden0, held, edge_back, recv_sum, send_sum,
         weights.at[2 * d : 3 * d], weights.at[3 * d : 4 * d],
     )
     turned = turned_product(send_sum[0], hit[...]) + turned_product(send_sum[1], src1[...])
@@ -339,7 +384,7 @@
         grad_rows = grad_edge[k * cap : (k + 1) * cap, :].astype(f32)
         edge_done[k] = (grad_rows + jnp.where(live, through, 0.0)).astype(bf16)
     ends = jnp.concatenate([w_in[d : 2 * d, :]] * 2 + [w_in[:d, :]] * 2, axis=1)
-    sums = jnp.concatenate([both_halves(recv_sum[...], 0), both_halves(send0[...], 0)], axis=0)
+    sums = jnp.concatenate([both_halves(unfolded_sums(s[...]), 0) for s in (recv_sum, send0)], axis=0)
     hit_done[...] = (
         grad_hit[...].astype(f32) + dot_nt(node_back[...], wn_in[:d, :]) + dot(ends, sums).T
     )
@@ -387,7 +432,7 @@
     )(*operands)
 
 
-def summed_over_chips(mine, total, sectors, beside):
+def summed_over_chips(mine, total, sectors, arrived, finish):
     axes = ("layer", "phi")
 
     def swap(value, mask):
@@ -403,8 +448,9 @@
         sent = mine.astype(bf16)
         mine = sum((swap(sent, m).astype(f32) for m in masks), sent.astype(f32))
         if at == 0:
-            mine, beside = lax.optimization_barrier((mine, beside))
-    mine = mine.astype(bf16)
+            mine, arrived = lax.optimization_barrier((mine, arrived))
+            beside = finish(arrived)
+    mine, beside = lax.optimization_barrier((mine.astype(bf16), beside))
     return mine, swap(mine, sectors), beside
 
 
@@ -420,7 +466,8 @@
     grad_hit = grad_hits[0, 0]
     layers, sectors = lax.axis_size("layer"), lax.axis_size("phi")
     devices = layers * sectors
-    me = jnp.stack([lax.axis_index("layer") % 2, lax.axis_index("phi") % 2]).astype(jnp.int32)
+    me = (lax.axis_index("layer") % 2).astype(jnp.int32).reshape(1)
+    odd = (lax.axis_index("phi") % 2).astype(jnp.int32).reshape(1)
     src2 = shifted(hit, "phi", 1, True)
     src3 = shifted(hit, "phi", -1, True)
     src1 = shifted(hit, "layer", 1, False)
@@ -434,7 +481,7 @@
     def tiles(count):
         return shape(count * cap // SPAN + 1, d, SPAN, dtype=bf16)
 
-    turned = shape(d, nodes)
+    turned = shape(FOLD * d, nodes // FOLD)
     node_half = shape(nodes, d, dtype=bf16)
     (part,) = on_device(
         local_kernel,
@@ -445,56 +492,64 @@
             pltpu.SMEM(counts.shape, jnp.int32),
             pltpu.VMEM(send.shape, jnp.int32),
             pltpu.VMEM(recv.shape, jnp.int32),
-            pltpu.VMEM((1, nodes, d), bf16),
+            pltpu.VMEM((nodes, d), bf16),
             pltpu.VMEM(edges.shape, bf16),
             pltpu.VMEM(w_edge_in.shape, bf16),
+            pltpu.VMEM((1, nodes // FOLD, FOLD * d), bf16),
             pltpu.SemaphoreType.DMA((6,)),
         ],
         hbm=True,
     )
     u0, rs0, hidden0, total = on_device(
         early_kernel,
-        [rows(3), rows(3), tiles(3), turned],
-        (counts, send, recv, src1, src2, w_edge_in, part),
+        [rows(2), rows(2), tiles(2), turned],
+        (counts, send, recv, src1, w_edge_in, part),
         2 * 10**9,
-        scratch=[pltpu.VMEM((2, nodes, d), bf16)],
+        scratch=[
+            pltpu.VMEM((1, nodes // FOLD, FOLD * d), bf16),
+            pltpu.VMEM((d, FORWARD * SPAN), f32),
+        ],
     )
     partial = shape(7 * d, d)
     far_back, near_back, second_back, recv_sum, node_back, inc_grad, partial = on_device(
         node_kernel,
         [
             node_half, node_half, shape(2 * cap + SPAN, d, dtype=bf16),
-            turned, node_half, node_half, partial,
+            turned, node_half, shape(nodes // FOLD, FOLD * d, dtype=bf16), partial,
         ],
         (counts, send, recv, hit, src2, src3, edges, grad_hit, grad_edge,
-         w_edge_in, w_edge_out, w_node_in, w_node_out, part, u0, rs0, hidden0, total, me),
+         w_edge_in, w_edge_out, w_node_in, w_node_out, part, total, odd),
         8 * 10**9,
         scratch=[
-            pltpu.VMEM((1, nodes, d), bf16),
-            pltpu.VMEM((2, d, nodes), f32),
+            pltpu.VMEM((2, nodes // FOLD, FOLD * d), bf16),
+            pltpu.VMEM((2, *turned.shape), f32),
             pltpu.VMEM((2 * cap + SPAN, d), f32),
             pltpu.VMEM((2 * cap + SPAN, d), f32),
             pltpu.VMEM((2 * cap // SPAN + 1, d, SPAN), bf16),
-            pltpu.VMEM((d, nodes), f32),
-            pltpu.SemaphoreType.DMA((3,)),
+            pltpu.VMEM(turned.shape, f32),
+            pltpu.VMEM((d, FORWARD * SPAN), f32),
+            pltpu.VMEM((d, BACKWARD * SPAN), f32),
         ],
-        scalars=(0, 18),
+        scalars=(0, 15),
     )
     route = [(i, (i + (2 if i % 2 else -2)) % sectors) for i in range(sectors)]
     relayed = lax.ppermute(far_back, "phi", route)
     back1, first_back, recv_sum, send0, mine, other = on_device(
         last_kernel,
         [
-            node_half, shape(3 * cap + SPAN, d, dtype=bf16), turned, turned,
+            node_half, shape(2 * cap + SPAN, d, dtype=bf16), turned, turned,
             shape(7 * d // 2, d), shape(7 * d // 2, d, dtype=bf16),
         ],
         (counts, send, recv, hit, src1, edges, grad_edge, w_edge_in, w_edge_out,
          u0, rs0, hidden0, recv_sum, inc_grad, partial, me),
         8 * 10**9,
-        scratch=[pltpu.VMEM((2, d, nodes), f32), pltpu.VMEM((7 * d, d), f32)],
+        scratch=[
+            pltpu.VMEM((2, *turned.shape), f32),
+            pltpu.VMEM((7 * d, d), f32),
+            pltpu.VMEM((d, BACKWARD * SPAN), f32),
+        ],
         scalars=(0, 15),
     )
-    from_upper = shifted(back1, "layer", -1, False)
     other, relayed = lax.optimization_barrier((other, relayed))
     from_beside = lax.ppermute(
         (near_back.astype(f32) + relayed.astype(f32)).astype(bf16),
@@ -509,8 +564,13 @@
          first_back, second_back, recv_sum, send0, node_back),
         10**6,
     )
-    hit_total = hit_done + from_upper.astype(f32) + from_beside.astype(f32)
-    mine, theirs, hit_total = summed_over_chips(mine, devices, sectors, hit_total)
+    hit_done, back1 = lax.optimization_barrier((hit_done, back1))
+    from_upper = shifted(back1, "layer", -1, False)
+
+    def hits(from_beside):
+        return hit_done + from_upper.astype(f32) + from_beside.astype(f32)
+
+    mine, theirs, hit_total = summed_over_chips(mine, devices, sectors, from_beside, hits)
     summed = on_device(
         functools.partial(closing_kernel, 1.0 / devices),
         [shape(3 * d, d), shape(d, d), shape(2 * d, d), shape(d, d)],

time: 67.5 us -> 63 us (0.933)
  waiting for transfers between devices: 19.7 us -> 15.2 us
  Pallas kernels: 23.8 us -> 19.9 us
  starting transfers between devices: 21.9 us -> 25.5 us
    ppermute x1, starting transfers between devices: 0.06 us -> 5.49 us  [body(): relayed = lax.ppermute(far_back, 'phi', route)]
    pallas_call x6, Pallas kernels: 23.8 us -> 19.9 us  [on_device(): pl.pallas_call(kernel, out_shape=outs, in_specs=in_specs, out_specs=[vmem...]
    ppermute x1, waiting for transfers between devices: 3.58 us -> 0.01 us  [body(): relayed = lax.ppermute(far_back, 'phi', route)]
    ppermute x7, waiting for transfers between devices: 10.1 us -> 8.05 us  [swap(): return lax.ppermute(value, axes, [(i, i ^ mask) for i in range(total)])]
    ppermute x1, waiting for transfers between devices: 1.38 us -> 0.01 us  [body(): lax.ppermute((near_back.astype(f32) + relayed.astype(f32)).astype(bf16),...]
    ppermute x1, waiting for transfers between devices: 0.03 us -> 1.31 us  [body(): lax.ppermute(other, 'layer', [(i, i ^ 1) for i in range(layers)])]
    ppermute x7, starting transfers between devices: 9.63 us -> 8.41 us  [swap(): return lax.ppermute(value, axes, [(i, i ^ mask) for i in range(total)])]
    ppermute x4, waiting for transfers between devices: 4.58 us -> 5.79 us  [shifted(): return lax.ppermute(value, axis, route)]
  transfers between devices with their start and end apart: 14 -> 14, of which waited for: 8 -> 7; matrix products, arithmetic and copies ran while one was open for 0% -> 2% of each run, Pallas kernels for 19% -> 19%
where the time goes in v3:
time: 63 us; the launch traced here: 62.6 us
  starting transfers between devices  25.5 us (40%)
  Pallas kernels  19.9 us (32%)
  waiting for transfers between devices  15.2 us (24%)
  other arithmetic  1.12 us (2%)
  between operations  0.89 us (1%)
    pallas_call x6, Pallas kernels, on_device(): pl.pallas_call(kernel, out_shape=outs, in_specs=in_specs, out_specs=[vmem...  19.9 us
    ppermute x4, starting transfers between devices, shifted(): return lax.ppermute(value, axis, route)  9.13 us
    ppermute x7, starting transfers between devices, swap(): return lax.ppermute(value, axes, [(i, i ^ mask) for i in range(total)])  8.41 us
    ppermute x7, waiting for transfers between devices, swap(): return lax.ppermute(value, axes, [(i, i ^ mask) for i in range(total)])  8.05 us
    ppermute x4, waiting for transfers between devices, shifted(): return lax.ppermute(value, axis, route)  5.79 us
    ppermute x1, starting transfers between devices, body(): relayed = lax.ppermute(far_back, 'phi', route)  5.49 us
    ppermute x1, starting transfers between devices, body(): lax.ppermute((near_back.astype(f32) + relayed.astype(f32)).astype(bf16),...  2.35 us
    ppermute x1, waiting for transfers between devices, body(): lax.ppermute(other, 'layer', [(i, i ^ 1) for i in range(layers)])  1.31 us
  transfers between devices with their start and end apart: 14, of which 7 were waited for; matrix products, arithmetic and copies ran while one was open for 2% of the time, Pallas kernels for 19%

profile of v3, /device:TPU:0, one launch (start us, length us, event | category | flops | bytes accessed | tf_op | source)
XLA Modules:
  0.0 62.6 jit_solution(11709957382083184384)
XLA Ops:
  0.6 2.4 %collective-permute-start = (bf16[1024,128]{1,0:T(8,128)(2,1)}, bf16[1024,128]{1,0:T(8,128)(2,1)S(1)}, u32[]{:S(2)}, u32[]{:S(2)}) collective-permute-start(bf16[1024,128]{1,0:T(8,128)(2,1)} %bitcast.24), channel_id=1, source_target_pairs={{0,8},{8,16},{16,24},{1,9},{9,17},{17,25},{2,10},{10,18},{18,26},{... | collective-permute-start | bytes 786440 | tf_op jit(solution)/shard_map/ppermute | solution.py:25
  3.0 2.4 %collective-permute-start.1 = (bf16[1024,128]{1,0:T(8,128)(2,1)}, bf16[1024,128]{1,0:T(8,128)(2,1)S(1)}, u32[]{:S(2)}, u32[]{:S(2)}) collective-permute-start(bf16[1024,128]{1,0:T(8,128)(2,1)} %bitcast.25), channel_id=1, source_target_pairs={{0,1},{1,2},{2,3},{3,4},{4,5},{5,6},{6,7},{7,0},{8,9},{9,10},{10,1... | collective-permute-start | bytes 786440 | tf_op jit(solution)/shard_map/ppermute | solution.py:25
  5.4 3.1 %collective-permute-start.2 = (bf16[1024,128]{1,0:T(8,128)(2,1)}, bf16[1024,128]{1,0:T(8,128)(2,1)S(1)}, u32[]{:S(2)}, u32[]{:S(2)}) collective-permute-start(bf16[1024,128]{1,0:T(8,128)(2,1)} %bitcast.26), channel_id=1, source_target_pairs={{0,7},{1,0},{2,1},{3,2},{4,3},{5,4},{6,5},{7,6},{8,15},{9,8},{10,9... | collective-permute-start | bytes 786440 | tf_op jit(solution)/shard_map/ppermute | solution.py:25
  8.5 3.6 %shard_map.154.part = f32[4352,128]{1,0:T(8,128)S(1)} custom-call(s32[4]{0:T(128)} %bitcast.16, s32[4,1024]{1,0:T(4,128)} %bitcast.30, s32[4,1024]{1,0:T(4,128)} %bitcast.34, bf16[1024,128]{1,0:T(8,128)(2,1)} %bitcast.27, bf16[4096,128]{1,0:T(8,128)(2,1)} %bitcast.21, bf16[384,128]{1,0:T(8,128)(2,1)} %w_in.7), custom_call_target="tpu_custom_call" | custom-call | flops 4000000000 | tf_op jit(solution)/shard_map/pallas_call | solution.py:424
  12.2 1.9 %shard_map.155 = (f32[2304,128]{1,0:T(8,128)S(1)}, f32[2304,128]{1,0:T(8,128)S(1)}, bf16[9,128,256]{2,1,0:T(8,128)(2,1)S(1)}, f32[512,256]{1,0:T(8,128)S(1)}) custom-call(s32[4]{0:T(128)S(1)} %bitcast.17, s32[4,1024]{1,0:T(4,128)S(1)} %bitcast.31, s32[4,1024]{1,0:T(4,128)S(1)} %bitcast.35, bf16[1024,128]{1,0:T(8,128)(2,1)S(1)} %collective-permute-done.src1, ...), custom_call_target="tpu_custom_call" | custom-call | flops 2000000000 | tf_op jit(solution)/shard_map/pallas_call | solution.py:424
  14.1 3.1 %collective-permute-done.1.src2 = bf16[1024,128]{1,0:T(8,128)(2,1)S(1)} collective-permute-done((bf16[1024,128]{1,0:T(8,128)(2,1)}, bf16[1024,128]{1,0:T(8,128)(2,1)S(1)}, u32[]{:S(2)}, u32[]{:S(2)}) %collective-permute-start.1) | collective-permute-done | bytes 262176 | tf_op jit(solution)/shard_map/ppermute | solution.py:25
  17.2 2.7 %collective-permute-done.2.src3 = bf16[1024,128]{1,0:T(8,128)(2,1)S(1)} collective-permute-done((bf16[1024,128]{1,0:T(8,128)(2,1)}, bf16[1024,128]{1,0:T(8,128)(2,1)S(1)}, u32[]{:S(2)}, u32[]{:S(2)}) %collective-permute-start.2) | collective-permute-done | bytes 262176 | tf_op jit(solution)/shard_map/ppermute | solution.py:25
  20.0 7.5 %shard_map.156 = (bf16[1024,128]{1,0:T(8,128)(2,1)S(1)}, bf16[1024,128]{1,0:T(8,128)(2,1)S(1)}, bf16[2304,128]{1,0:T(8,128)(2,1)S(1)}, f32[512,256]{1,0:T(8,128)...) custom-call(s32[4]{0:T(128)S(1)} %bitcast.18, s32[4,1024]{1,0:T(4,128)S(1)} %bitcast.32, ...), custom_call_target="tpu_custom_call" | custom-call | flops 8000000000 | tf_op jit(solution)/shard_map/pallas_call | solution.py:424
  27.5 5.5 %collective-permute-start.3 = (bf16[1024,128]{1,0:T(8,128)(2,1)S(1)}, bf16[1024,128]{1,0:T(8,128)(2,1)S(1)}, u32[]{:S(2)}, u32[]{:S(2)}) collective-permute-start(bf16[1024,128]{1,0:T(8,128)(2,1)S(1)} %get-tuple-element.46), channel_id=1, source_target_pairs={{0,6},{1,3},{2,0},{3,5},{4,2},{5,7},{6,4},{7,1},{8,14},{9,11},{10,... | collective-permute-start | bytes 786440 | tf_op jit(solution)/shard_map/ppermute | solution.py:536
  33.0 4.0 %shard_map.157 = (bf16[1024,128]{1,0:T(8,128)(2,1)S(1)}, bf16[2304,128]{1,0:T(8,128)(2,1)S(1)}, f32[512,256]{1,0:T(8,128)S(1)}, f32[512,256]{1,0:T(8,128)S(1)}, ...) custom-call(s32[4]{0:T(128)S(1)} %bitcast.19, s32[4,1024]{1,0:T(4,128)S(1)} %bitcast.33, s32[4,1024]{1,0:T(4,128)S(1)} %bitcast.37, ...), custom_call_target="tpu_custom_call" | custom-call | flops 8000000000 | tf_op jit(solution)/shard_map/pallas_call | solution.py:424
  37.1 1.3 %collective-permute-done.4 = bf16[448,128]{1,0:T(8,128)(2,1)S(1)} collective-permute-done((bf16[448,128]{1,0:T(8,128)(2,1)S(1)}, bf16[448,128]{1,0:T(8,128)(2,1)S(1)}, u32[]{:S(2)}, u32[]{:S(2)}) %collective-permute-start.4) | collective-permute-done | bytes 114720 | tf_op jit(solution)/shard_map/ppermute | solution.py:559
  38.4 4.1 %collective-permute-start.7 = (bf16[448,128]{1,0:T(8,128)(2,1)S(1)}, bf16[448,128]{1,0:T(8,128)(2,1)S(1)}, u32[]{:S(2)}, u32[]{:S(2)}) collective-permute-start(bf16[448,128]{1,0:T(8,128)(2,1)S(1)} %add_convert_fusion.2), channel_id=1, source_target_pairs={{0,6},{1,7},{2,4},{3,5},{4,2},{5,3},{6,0},{7,1},{8,14},{9,15},{10,... | collective-permute-start | bytes 344072 | tf_op jit(solution)/shard_map/ppermute | solution.py:439
  42.6 0.6 %collective-permute-start.5 = (bf16[448,128]{1,0:T(8,128)(2,1)S(1)}, bf16[448,128]{1,0:T(8,128)(2,1)S(1)}, u32[]{:S(2)}, u32[]{:S(2)}) collective-permute-start(bf16[448,128]{1,0:T(8,128)(2,1)S(1)} %add_convert_fusion.2), channel_id=1, source_target_pairs={{0,2},{1,3},{2,0},{3,1},{4,6},{5,7},{6,4},{7,5},{8,10},{9,11},{10,... | collective-permute-start | bytes 344072 | tf_op jit(solution)/shard_map/ppermute | solution.py:439
  43.3 2.3 %collective-permute-start.8 = (bf16[1024,128]{1,0:T(8,128)(2,1)S(1)}, bf16[1024,128]{1,0:T(8,128)(2,1)S(1)}, u32[]{:S(2)}, u32[]{:S(2)}) collective-permute-start(bf16[1024,128]{1,0:T(8,128)(2,1)S(1)} %add_convert_fusion), channel_id=1, source_target_pairs={{0,1},{1,0},{2,3},{3,2},{4,5},{5,4},{6,7},{7,6},{8,9},{9,8},{10,11... | collective-permute-start | bytes 786440 | tf_op jit(solution)/shard_map/ppermute | solution.py:554
  45.6 2.2 %shard_map.158 = (bf16[4,1024,128]{2,1,0:T(8,128)(2,1)}, f32[1024,128]{1,0:T(8,128)S(1)}) custom-call(s32[4]{0:T(128)S(1)} %bitcast.20, bf16[1024,128]{1,0:T(8,128)(2,1)S(1)} %bitcast.15, bf16[4096,128]{1,0:T(8,128)(2,1)S(1)} %bitcast.13, bf16[384,128]{1,0:T(8,128)(2,1)S(1)} %copy-done.2, bf16[256,128]{1,0:T(8,128)(2,1)S(1)} %copy-done.3, ...), custom_call_target="tpu_custom_call" | custom-call | flops 1000000 | tf_op jit(solution)/shard_map/pallas_call | solution.py:424
  47.8 1.3 %collective-permute-start.12 = (bf16[1024,128]{1,0:T(8,128)(2,1)S(1)}, bf16[1024,128]{1,0:T(8,128)(2,1)S(1)}, u32[]{:S(2)}, u32[]{:S(2)}) collective-permute-start(bf16[1024,128]{1,0:T(8,128)(2,1)S(1)} %get-tuple-element.59), channel_id=1, source_target_pairs={{8,0},{16,8},{24,16},{9,1},{17,9},{25,17},{10,2},{18,10},{26,18},{... | collective-permute-start | bytes 786440 | tf_op jit(solution)/shard_map/ppermute | solution.py:25
  49.1 3.4 %collective-permute-done.6 = bf16[448,128]{1,0:T(8,128)(2,1)S(1)} collective-permute-done((bf16[448,128]{1,0:T(8,128)(2,1)S(1)}, bf16[448,128]{1,0:T(8,128)(2,1)S(1)}, u32[]{:S(2)}, u32[]{:S(2)}) %collective-permute-start.6) | collective-permute-done | bytes 114720 | tf_op jit(solution)/shard_map/ppermute | solution.py:439
  52.7 2.1 %collective-permute-start.10 = (bf16[448,128]{1,0:T(8,128)(2,1)S(1)}, bf16[448,128]{1,0:T(8,128)(2,1)S(1)}, u32[]{:S(2)}, u32[]{:S(2)}) collective-permute-start(bf16[448,128]{1,0:T(8,128)(2,1)S(1)} %convert_add_fusion.1), channel_id=1, source_target_pairs={{0,16},{1,17},{2,18},{3,19},{4,20},{5,21},{6,22},{7,23},{8,24},{9,... | collective-permute-start | bytes 344072 | tf_op jit(solution)/shard_map/ppermute | solution.py:439
  54.8 1.3 %collective-permute-start.9 = (bf16[448,128]{1,0:T(8,128)(2,1)S(1)}, bf16[448,128]{1,0:T(8,128)(2,1)S(1)}, u32[]{:S(2)}, u32[]{:S(2)}) collective-permute-start(bf16[448,128]{1,0:T(8,128)(2,1)S(1)} %convert_add_fusion.1), channel_id=1, source_target_pairs={{0,1},{1,0},{2,3},{3,2},{4,5},{5,4},{6,7},{7,6},{8,9},{9,8},{10,11... | collective-permute-start | bytes 344072 | tf_op jit(solution)/shard_map/ppermute | solution.py:439
  56.2 0.9 %convert_add_fusion = f32[1024,128]{1,0:T(8,128)} fusion(bf16[1024,128]{1,0:T(8,128)(2,1)S(1)} %collective-permute-done.8, f32[1024,128]{1,0:T(8,128)S(1)} %get-tuple-element.58, bf16[1024,128]{1,0:T(8,128)(2,1)S(1)} %collective-permute-done.12), kind=kLoop, calls=%fused_computation | loop fusion | flops 524288 | bytes 1572864 | tf_op jit(solution)/shard_map/add | solution.py:571
  57.0 2.5 %collective-permute-done.11 = bf16[448,128]{1,0:T(8,128)(2,1)S(1)} collective-permute-done((bf16[448,128]{1,0:T(8,128)(2,1)S(1)}, bf16[448,128]{1,0:T(8,128)(2,1)S(1)}, u32[]{:S(2)}, u32[]{:S(2)}) %collective-permute-start.11) | collective-permute-done | bytes 114720 | tf_op jit(solution)/shard_map/ppermute | solution.py:439
  59.5 0.8 %collective-permute-done.10 = bf16[448,128]{1,0:T(8,128)(2,1)S(1)} collective-permute-done((bf16[448,128]{1,0:T(8,128)(2,1)S(1)}, bf16[448,128]{1,0:T(8,128)(2,1)S(1)}, u32[]{:S(2)}, u32[]{:S(2)}) %collective-permute-start.10) | collective-permute-done | bytes 114720 | tf_op jit(solution)/shard_map/ppermute | solution.py:439
  60.5 1.3 %collective-permute-done.13.theirs = bf16[448,128]{1,0:T(8,128)(2,1)S(1)} collective-permute-done((bf16[448,128]{1,0:T(8,128)(2,1)S(1)}, bf16[448,128]{1,0:T(8,128)(2,1)S(1)}, u32[]{:S(2)}, u32[]{:S(2)}) %collective-permute-start.13) | collective-permute-done | bytes 114720 | tf_op jit(solution)/shard_map/ppermute | solution.py:439
  61.8 0.8 %shard_map.159 = (f32[384,128]{1,0:T(8,128)}, f32[128,128]{1,0:T(8,128)}, f32[256,128]{1,0:T(8,128)}, f32[128,128]{1,0:T(8,128)}) custom-call(s32[1]{0:T(128)} %bitcast.8.me, bf16[448,128]{1,0:T(8,128)(2,1)S(1)} %add_convert_fusion.1.mine, bf16[448,128]{1,0:T(8,128)(2,1)S(1)} %collective-permute-done.13.theirs), custom_call_target="tpu_custom_call" | custom-call | flops 1000000 | tf_op jit(solution)/shard_map/pallas_call | solution.py:424
  (37 shorter events, 0.6 us)
Async XLA Ops:
  0.6 11.6 %collective-permute-start = (bf16[1024,128]{1,0:T(8,128)(2,1)}, bf16[1024,128]{1,0:T(8,128)(2,1)S(1)}, u32[]{:S(2)}, u32[]{:S(2)}) collective-permute-start(bf16[1024,128]{1,0:T(8,128)(2,1)} %bitcast.24), channel_id=1, source_target_pairs={{0,8},{8,16},{16,24},{1,9},{9,17},{17,25},{2,10},{10,18},{18,26},{... | collective-permute-start | bytes 786440 | tf_op jit(solution)/shard_map/ppermute | solution.py:25
  3.0 14.2 %collective-permute-start.1 = (bf16[1024,128]{1,0:T(8,128)(2,1)}, bf16[1024,128]{1,0:T(8,128)(2,1)S(1)}, u32[]{:S(2)}, u32[]{:S(2)}) collective-permute-start(bf16[1024,128]{1,0:T(8,128)(2,1)} %bitcast.25), channel_id=1, source_target_pairs={{0,1},{1,2},{2,3},{3,4},{4,5},{5,6},{6,7},{7,0},{8,9},{9,10},{10,1... | collective-permute-start | bytes 786440 | tf_op jit(solution)/shard_map/ppermute | solution.py:25
  5.4 14.5 %collective-permute-start.2 = (bf16[1024,128]{1,0:T(8,128)(2,1)}, bf16[1024,128]{1,0:T(8,128)(2,1)S(1)}, u32[]{:S(2)}, u32[]{:S(2)}) collective-permute-start(bf16[1024,128]{1,0:T(8,128)(2,1)} %bitcast.26), channel_id=1, source_target_pairs={{0,7},{1,0},{2,1},{3,2},{4,3},{5,4},{6,5},{7,6},{8,15},{9,8},{10,9... | collective-permute-start | bytes 786440 | tf_op jit(solution)/shard_map/ppermute | solution.py:25
  8.5 3.7 %copy-start.4 = (s32[1,1,4]{2,1,0:T(1,128)S(1)}, s32[1,1,4]{2,1,0:T(1,128)}, u32[]{:S(2)}) copy-start(s32[1,1,4]{2,1,0:T(1,128)} %param.15) | copy-start | bytes 52
  8.5 3.7 %copy-start.9 = (s32[1,1,4,1024]{3,2,1,0:T(4,128)S(1)}, s32[1,1,4,1024]{3,2,1,0:T(4,128)}, u32[]{:S(2)}) copy-start(s32[1,1,4,1024]{3,2,1,0:T(4,128)} %param.13) | copy-start | bytes 49156
  8.5 3.7 %copy-start.10 = (s32[1,1,4,1024]{3,2,1,0:T(4,128)S(1)}, s32[1,1,4,1024]{3,2,1,0:T(4,128)}, u32[]{:S(2)}) copy-start(s32[1,1,4,1024]{3,2,1,0:T(4,128)} %param.14) | copy-start | bytes 49156
  12.1 7.8 %copy-start = (bf16[1,1,4,1024,128]{4,3,2,1,0:T(8,128)(2,1)S(1)}, bf16[1,1,4,1024,128]{4,3,2,1,0:T(8,128)(2,1)}, u32[]{:S(2)}) copy-start(bf16[1,1,4,1024,128]{4,3,2,1,0:T(8,128)(2,1)} %param.17) | copy-start | bytes 3145732
  12.1 7.8 %copy-start.1 = (bf16[1,1,1024,128]{3,2,1,0:T(8,128)(2,1)S(1)}, bf16[1,1,1024,128]{3,2,1,0:T(8,128)(2,1)}, u32[]{:S(2)}) copy-start(bf16[1,1,1024,128]{3,2,1,0:T(8,128)(2,1)} %param.16) | copy-start | bytes 786436
  12.1 7.8 %copy-start.3 = (bf16[256,128]{1,0:T(8,128)(2,1)S(1)}, bf16[256,128]{1,0:T(8,128)(2,1)}, u32[]{:S(2)}) copy-start(bf16[256,128]{1,0:T(8,128)(2,1)} %wn_in.3) | copy-start | bytes 196612
  12.1 7.8 %copy-start.5 = (bf16[1,1,4,1024,128]{4,3,2,1,0:T(8,128)(2,1)S(1)}, bf16[1,1,4,1024,128]{4,3,2,1,0:T(8,128)(2,1)}, u32[]{:S(2)}) copy-start(bf16[1,1,4,1024,128]{4,3,2,1,0:T(8,128)(2,1)} %param.12) | copy-start | bytes 3145732
  12.2 7.8 %copy-start.6 = (bf16[1,1,1024,128]{3,2,1,0:T(8,128)(2,1)S(1)}, bf16[1,1,1024,128]{3,2,1,0:T(8,128)(2,1)}, u32[]{:S(2)}) copy-start(bf16[1,1,1024,128]{3,2,1,0:T(8,128)(2,1)} %param.11) | copy-start | bytes 786436
  12.2 7.8 %copy-start.7 = (bf16[128,128]{1,0:T(8,128)(2,1)S(1)}, bf16[128,128]{1,0:T(8,128)(2,1)}, u32[]{:S(2)}) copy-start(bf16[128,128]{1,0:T(8,128)(2,1)} %wn_out.1) | copy-start | bytes 98308
  12.2 7.8 %copy-start.8 = (bf16[128,128]{1,0:T(8,128)(2,1)S(1)}, bf16[128,128]{1,0:T(8,128)(2,1)}, u32[]{:S(2)}) copy-start(bf16[128,128]{1,0:T(8,128)(2,1)} %w_out.3) | copy-start | bytes 98308
  27.5 9.5 %collective-permute-start.3 = (bf16[1024,128]{1,0:T(8,128)(2,1)S(1)}, bf16[1024,128]{1,0:T(8,128)(2,1)S(1)}, u32[]{:S(2)}, u32[]{:S(2)}) collective-permute-start(bf16[1024,128]{1,0:T(8,128)(2,1)S(1)} %get-tuple-element.46), channel_id=1, source_target_pairs={{0,6},{1,3},{2,0},{3,5},{4,2},{5,7},{6,4},{7,1},{8,14},{9,11},{10,... | collective-permute-start | bytes 786440 | tf_op jit(solution)/shard_map/ppermute | solution.py:536
  37.0 1.4 %collective-permute-start.4 = (bf16[448,128]{1,0:T(8,128)(2,1)S(1)}, bf16[448,128]{1,0:T(8,128)(2,1)S(1)}, u32[]{:S(2)}, u32[]{:S(2)}) collective-permute-start(bf16[448,128]{1,0:T(8,128)(2,1)S(1)} %get-tuple-element.47), channel_id=1, source_target_pairs={{0,8},{8,0},{16,24},{24,16},{1,9},{9,1},{17,25},{25,17},{2,10},{10... | collective-permute-start | bytes 344072 | tf_op jit(solution)/shard_map/ppermute | solution.py:559
  38.4 10.7 %collective-permute-start.7 = (bf16[448,128]{1,0:T(8,128)(2,1)S(1)}, bf16[448,128]{1,0:T(8,128)(2,1)S(1)}, u32[]{:S(2)}, u32[]{:S(2)}) collective-permute-start(bf16[448,128]{1,0:T(8,128)(2,1)S(1)} %add_convert_fusion.2), channel_id=1, source_target_pairs={{0,6},{1,7},{2,4},{3,5},{4,2},{5,3},{6,0},{7,1},{8,14},{9,15},{10,... | collective-permute-start | bytes 344072 | tf_op jit(solution)/shard_map/ppermute | solution.py:439
  42.5 10.0 %collective-permute-start.6 = (bf16[448,128]{1,0:T(8,128)(2,1)S(1)}, bf16[448,128]{1,0:T(8,128)(2,1)S(1)}, u32[]{:S(2)}, u32[]{:S(2)}) collective-permute-start(bf16[448,128]{1,0:T(8,128)(2,1)S(1)} %add_convert_fusion.2), channel_id=1, source_target_pairs={{0,4},{1,5},{2,6},{3,7},{4,0},{5,1},{6,2},{7,3},{8,12},{9,13},{10,... | collective-permute-start | bytes 344072 | tf_op jit(solution)/shard_map/ppermute | solution.py:439
  42.6 10.0 %collective-permute-start.5 = (bf16[448,128]{1,0:T(8,128)(2,1)S(1)}, bf16[448,128]{1,0:T(8,128)(2,1)S(1)}, u32[]{:S(2)}, u32[]{:S(2)}) collective-permute-start(bf16[448,128]{1,0:T(8,128)(2,1)S(1)} %add_convert_fusion.2), channel_id=1, source_target_pairs={{0,2},{1,3},{2,0},{3,1},{4,6},{5,7},{6,4},{7,5},{8,10},{9,11},{10,... | collective-permute-start | bytes 344072 | tf_op jit(solution)/shard_map/ppermute | solution.py:439
  43.3 9.3 %collective-permute-start.8 = (bf16[1024,128]{1,0:T(8,128)(2,1)S(1)}, bf16[1024,128]{1,0:T(8,128)(2,1)S(1)}, u32[]{:S(2)}, u32[]{:S(2)}) collective-permute-start(bf16[1024,128]{1,0:T(8,128)(2,1)S(1)} %add_convert_fusion), channel_id=1, source_target_pairs={{0,1},{1,0},{2,3},{3,2},{4,5},{5,4},{6,7},{7,6},{8,9},{9,8},{10,11... | collective-permute-start | bytes 786440 | tf_op jit(solution)/shard_map/ppermute | solution.py:554
  47.8 8.4 %collective-permute-start.12 = (bf16[1024,128]{1,0:T(8,128)(2,1)S(1)}, bf16[1024,128]{1,0:T(8,128)(2,1)S(1)}, u32[]{:S(2)}, u32[]{:S(2)}) collective-permute-start(bf16[1024,128]{1,0:T(8,128)(2,1)S(1)} %get-tuple-element.59), channel_id=1, source_target_pairs={{8,0},{16,8},{24,16},{9,1},{17,9},{25,17},{10,2},{18,10},{26,18},{... | collective-permute-start | bytes 786440 | tf_op jit(solution)/shard_map/ppermute | solution.py:25
  52.6 6.9 %collective-permute-start.11 = (bf16[448,128]{1,0:T(8,128)(2,1)S(1)}, bf16[448,128]{1,0:T(8,128)(2,1)S(1)}, u32[]{:S(2)}, u32[]{:S(2)}) collective-permute-start(bf16[448,128]{1,0:T(8,128)(2,1)S(1)} %convert_add_fusion.1), channel_id=1, source_target_pairs={{0,17},{1,16},{2,19},{3,18},{4,21},{5,20},{6,23},{7,22},{8,25},{9,... | collective-permute-start | bytes 344072 | tf_op jit(solution)/shard_map/ppermute | solution.py:439
  52.7 7.6 %collective-permute-start.10 = (bf16[448,128]{1,0:T(8,128)(2,1)S(1)}, bf16[448,128]{1,0:T(8,128)(2,1)S(1)}, u32[]{:S(2)}, u32[]{:S(2)}) collective-permute-start(bf16[448,128]{1,0:T(8,128)(2,1)S(1)} %convert_add_fusion.1), channel_id=1, source_target_pairs={{0,16},{1,17},{2,18},{3,19},{4,20},{5,21},{6,22},{7,23},{8,24},{9,... | collective-permute-start | bytes 344072 | tf_op jit(solution)/shard_map/ppermute | solution.py:439
  54.8 5.5 %collective-permute-start.9 = (bf16[448,128]{1,0:T(8,128)(2,1)S(1)}, bf16[448,128]{1,0:T(8,128)(2,1)S(1)}, u32[]{:S(2)}, u32[]{:S(2)}) collective-permute-start(bf16[448,128]{1,0:T(8,128)(2,1)S(1)} %convert_add_fusion.1), channel_id=1, source_target_pairs={{0,1},{1,0},{2,3},{3,2},{4,5},{5,4},{6,7},{7,6},{8,9},{9,8},{10,11... | collective-permute-start | bytes 344072 | tf_op jit(solution)/shard_map/ppermute | solution.py:439
  60.4 1.4 %collective-permute-start.13 = (bf16[448,128]{1,0:T(8,128)(2,1)S(1)}, bf16[448,128]{1,0:T(8,128)(2,1)S(1)}, u32[]{:S(2)}, u32[]{:S(2)}) collective-permute-start(bf16[448,128]{1,0:T(8,128)(2,1)S(1)} %add_convert_fusion.1.mine), channel_id=1, source_target_pairs={{0,8},{1,9},{2,10},{3,11},{4,12},{5,13},{6,14},{7,15},{8,0},{9,1},... | collective-permute-start | bytes 344072 | tf_op jit(solution)/shard_map/ppermute | solution.py:439
  (1 other events, 3.7 us)

commit v4 on v3

--- a/solution.py
+++ b/solution.py
@@ -308,8 +308,8 @@
 def node_kernel(
     counts, send, recv, hit, src2, src3, edges, grad_hit, grad_edge,
     w_in, w_out, wn_in, wn_out, part, total_in, odd,
-    far_back, near_back, edge_back, recv_sum, node_back, inc_grad, partial,
-    source, send_sum, u_all, rs_all, hidden_all, total, held, held_back,
+    far_back, edge_back, recv_sum, node_back, inc_grad, partial, u_all, rs_all, hidden_all,
+    source, send_sum, total, held, held_back,
 ):
     nodes, d = hit.shape
     cap = send.shape[1]
@@ -336,19 +336,19 @@
     recv_sum[...] = jnp.zeros_like(recv_sum)
     send_sum[...] = jnp.zeros_like(send_sum)
     backward(
-        Tiles(counts, (2, 3), cap, 2, 2), send, recv, edges, grad_edge, w_out, inc_grad,
+        Tiles(counts, (2 + odd[0],), cap, 2, 2), send, recv, edges, grad_edge, w_out, inc_grad,
         u_all, rs_all, hidden_all, held_back, edge_back, recv_sum, send_sum,
         partial.at[2 * d : 3 * d], partial.at[3 * d : 4 * d],
     )
-    partial[:d, :] = turned_product(send_sum[0], src2[...]) + turned_product(send_sum[1], src3[...])
-    far_back[...] = senders_back(send_sum[odd[0]], w_in)
-    near_back[...] = senders_back(send_sum[1 - odd[0]], w_in)
+    far = jnp.where(odd[0] == 1, src3[...].astype(f32), src2[...].astype(f32)).astype(bf16)
+    partial[:d, :] = turned_product(send_sum[0], far)
+    far_back[...] = senders_back(send_sum[0], w_in)
 
 
 def last_kernel(
-    counts, send, recv, hit, src1, edges, grad_edge, w_in, w_out,
-    u0, rs0, hidden0, recv_in, inc_grad, partial, me,
-    back1, edge_back, recv_sum, send0, mine, other,
+    counts, send, recv, hit, src1, src2, src3, edges, grad_edge, w_in, w_out,
+    u0, rs0, hidden0, u2, rs2, hidden2, recv_in, inc_grad, partial, me, odd,
+    back1, near_back, edge_back, near_edge, recv_sum, send0, mine, other,
     send_sum, weights, held,
 ):
     cap, d = send.shape[1], hit.shape[1]
@@ -360,7 +360,15 @@
         u0, rs0, hidden0, held, edge_back, recv_sum, send_sum,
         weights.at[2 * d : 3 * d], weights.at[3 * d : 4 * d],
     )
+    backward(
+        Tiles(counts, (3 - odd[0],), cap, 2, 2), send, recv, edges, grad_edge, w_out, inc_grad,
+        u2, rs2, hidden2, held, near_edge, recv_sum, send_sum.at[2:],
+        weights.at[2 * d : 3 * d], weights.at[3 * d : 4 * d],
+    )
+    near = jnp.where(odd[0] == 1, src2[...].astype(f32), src3[...].astype(f32)).astype(bf16)
+    near_back[...] = senders_back(send_sum[2], w_in)
     turned = turned_product(send_sum[0], hit[...]) + turned_product(send_sum[1], src1[...])
+    turned += turned_product(send_sum[2], near)
     weights[:d, :] = (weights[:d, :] + turned).T
     weights[d : 2 * d, :] = turned_product(recv_sum[...], hit[...]).T
     weights[2 * d : 3 * d, :] = weights[2 * d : 3 * d, :].T
@@ -372,17 +380,22 @@
 
 
 def edge_kernel(
-    counts, grad_hit, grad_edge, w_in, wn_in, first_back, second_back, recv_sum, send0, node_back,
+    counts, grad_hit, grad_edge, w_in, wn_in, first_back, far_edge, near_edge, recv_sum, send0, node_back, odd,
     edge_done, hit_done,
 ):
     d = w_in.shape[1]
-    kinds, cap = edge_done.shape[:2]
-    for k in range(kinds):
-        back = (first_back, second_back)[k // 2][k % 2 * cap : (k % 2 + 1) * cap, :]
-        through = dot_nt(back, w_in[2 * d :, :])
-        live = lax.broadcasted_iota(jnp.int32, through.shape, 0) < counts[k]
-        grad_rows = grad_edge[k * cap : (k + 1) * cap, :].astype(f32)
-        edge_done[k] = (grad_rows + jnp.where(live, through, 0.0)).astype(bf16)
+    cap = edge_done.shape[1]
+
+    def put(kind, back, row):
+        through = dot_nt(back[pl.ds(row * cap, cap), :], w_in[2 * d :, :])
+        live = lax.broadcasted_iota(jnp.int32, through.shape, 0) < counts[kind]
+        grad_rows = grad_edge[pl.ds(kind * cap, cap), :].astype(f32)
+        edge_done[kind] = (grad_rows + jnp.where(live, through, 0.0)).astype(bf16)
+
+    put(0, first_back, 0)
+    put(1, first_back, 1)
+    put(2 + odd[0], far_edge, odd[0])
+    put(3 - odd[0], near_edge, 1 - odd[0])
     ends = jnp.concatenate([w_in[d : 2 * d, :]] * 2 + [w_in[:d, :]] * 2, axis=1)
     sums = jnp.concatenate([both_halves(unfolded_sums(s[...]), 0) for s in (recv_sum, send0)], axis=0)
     hit_done[...] = (
@@ -470,7 +483,7 @@
     odd = (lax.axis_index("phi") % 2).astype(jnp.int32).reshape(1)
     src2 = shifted(hit, "phi", 1, True)
     src3 = shifted(hit, "phi", -1, True)
-    src1 = shifted(hit, "layer", 1, False)
+    src1 = shifted(lax.optimization_barrier(hit), "layer", 1, False)
 
     def shape(*dims, dtype=f32):
         return jax.ShapeDtypeStruct(dims, dtype)
@@ -511,21 +524,19 @@
         ],
     )
     partial = shape(7 * d, d)
-    far_back, near_back, second_back, recv_sum, node_back, inc_grad, partial = on_device(
+    far_back, far_edge, recv_sum, node_back, inc_grad, partial, u2, rs2, hidden2 = on_device(
         node_kernel,
         [
-            node_half, node_half, shape(2 * cap + SPAN, d, dtype=bf16),
+            node_half, shape(2 * cap + SPAN, d, dtype=bf16),
             turned, node_half, shape(nodes // FOLD, FOLD * d, dtype=bf16), partial,
+            rows(2), rows(2), tiles(2),
         ],
         (counts, send, recv, hit, src2, src3, edges, grad_hit, grad_edge,
          w_edge_in, w_edge_out, w_node_in, w_node_out, part, total, odd),
         8 * 10**9,
         scratch=[
             pltpu.VMEM((2, nodes // FOLD, FOLD * d), bf16),
-            pltpu.VMEM((2, *turned.shape), f32),
-            pltpu.VMEM((2 * cap + SPAN, d), f32),
-            pltpu.VMEM((2 * cap + SPAN, d), f32),
-            pltpu.VMEM((2 * cap // SPAN + 1, d, SPAN), bf16),
+            pltpu.VMEM((1, *turned.shape), f32),
             pltpu.VMEM(turned.shape, f32),
             pltpu.VMEM((d, FORWARD * SPAN), f32),
             pltpu.VMEM((d, BACKWARD * SPAN), f32),
@@ -534,38 +545,37 @@
     )
     route = [(i, (i + (2 if i % 2 else -2)) % sectors) for i in range(sectors)]
     relayed = lax.ppermute(far_back, "phi", route)
-    back1, first_back, recv_sum, send0, mine, other = on_device(
+    back1, near_back, first_back, near_edge, recv_sum, send0, mine, other = on_device(
         last_kernel,
         [
-            node_half, shape(2 * cap + SPAN, d, dtype=bf16), turned, turned,
+            node_half, node_half, shape(2 * cap + SPAN, d, dtype=bf16),
+            shape(2 * cap + SPAN, d, dtype=bf16), turned, turned,
             shape(7 * d // 2, d), shape(7 * d // 2, d, dtype=bf16),
         ],
-        (counts, send, recv, hit, src1, edges, grad_edge, w_edge_in, w_edge_out,
-         u0, rs0, hidden0, recv_sum, inc_grad, partial, me),
+        (counts, send, recv, hit, src1, src2, src3, edges, grad_edge, w_edge_in, w_edge_out,
+         u0, rs0, hidden0, u2, rs2, hidden2, recv_sum, inc_grad, partial, me, odd),
         8 * 10**9,
         scratch=[
-            pltpu.VMEM((2, *turned.shape), f32),
+            pltpu.VMEM((3, *turned.shape), f32),
             pltpu.VMEM((7 * d, d), f32),
             pltpu.VMEM((d, BACKWARD * SPAN), f32),
         ],
-        scalars=(0, 15),
+        scalars=(0, 20, 21),
     )
     other, relayed = lax.optimization_barrier((other, relayed))
-    from_beside = lax.ppermute(
-        (near_back.astype(f32) + relayed.astype(f32)).astype(bf16),
-        "phi",
-        [(i, i ^ 1) for i in range(sectors)],
-    )
+    near_back = (near_back.astype(f32) + relayed.astype(f32)).astype(bf16)
+    near_back, back1 = lax.optimization_barrier((near_back, back1))
+    from_beside = lax.ppermute(near_back, "phi", [(i, i ^ 1) for i in range(sectors)])
+    from_upper = shifted(back1, "layer", -1, False)
     mine = mine + lax.ppermute(other, "layer", [(i, i ^ 1) for i in range(layers)]).astype(f32)
     edge_done, hit_done = on_device(
         edge_kernel,
         [shape(kinds, cap, d, dtype=bf16), shape(nodes, d)],
         (counts, grad_hit, grad_edge, w_edge_in, w_node_in,
-         first_back, second_back, recv_sum, send0, node_back),
+         first_back, far_edge, near_edge, recv_sum, send0, node_back, odd),
         10**6,
-    )
-    hit_done, back1 = lax.optimization_barrier((hit_done, back1))
-    from_upper = shifted(back1, "layer", -1, False)
+        scalars=(0, 11),
+    )
 
     def hits(from_beside):
         return hit_done + from_upper.astype(f32) + from_beside.astype(f32)

time: 63 us -> 60.4 us (0.959)
  waiting for transfers between devices: 15.2 us -> 14.1 us
  Pallas kernels: 19.9 us -> 19.2 us
    ppermute x1, starting transfers between devices: 0.07 us -> 3.23 us  [body(): lax.ppermute(other, 'layer', [(i, i ^ 1) for i in range(layers)])]
    ppermute x4, waiting for transfers between devices: 5.79 us -> 3.49 us  [shifted(): return lax.ppermute(value, axis, route)]
    ppermute x1, starting transfers between devices: 5.49 us -> 3.27 us  [body(): relayed = lax.ppermute(far_back, 'phi', route)]
    ppermute x1, starting transfers between devices: 2.35 us -> 1.12 us  [body(): lax.ppermute(near_back, 'phi', [(i, i ^ 1) for i in range(sectors)])]
    ppermute x7, waiting for transfers between devices: 8.05 us -> 9.19 us  [swap(): return lax.ppermute(value, axes, [(i, i ^ mask) for i in range(total)])]
    pallas_call x6, Pallas kernels: 19.9 us -> 19.2 us  [on_device(): pl.pallas_call(kernel, out_shape=outs, in_specs=in_specs, out_specs=[vmem...]
  transfers between devices with their start and end apart: 14 -> 14, of which waited for: 7 -> 8; matrix products, arithmetic and copies ran while one was open for 2% -> 2% of each run, Pallas kernels for 19% -> 22%
where the time goes in v4:
time: 60.4 us; the launch traced here: 60.6 us
  starting transfers between devices  25.1 us (42%)
  Pallas kernels  19.2 us (32%)
  waiting for transfers between devices  14.1 us (23%)
  other arithmetic  1.12 us (2%)
  between operations  0.9 us (1%)
    pallas_call x6, Pallas kernels, on_device(): pl.pallas_call(kernel, out_shape=outs, in_specs=in_specs, out_specs=[vmem...  19.2 us
    ppermute x7, waiting for transfers between devices, swap(): return lax.ppermute(value, axes, [(i, i ^ mask) for i in range(total)])  9.19 us
    ppermute x4, starting transfers between devices, shifted(): return lax.ppermute(value, axis, route)  8.78 us
    ppermute x7, starting transfers between devices, swap(): return lax.ppermute(value, axes, [(i, i ^ mask) for i in range(total)])  8.72 us
    ppermute x4, waiting for transfers between devices, shifted(): return lax.ppermute(value, axis, route)  3.49 us
    ppermute x1, starting transfers between devices, body(): relayed = lax.ppermute(far_back, 'phi', route)  3.27 us
    ppermute x1, starting transfers between devices, body(): lax.ppermute(other, 'layer', [(i, i ^ 1) for i in range(layers)])  3.23 us
  transfers between devices with their start and end apart: 14, of which 8 were waited for; matrix products, arithmetic and copies ran while one was open for 2% of the time, Pallas kernels for 22%

profile of v4, /device:TPU:0, one launch (start us, length us, event | category | flops | bytes accessed | tf_op | source)
XLA Modules:
  0.0 60.6 jit_solution(8602559503819615432)
XLA Ops:
  0.6 6.0 %collective-permute-start.2 = (bf16[1024,128]{1,0:T(8,128)(2,1)}, bf16[1024,128]{1,0:T(8,128)(2,1)S(1)}, u32[]{:S(2)}, u32[]{:S(2)}) collective-permute-start(bf16[1024,128]{1,0:T(8,128)(2,1)} %bitcast.24), channel_id=1, source_target_pairs={{0,7},{1,0},{2,1},{3,2},{4,3},{5,4},{6,5},{7,6},{8,15},{9,8},{10,9... | collective-permute-start | bytes 786440 | tf_op jit(solution)/shard_map/ppermute | solution.py:25
  6.7 1.5 %collective-permute-start = (bf16[1024,128]{1,0:T(8,128)(2,1)}, bf16[1024,128]{1,0:T(8,128)(2,1)S(1)}, u32[]{:S(2)}, u32[]{:S(2)}) collective-permute-start(bf16[1024,128]{1,0:T(8,128)(2,1)} %bitcast.26), channel_id=1, source_target_pairs={{0,8},{8,16},{16,24},{1,9},{9,17},{17,25},{2,10},{10,18},{18,26},{... | collective-permute-start | bytes 786440 | tf_op jit(solution)/shard_map/ppermute | solution.py:25
  8.2 3.6 %shard_map.154.part = f32[4352,128]{1,0:T(8,128)S(1)} custom-call(s32[4]{0:T(128)} %bitcast.16, s32[4,1024]{1,0:T(4,128)} %bitcast.30, s32[4,1024]{1,0:T(4,128)} %bitcast.34, bf16[1024,128]{1,0:T(8,128)(2,1)} %bitcast.27, bf16[4096,128]{1,0:T(8,128)(2,1)} %bitcast.21, bf16[384,128]{1,0:T(8,128)(2,1)} %w_in.7), custom_call_target="tpu_custom_call" | custom-call | flops 4000000000 | tf_op jit(solution)/shard_map/pallas_call | solution.py:437
  11.9 1.9 %shard_map.155 = (f32[2304,128]{1,0:T(8,128)S(1)}, f32[2304,128]{1,0:T(8,128)S(1)}, bf16[9,128,256]{2,1,0:T(8,128)(2,1)S(1)}, f32[512,256]{1,0:T(8,128)S(1)}) custom-call(s32[4]{0:T(128)S(1)} %bitcast.17, s32[4,1024]{1,0:T(4,128)S(1)} %bitcast.31, s32[4,1024]{1,0:T(4,128)S(1)} %bitcast.35, bf16[1024,128]{1,0:T(8,128)(2,1)S(1)} %collective-permute-done.src1, ...), custom_call_target="tpu_custom_call" | custom-call | flops 2000000000 | tf_op jit(solution)/shard_map/pallas_call | solution.py:437
  13.9 3.5 %collective-permute-done.1.src2 = bf16[1024,128]{1,0:T(8,128)(2,1)S(1)} collective-permute-done((bf16[1024,128]{1,0:T(8,128)(2,1)}, bf16[1024,128]{1,0:T(8,128)(2,1)S(1)}, u32[]{:S(2)}, u32[]{:S(2)}) %collective-permute-start.1) | collective-permute-done | bytes 262176 | tf_op jit(solution)/shard_map/ppermute | solution.py:25
  17.4 5.2 %shard_map.156 = (bf16[1024,128]{1,0:T(8,128)(2,1)S(1)}, bf16[2304,128]{1,0:T(8,128)(2,1)S(1)}, f32[512,256]{1,0:T(8,128)S(1)}, bf16[1024,128]{1,0:T(8,128)(2,1)...) custom-call(s32[4]{0:T(128)S(1)} %bitcast.18, ...), custom_call_target="tpu_custom_call" | custom-call | flops 8000000000 | tf_op jit(solution)/shard_map/pallas_call | solution.py:437
  22.6 3.3 %collective-permute-start.3 = (bf16[1024,128]{1,0:T(8,128)(2,1)S(1)}, bf16[1024,128]{1,0:T(8,128)(2,1)S(1)}, u32[]{:S(2)}, u32[]{:S(2)}) collective-permute-start(bf16[1024,128]{1,0:T(8,128)(2,1)S(1)} %get-tuple-element.53), channel_id=1, source_target_pairs={{0,6},{1,3},{2,0},{3,5},{4,2},{5,7},{6,4},{7,1},{8,14},{9,11},{10,... | collective-permute-start | bytes 786440 | tf_op jit(solution)/shard_map/ppermute | solution.py:547
  25.9 5.6 %shard_map.157 = (bf16[1024,128]{1,0:T(8,128)(2,1)S(1)}, bf16[1024,128]{1,0:T(8,128)(2,1)S(1)}, bf16[2304,128]{1,0:T(8,128)(2,1)S(1)}, bf16[2304,128]{1,0:T(8,12...) custom-call(s32[4]{0:T(128)S(1)} %bitcast.19, ...), custom_call_target="tpu_custom_call" | custom-call | flops 8000000000 | tf_op jit(solution)/shard_map/pallas_call | solution.py:437
  31.9 3.2 %collective-permute-start.4 = (bf16[448,128]{1,0:T(8,128)(2,1)S(1)}, bf16[448,128]{1,0:T(8,128)(2,1)S(1)}, u32[]{:S(2)}, u32[]{:S(2)}) collective-permute-start(bf16[448,128]{1,0:T(8,128)(2,1)S(1)} %get-tuple-element.54), channel_id=1, source_target_pairs={{0,8},{8,0},{16,24},{24,16},{1,9},{9,1},{17,25},{25,17},{2,10},{10... | collective-permute-start | bytes 344072 | tf_op jit(solution)/shard_map/ppermute | solution.py:570
  35.1 1.0 %collective-permute-done.4 = bf16[448,128]{1,0:T(8,128)(2,1)S(1)} collective-permute-done((bf16[448,128]{1,0:T(8,128)(2,1)S(1)}, bf16[448,128]{1,0:T(8,128)(2,1)S(1)}, u32[]{:S(2)}, u32[]{:S(2)}) %collective-permute-start.4) | collective-permute-done | bytes 114720 | tf_op jit(solution)/shard_map/ppermute | solution.py:570
  36.1 1.6 %collective-permute-start.7 = (bf16[448,128]{1,0:T(8,128)(2,1)S(1)}, bf16[448,128]{1,0:T(8,128)(2,1)S(1)}, u32[]{:S(2)}, u32[]{:S(2)}) collective-permute-start(bf16[448,128]{1,0:T(8,128)(2,1)S(1)} %add_convert_fusion.2), channel_id=1, source_target_pairs={{0,6},{1,7},{2,4},{3,5},{4,2},{5,3},{6,0},{7,1},{8,14},{9,15},{10,... | collective-permute-start | bytes 344072 | tf_op jit(solution)/shard_map/ppermute | solution.py:452
  37.8 2.8 %collective-permute-start.5 = (bf16[448,128]{1,0:T(8,128)(2,1)S(1)}, bf16[448,128]{1,0:T(8,128)(2,1)S(1)}, u32[]{:S(2)}, u32[]{:S(2)}) collective-permute-start(bf16[448,128]{1,0:T(8,128)(2,1)S(1)} %add_convert_fusion.2), channel_id=1, source_target_pairs={{0,2},{1,3},{2,0},{3,1},{4,6},{5,7},{6,4},{7,5},{8,10},{9,11},{10,... | collective-permute-start | bytes 344072 | tf_op jit(solution)/shard_map/ppermute | solution.py:452
  40.6 1.1 %collective-permute-start.8 = (bf16[1024,128]{1,0:T(8,128)(2,1)S(1)}, bf16[1024,128]{1,0:T(8,128)(2,1)S(1)}, u32[]{:S(2)}, u32[]{:S(2)}) collective-permute-start(bf16[1024,128]{1,0:T(8,128)(2,1)S(1)} %add_convert_fusion), channel_id=1, source_target_pairs={{0,1},{1,0},{2,3},{3,2},{4,5},{5,4},{6,7},{7,6},{8,9},{9,8},{10,11... | collective-permute-start | bytes 786440 | tf_op jit(solution)/shard_map/ppermute | solution.py:568
  41.8 1.3 %collective-permute-start.12 = (bf16[1024,128]{1,0:T(8,128)(2,1)S(1)}, bf16[1024,128]{1,0:T(8,128)(2,1)S(1)}, u32[]{:S(2)}, u32[]{:S(2)}) collective-permute-start(bf16[1024,128]{1,0:T(8,128)(2,1)S(1)} %get-tuple-element.67), channel_id=1, source_target_pairs={{8,0},{16,8},{24,16},{9,1},{17,9},{25,17},{10,2},{18,10},{26,18},{... | collective-permute-start | bytes 786440 | tf_op jit(solution)/shard_map/ppermute | solution.py:25
  43.0 2.2 %shard_map.158 = (bf16[4,1024,128]{2,1,0:T(8,128)(2,1)}, f32[1024,128]{1,0:T(8,128)S(1)}) custom-call(s32[4]{0:T(128)S(1)} %bitcast.20, bf16[1024,128]{1,0:T(8,128)(2,1)S(1)} %bitcast.15, bf16[4096,128]{1,0:T(8,128)(2,1)S(1)} %bitcast.13, bf16[384,128]{1,0:T(8,128)(2,1)S(1)} %copy-done.2, bf16[256,128]{1,0:T(8,128)(2,1)S(1)} %copy-done.3, ...), custom_call_target="tpu_custom_call" | custom-call | flops 1000000 | tf_op jit(solution)/shard_map/pallas_call | solution.py:437
  45.2 3.1 %collective-permute-done.6 = bf16[448,128]{1,0:T(8,128)(2,1)S(1)} collective-permute-done((bf16[448,128]{1,0:T(8,128)(2,1)S(1)}, bf16[448,128]{1,0:T(8,128)(2,1)S(1)}, u32[]{:S(2)}, u32[]{:S(2)}) %collective-permute-start.6) | collective-permute-done | bytes 114720 | tf_op jit(solution)/shard_map/ppermute | solution.py:452
  48.4 2.4 %collective-permute-start.10 = (bf16[448,128]{1,0:T(8,128)(2,1)S(1)}, bf16[448,128]{1,0:T(8,128)(2,1)S(1)}, u32[]{:S(2)}, u32[]{:S(2)}) collective-permute-start(bf16[448,128]{1,0:T(8,128)(2,1)S(1)} %convert_add_fusion.1), channel_id=1, source_target_pairs={{0,16},{1,17},{2,18},{3,19},{4,20},{5,21},{6,22},{7,23},{8,24},{9,... | collective-permute-start | bytes 344072 | tf_op jit(solution)/shard_map/ppermute | solution.py:452
  50.9 1.7 %collective-permute-start.9 = (bf16[448,128]{1,0:T(8,128)(2,1)S(1)}, bf16[448,128]{1,0:T(8,128)(2,1)S(1)}, u32[]{:S(2)}, u32[]{:S(2)}) collective-permute-start(bf16[448,128]{1,0:T(8,128)(2,1)S(1)} %convert_add_fusion.1), channel_id=1, source_target_pairs={{0,1},{1,0},{2,3},{3,2},{4,5},{5,4},{6,7},{7,6},{8,9},{9,8},{10,11... | collective-permute-start | bytes 344072 | tf_op jit(solution)/shard_map/ppermute | solution.py:452
  52.6 0.9 %convert_add_fusion = f32[1024,128]{1,0:T(8,128)} fusion(bf16[1024,128]{1,0:T(8,128)(2,1)S(1)} %collective-permute-done.8, f32[1024,128]{1,0:T(8,128)S(1)} %get-tuple-element.66, bf16[1024,128]{1,0:T(8,128)(2,1)S(1)} %collective-permute-done.12), kind=kLoop, calls=%fused_computation | loop fusion | flops 524288 | bytes 1572864 | tf_op jit(solution)/shard_map/add | solution.py:581
  53.5 0.9 %collective-permute-done.10 = bf16[448,128]{1,0:T(8,128)(2,1)S(1)} collective-permute-done((bf16[448,128]{1,0:T(8,128)(2,1)S(1)}, bf16[448,128]{1,0:T(8,128)(2,1)S(1)}, u32[]{:S(2)}, u32[]{:S(2)}) %collective-permute-start.10) | collective-permute-done | bytes 114720 | tf_op jit(solution)/shard_map/ppermute | solution.py:452
  54.4 1.5 %collective-permute-done.9 = bf16[448,128]{1,0:T(8,128)(2,1)S(1)} collective-permute-done((bf16[448,128]{1,0:T(8,128)(2,1)S(1)}, bf16[448,128]{1,0:T(8,128)(2,1)S(1)}, u32[]{:S(2)}, u32[]{:S(2)}) %collective-permute-start.9) | collective-permute-done | bytes 114720 | tf_op jit(solution)/shard_map/ppermute | solution.py:452
  55.9 2.4 %collective-permute-done.11 = bf16[448,128]{1,0:T(8,128)(2,1)S(1)} collective-permute-done((bf16[448,128]{1,0:T(8,128)(2,1)S(1)}, bf16[448,128]{1,0:T(8,128)(2,1)S(1)}, u32[]{:S(2)}, u32[]{:S(2)}) %collective-permute-start.11) | collective-permute-done | bytes 114720 | tf_op jit(solution)/shard_map/ppermute | solution.py:452
  58.4 1.3 %collective-permute-done.13.theirs = bf16[448,128]{1,0:T(8,128)(2,1)S(1)} collective-permute-done((bf16[448,128]{1,0:T(8,128)(2,1)S(1)}, bf16[448,128]{1,0:T(8,128)(2,1)S(1)}, u32[]{:S(2)}, u32[]{:S(2)}) %collective-permute-start.13) | collective-permute-done | bytes 114720 | tf_op jit(solution)/shard_map/ppermute | solution.py:452
  59.8 0.8 %shard_map.159 = (f32[384,128]{1,0:T(8,128)}, f32[128,128]{1,0:T(8,128)}, f32[256,128]{1,0:T(8,128)}, f32[128,128]{1,0:T(8,128)}) custom-call(s32[1]{0:T(128)} %bitcast.8.me, bf16[448,128]{1,0:T(8,128)(2,1)S(1)} %add_convert_fusion.1.mine, bf16[448,128]{1,0:T(8,128)(2,1)S(1)} %collective-permute-done.13.theirs), custom_call_target="tpu_custom_call" | custom-call | flops 1000000 | tf_op jit(solution)/shard_map/pallas_call | solution.py:437
  (37 shorter events, 0.9 us)
Async XLA Ops:
  0.6 13.2 %collective-permute-start.2 = (bf16[1024,128]{1,0:T(8,128)(2,1)}, bf16[1024,128]{1,0:T(8,128)(2,1)S(1)}, u32[]{:S(2)}, u32[]{:S(2)}) collective-permute-start(bf16[1024,128]{1,0:T(8,128)(2,1)} %bitcast.24), channel_id=1, source_target_pairs={{0,7},{1,0},{2,1},{3,2},{4,3},{5,4},{6,5},{7,6},{8,15},{9,8},{10,9... | collective-permute-start | bytes 786440 | tf_op jit(solution)/shard_map/ppermute | solution.py:25
  6.7 10.7 %collective-permute-start.1 = (bf16[1024,128]{1,0:T(8,128)(2,1)}, bf16[1024,128]{1,0:T(8,128)(2,1)S(1)}, u32[]{:S(2)}, u32[]{:S(2)}) collective-permute-start(bf16[1024,128]{1,0:T(8,128)(2,1)} %bitcast.25), channel_id=1, source_target_pairs={{0,1},{1,2},{2,3},{3,4},{4,5},{5,6},{6,7},{7,0},{8,9},{9,10},{10,1... | collective-permute-start | bytes 786440 | tf_op jit(solution)/shard_map/ppermute | solution.py:25
  6.7 5.2 %collective-permute-start = (bf16[1024,128]{1,0:T(8,128)(2,1)}, bf16[1024,128]{1,0:T(8,128)(2,1)S(1)}, u32[]{:S(2)}, u32[]{:S(2)}) collective-permute-start(bf16[1024,128]{1,0:T(8,128)(2,1)} %bitcast.26), channel_id=1, source_target_pairs={{0,8},{8,16},{16,24},{1,9},{9,17},{17,25},{2,10},{10,18},{18,26},{... | collective-permute-start | bytes 786440 | tf_op jit(solution)/shard_map/ppermute | solution.py:25
  8.1 3.8 %copy-start.2 = (bf16[384,128]{1,0:T(8,128)(2,1)S(1)}, bf16[384,128]{1,0:T(8,128)(2,1)}, u32[]{:S(2)}) copy-start(bf16[384,128]{1,0:T(8,128)(2,1)} %w_in.7) | copy-start | bytes 294916
  8.1 3.8 %copy-start.4 = (s32[1,1,4]{2,1,0:T(1,128)S(1)}, s32[1,1,4]{2,1,0:T(1,128)}, u32[]{:S(2)}) copy-start(s32[1,1,4]{2,1,0:T(1,128)} %param.15) | copy-start | bytes 52
  8.2 3.8 %copy-start.9 = (s32[1,1,4,1024]{3,2,1,0:T(4,128)S(1)}, s32[1,1,4,1024]{3,2,1,0:T(4,128)}, u32[]{:S(2)}) copy-start(s32[1,1,4,1024]{3,2,1,0:T(4,128)} %param.13) | copy-start | bytes 49156
  11.8 5.5 %copy-start = (bf16[1,1,4,1024,128]{4,3,2,1,0:T(8,128)(2,1)S(1)}, bf16[1,1,4,1024,128]{4,3,2,1,0:T(8,128)(2,1)}, u32[]{:S(2)}) copy-start(bf16[1,1,4,1024,128]{4,3,2,1,0:T(8,128)(2,1)} %param.17) | copy-start | bytes 3145732
  11.8 5.5 %copy-start.1 = (bf16[1,1,1024,128]{3,2,1,0:T(8,128)(2,1)S(1)}, bf16[1,1,1024,128]{3,2,1,0:T(8,128)(2,1)}, u32[]{:S(2)}) copy-start(bf16[1,1,1024,128]{3,2,1,0:T(8,128)(2,1)} %param.16) | copy-start | bytes 786436
  11.8 5.5 %copy-start.3 = (bf16[256,128]{1,0:T(8,128)(2,1)S(1)}, bf16[256,128]{1,0:T(8,128)(2,1)}, u32[]{:S(2)}) copy-start(bf16[256,128]{1,0:T(8,128)(2,1)} %wn_in.3) | copy-start | bytes 196612
  11.8 5.5 %copy-start.5 = (bf16[1,1,4,1024,128]{4,3,2,1,0:T(8,128)(2,1)S(1)}, bf16[1,1,4,1024,128]{4,3,2,1,0:T(8,128)(2,1)}, u32[]{:S(2)}) copy-start(bf16[1,1,4,1024,128]{4,3,2,1,0:T(8,128)(2,1)} %param.12) | copy-start | bytes 3145732
  11.9 5.5 %copy-start.6 = (bf16[1,1,1024,128]{3,2,1,0:T(8,128)(2,1)S(1)}, bf16[1,1,1024,128]{3,2,1,0:T(8,128)(2,1)}, u32[]{:S(2)}) copy-start(bf16[1,1,1024,128]{3,2,1,0:T(8,128)(2,1)} %param.11) | copy-start | bytes 786436
  11.9 5.5 %copy-start.7 = (bf16[128,128]{1,0:T(8,128)(2,1)S(1)}, bf16[128,128]{1,0:T(8,128)(2,1)}, u32[]{:S(2)}) copy-start(bf16[128,128]{1,0:T(8,128)(2,1)} %wn_out.1) | copy-start | bytes 98308
  11.9 5.5 %copy-start.8 = (bf16[128,128]{1,0:T(8,128)(2,1)S(1)}, bf16[128,128]{1,0:T(8,128)(2,1)}, u32[]{:S(2)}) copy-start(bf16[128,128]{1,0:T(8,128)(2,1)} %w_out.3) | copy-start | bytes 98308
  22.6 9.3 %collective-permute-start.3 = (bf16[1024,128]{1,0:T(8,128)(2,1)S(1)}, bf16[1024,128]{1,0:T(8,128)(2,1)S(1)}, u32[]{:S(2)}, u32[]{:S(2)}) collective-permute-start(bf16[1024,128]{1,0:T(8,128)(2,1)S(1)} %get-tuple-element.53), channel_id=1, source_target_pairs={{0,6},{1,3},{2,0},{3,5},{4,2},{5,7},{6,4},{7,1},{8,14},{9,11},{10,... | collective-permute-start | bytes 786440 | tf_op jit(solution)/shard_map/ppermute | solution.py:547
  31.9 4.2 %collective-permute-start.4 = (bf16[448,128]{1,0:T(8,128)(2,1)S(1)}, bf16[448,128]{1,0:T(8,128)(2,1)S(1)}, u32[]{:S(2)}, u32[]{:S(2)}) collective-permute-start(bf16[448,128]{1,0:T(8,128)(2,1)S(1)} %get-tuple-element.54), channel_id=1, source_target_pairs={{0,8},{8,0},{16,24},{24,16},{1,9},{9,1},{17,25},{25,17},{2,10},{10... | collective-permute-start | bytes 344072 | tf_op jit(solution)/shard_map/ppermute | solution.py:570
  36.1 9.1 %collective-permute-start.7 = (bf16[448,128]{1,0:T(8,128)(2,1)S(1)}, bf16[448,128]{1,0:T(8,128)(2,1)S(1)}, u32[]{:S(2)}, u32[]{:S(2)}) collective-permute-start(bf16[448,128]{1,0:T(8,128)(2,1)S(1)} %add_convert_fusion.2), channel_id=1, source_target_pairs={{0,6},{1,7},{2,4},{3,5},{4,2},{5,3},{6,0},{7,1},{8,14},{9,15},{10,... | collective-permute-start | bytes 344072 | tf_op jit(solution)/shard_map/ppermute | solution.py:452
  37.8 10.6 %collective-permute-start.6 = (bf16[448,128]{1,0:T(8,128)(2,1)S(1)}, bf16[448,128]{1,0:T(8,128)(2,1)S(1)}, u32[]{:S(2)}, u32[]{:S(2)}) collective-permute-start(bf16[448,128]{1,0:T(8,128)(2,1)S(1)} %add_convert_fusion.2), channel_id=1, source_target_pairs={{0,4},{1,5},{2,6},{3,7},{4,0},{5,1},{6,2},{7,3},{8,12},{9,13},{10,... | collective-permute-start | bytes 344072 | tf_op jit(solution)/shard_map/ppermute | solution.py:452
  37.8 10.6 %collective-permute-start.5 = (bf16[448,128]{1,0:T(8,128)(2,1)S(1)}, bf16[448,128]{1,0:T(8,128)(2,1)S(1)}, u32[]{:S(2)}, u32[]{:S(2)}) collective-permute-start(bf16[448,128]{1,0:T(8,128)(2,1)S(1)} %add_convert_fusion.2), channel_id=1, source_target_pairs={{0,2},{1,3},{2,0},{3,1},{4,6},{5,7},{6,4},{7,5},{8,10},{9,11},{10,... | collective-permute-start | bytes 344072 | tf_op jit(solution)/shard_map/ppermute | solution.py:452
  40.6 7.8 %collective-permute-start.8 = (bf16[1024,128]{1,0:T(8,128)(2,1)S(1)}, bf16[1024,128]{1,0:T(8,128)(2,1)S(1)}, u32[]{:S(2)}, u32[]{:S(2)}) collective-permute-start(bf16[1024,128]{1,0:T(8,128)(2,1)S(1)} %add_convert_fusion), channel_id=1, source_target_pairs={{0,1},{1,0},{2,3},{3,2},{4,5},{5,4},{6,7},{7,6},{8,9},{9,8},{10,11... | collective-permute-start | bytes 786440 | tf_op jit(solution)/shard_map/ppermute | solution.py:568
  41.8 10.9 %collective-permute-start.12 = (bf16[1024,128]{1,0:T(8,128)(2,1)S(1)}, bf16[1024,128]{1,0:T(8,128)(2,1)S(1)}, u32[]{:S(2)}, u32[]{:S(2)}) collective-permute-start(bf16[1024,128]{1,0:T(8,128)(2,1)S(1)} %get-tuple-element.67), channel_id=1, source_target_pairs={{8,0},{16,8},{24,16},{9,1},{17,9},{25,17},{10,2},{18,10},{26,18},{... | collective-permute-start | bytes 786440 | tf_op jit(solution)/shard_map/ppermute | solution.py:25
  48.4 6.0 %collective-permute-start.10 = (bf16[448,128]{1,0:T(8,128)(2,1)S(1)}, bf16[448,128]{1,0:T(8,128)(2,1)S(1)}, u32[]{:S(2)}, u32[]{:S(2)}) collective-permute-start(bf16[448,128]{1,0:T(8,128)(2,1)S(1)} %convert_add_fusion.1), channel_id=1, source_target_pairs={{0,16},{1,17},{2,18},{3,19},{4,20},{5,21},{6,22},{7,23},{8,24},{9,... | collective-permute-start | bytes 344072 | tf_op jit(solution)/shard_map/ppermute | solution.py:452
  50.9 5.0 %collective-permute-start.9 = (bf16[448,128]{1,0:T(8,128)(2,1)S(1)}, bf16[448,128]{1,0:T(8,128)(2,1)S(1)}, u32[]{:S(2)}, u32[]{:S(2)}) collective-permute-start(bf16[448,128]{1,0:T(8,128)(2,1)S(1)} %convert_add_fusion.1), channel_id=1, source_target_pairs={{0,1},{1,0},{2,3},{3,2},{4,5},{5,4},{6,7},{7,6},{8,9},{9,8},{10,11... | collective-permute-start | bytes 344072 | tf_op jit(solution)/shard_map/ppermute | solution.py:452
  52.6 5.7 %collective-permute-start.11 = (bf16[448,128]{1,0:T(8,128)(2,1)S(1)}, bf16[448,128]{1,0:T(8,128)(2,1)S(1)}, u32[]{:S(2)}, u32[]{:S(2)}) collective-permute-start(bf16[448,128]{1,0:T(8,128)(2,1)S(1)} %convert_add_fusion.1), channel_id=1, source_target_pairs={{0,17},{1,16},{2,19},{3,18},{4,21},{5,20},{6,23},{7,22},{8,25},{9,... | collective-permute-start | bytes 344072 | tf_op jit(solution)/shard_map/ppermute | solution.py:452
  58.4 1.4 %collective-permute-start.13 = (bf16[448,128]{1,0:T(8,128)(2,1)S(1)}, bf16[448,128]{1,0:T(8,128)(2,1)S(1)}, u32[]{:S(2)}, u32[]{:S(2)}) collective-permute-start(bf16[448,128]{1,0:T(8,128)(2,1)S(1)} %add_convert_fusion.1.mine), channel_id=1, source_target_pairs={{0,8},{1,9},{2,10},{3,11},{4,12},{5,13},{6,14},{7,15},{8,0},{9,1},... | collective-permute-start | bytes 344072 | tf_op jit(solution)/shard_map/ppermute | solution.py:452
  (1 other events, 3.8 us)

commit v5 on v4

--- a/solution.py
+++ b/solution.py
@@ -461,7 +461,6 @@
         sent = mine.astype(bf16)
         mine = sum((swap(sent, m).astype(f32) for m in masks), sent.astype(f32))
         if at == 0:
-            mine, arrived = lax.optimization_barrier((mine, arrived))
             beside = finish(arrived)
     mine, beside = lax.optimization_barrier((mine.astype(bf16), beside))
     return mine, swap(mine, sectors), beside

time: 60.4 us -> 59.1 us (0.978); the launches traced: 60.6 us -> 58.4 us
  Pallas kernels: 19.2 us -> 16.9 us
    ppermute x1, starting transfers between devices: 3.23 us -> 0.01 us  [body(): lax.ppermute(other, 'layer', [(i, i ^ 1) for i in range(layers)])]
    pallas_call x6, Pallas kernels: 19.2 us -> 16.9 us  [on_device(): pl.pallas_call(kernel, out_shape=outs, in_specs=in_specs, out_specs=[vmem...]
    ppermute x1, starting transfers between devices: 1.12 us -> 2.93 us  [body(): lax.ppermute(near_back, 'phi', [(i, i ^ 1) for i in range(sectors)])]
    ppermute x7, starting transfers between devices: 8.72 us -> 10.4 us  [swap(): return lax.ppermute(value, axes, [(i, i ^ mask) for i in range(total)])]
    ppermute x7, waiting for transfers between devices: 9.19 us -> 7.75 us  [swap(): return lax.ppermute(value, axes, [(i, i ^ mask) for i in range(total)])]
    ppermute x4, waiting for transfers between devices: 3.49 us -> 4.73 us  [shifted(): return lax.ppermute(value, axis, route)]
  transfers between devices with their start and end apart: 14 -> 14, of which waited for: 8 -> 7; matrix products, arithmetic and copies ran while one was open for 2% -> 2% of each run, Pallas kernels for 22% -> 19%
where the time goes in v5:
time: 59.1 us; the launch traced here: 58.4 us
  starting transfers between devices  25.4 us (43%)
  Pallas kernels  16.9 us (29%)
  waiting for transfers between devices  14 us (24%)
  other arithmetic  1.12 us (2%)
  between operations  0.9 us (2%)
    pallas_call x6, Pallas kernels, on_device(): pl.pallas_call(kernel, out_shape=outs, in_specs=in_specs, out_specs=[vmem...  16.9 us
    ppermute x7, starting transfers between devices, swap(): return lax.ppermute(value, axes, [(i, i ^ mask) for i in range(total)])  10.4 us
    ppermute x4, starting transfers between devices, shifted(): return lax.ppermute(value, axis, route)  8.79 us
    ppermute x7, waiting for transfers between devices, swap(): return lax.ppermute(value, axes, [(i, i ^ mask) for i in range(total)])  7.75 us
    ppermute x4, waiting for transfers between devices, shifted(): return lax.ppermute(value, axis, route)  4.73 us
    ppermute x1, starting transfers between devices, body(): relayed = lax.ppermute(far_back, 'phi', route)  3.27 us
    ppermute x1, starting transfers between devices, body(): lax.ppermute(near_back, 'phi', [(i, i ^ 1) for i in range(sectors)])  2.93 us
    ppermute x1, waiting for transfers between devices, body(): lax.ppermute(other, 'layer', [(i, i ^ 1) for i in range(layers)])  1.32 us
  transfers between devices with their start and end apart: 14, of which 7 were waited for; matrix products, arithmetic and copies ran while one was open for 2% of the time, Pallas kernels for 19%

profile of v5, /device:TPU:0, one launch (start us, length us, event | category | flops | bytes accessed | tf_op | source)
XLA Modules:
  0.0 58.4 jit_solution(16671630998340104632)
XLA Ops:
  0.6 6.0 %collective-permute-start.2 = (bf16[1024,128]{1,0:T(8,128)(2,1)}, bf16[1024,128]{1,0:T(8,128)(2,1)S(1)}, u32[]{:S(2)}, u32[]{:S(2)}) collective-permute-start(bf16[1024,128]{1,0:T(8,128)(2,1)} %bitcast.24), channel_id=1, source_target_pairs={{0,7},{1,0},{2,1},{3,2},{4,3},{5,4},{6,5},{7,6},{8,15},{9,8},{10,9... | collective-permute-start | bytes 786440 | tf_op jit(solution)/shard_map/ppermute | solution.py:25
  6.7 1.5 %collective-permute-start = (bf16[1024,128]{1,0:T(8,128)(2,1)}, bf16[1024,128]{1,0:T(8,128)(2,1)S(1)}, u32[]{:S(2)}, u32[]{:S(2)}) collective-permute-start(bf16[1024,128]{1,0:T(8,128)(2,1)} %bitcast.26), channel_id=1, source_target_pairs={{0,8},{8,16},{16,24},{1,9},{9,17},{17,25},{2,10},{10,18},{18,26},{... | collective-permute-start | bytes 786440 | tf_op jit(solution)/shard_map/ppermute | solution.py:25
  8.2 2.9 %shard_map.154.part = f32[4352,128]{1,0:T(8,128)S(1)} custom-call(s32[4]{0:T(128)} %bitcast.16, s32[4,1024]{1,0:T(4,128)} %bitcast.30, s32[4,1024]{1,0:T(4,128)} %bitcast.34, bf16[1024,128]{1,0:T(8,128)(2,1)} %bitcast.27, bf16[4096,128]{1,0:T(8,128)(2,1)} %bitcast.21, bf16[384,128]{1,0:T(8,128)(2,1)} %w_in.7), custom_call_target="tpu_custom_call" | custom-call | flops 4000000000 | tf_op jit(solution)/shard_map/pallas_call | solution.py:437
  11.2 1.4 %shard_map.155 = (f32[2304,128]{1,0:T(8,128)S(1)}, f32[2304,128]{1,0:T(8,128)S(1)}, bf16[9,128,256]{2,1,0:T(8,128)(2,1)S(1)}, f32[512,256]{1,0:T(8,128)S(1)}) custom-call(s32[4]{0:T(128)S(1)} %bitcast.17, s32[4,1024]{1,0:T(4,128)S(1)} %bitcast.31, s32[4,1024]{1,0:T(4,128)S(1)} %bitcast.35, bf16[1024,128]{1,0:T(8,128)(2,1)S(1)} %collective-permute-done.src1, ...), custom_call_target="tpu_custom_call" | custom-call | flops 2000000000 | tf_op jit(solution)/shard_map/pallas_call | solution.py:437
  12.6 4.7 %collective-permute-done.1.src2 = bf16[1024,128]{1,0:T(8,128)(2,1)S(1)} collective-permute-done((bf16[1024,128]{1,0:T(8,128)(2,1)}, bf16[1024,128]{1,0:T(8,128)(2,1)S(1)}, u32[]{:S(2)}, u32[]{:S(2)}) %collective-permute-start.1) | collective-permute-done | bytes 262176 | tf_op jit(solution)/shard_map/ppermute | solution.py:25
  17.4 5.2 %shard_map.156 = (bf16[1024,128]{1,0:T(8,128)(2,1)S(1)}, bf16[2304,128]{1,0:T(8,128)(2,1)S(1)}, f32[512,256]{1,0:T(8,128)S(1)}, bf16[1024,128]{1,0:T(8,128)(2,1)...) custom-call(s32[4]{0:T(128)S(1)} %bitcast.18, ...), custom_call_target="tpu_custom_call" | custom-call | flops 8000000000 | tf_op jit(solution)/shard_map/pallas_call | solution.py:437
  22.6 3.3 %collective-permute-start.3 = (bf16[1024,128]{1,0:T(8,128)(2,1)S(1)}, bf16[1024,128]{1,0:T(8,128)(2,1)S(1)}, u32[]{:S(2)}, u32[]{:S(2)}) collective-permute-start(bf16[1024,128]{1,0:T(8,128)(2,1)S(1)} %get-tuple-element.51), channel_id=1, source_target_pairs={{0,6},{1,3},{2,0},{3,5},{4,2},{5,7},{6,4},{7,1},{8,14},{9,11},{10,... | collective-permute-start | bytes 786440 | tf_op jit(solution)/shard_map/ppermute | solution.py:546
  25.9 4.5 %shard_map.157 = (bf16[1024,128]{1,0:T(8,128)(2,1)S(1)}, bf16[1024,128]{1,0:T(8,128)(2,1)S(1)}, bf16[2304,128]{1,0:T(8,128)(2,1)S(1)}, bf16[2304,128]{1,0:T(8,12...) custom-call(s32[4]{0:T(128)S(1)} %bitcast.19, ...), custom_call_target="tpu_custom_call" | custom-call | flops 8000000000 | tf_op jit(solution)/shard_map/pallas_call | solution.py:437
  30.4 0.2 collective-permute-done.3
  30.6 1.3 %collective-permute-done.4 = bf16[448,128]{1,0:T(8,128)(2,1)S(1)} collective-permute-done((bf16[448,128]{1,0:T(8,128)(2,1)S(1)}, bf16[448,128]{1,0:T(8,128)(2,1)S(1)}, u32[]{:S(2)}, u32[]{:S(2)}) %collective-permute-start.4) | collective-permute-done | bytes 114720 | tf_op jit(solution)/shard_map/ppermute | solution.py:569
  31.9 4.3 %collective-permute-start.7 = (bf16[448,128]{1,0:T(8,128)(2,1)S(1)}, bf16[448,128]{1,0:T(8,128)(2,1)S(1)}, u32[]{:S(2)}, u32[]{:S(2)}) collective-permute-start(bf16[448,128]{1,0:T(8,128)(2,1)S(1)} %add_convert_fusion.3), channel_id=1, source_target_pairs={{0,6},{1,7},{2,4},{3,5},{4,2},{5,3},{6,0},{7,1},{8,14},{9,15},{10,... | collective-permute-start | bytes 344072 | tf_op jit(solution)/shard_map/ppermute | solution.py:452
  36.3 0.6 %collective-permute-start.5 = (bf16[448,128]{1,0:T(8,128)(2,1)S(1)}, bf16[448,128]{1,0:T(8,128)(2,1)S(1)}, u32[]{:S(2)}, u32[]{:S(2)}) collective-permute-start(bf16[448,128]{1,0:T(8,128)(2,1)S(1)} %add_convert_fusion.3), channel_id=1, source_target_pairs={{0,2},{1,3},{2,0},{3,1},{4,6},{5,7},{6,4},{7,5},{8,10},{9,11},{10,... | collective-permute-start | bytes 344072 | tf_op jit(solution)/shard_map/ppermute | solution.py:452
  36.9 0.1 add_convert_fusion
  37.0 1.3 %collective-permute-start.11 = (bf16[1024,128]{1,0:T(8,128)(2,1)S(1)}, bf16[1024,128]{1,0:T(8,128)(2,1)S(1)}, u32[]{:S(2)}, u32[]{:S(2)}) collective-permute-start(bf16[1024,128]{1,0:T(8,128)(2,1)S(1)} %get-tuple-element.63), channel_id=1, source_target_pairs={{8,0},{16,8},{24,16},{9,1},{17,9},{25,17},{10,2},{18,10},{26,18},{... | collective-permute-start | bytes 786440 | tf_op jit(solution)/shard_map/ppermute | solution.py:25
  38.3 2.9 %collective-permute-start.12 = (bf16[1024,128]{1,0:T(8,128)(2,1)S(1)}, bf16[1024,128]{1,0:T(8,128)(2,1)S(1)}, u32[]{:S(2)}, u32[]{:S(2)}) collective-permute-start(bf16[1024,128]{1,0:T(8,128)(2,1)S(1)} %add_convert_fusion), channel_id=1, source_target_pairs={{0,1},{1,0},{2,3},{3,2},{4,5},{5,4},{6,7},{7,6},{8,9},{9,8},{10,11... | collective-permute-start | bytes 786440 | tf_op jit(solution)/shard_map/ppermute | solution.py:567
  41.2 2.2 %shard_map.158 = (bf16[4,1024,128]{2,1,0:T(8,128)(2,1)}, f32[1024,128]{1,0:T(8,128)S(1)}) custom-call(s32[4]{0:T(128)S(1)} %bitcast.20, bf16[1024,128]{1,0:T(8,128)(2,1)S(1)} %bitcast.15, bf16[4096,128]{1,0:T(8,128)(2,1)S(1)} %bitcast.13, bf16[384,128]{1,0:T(8,128)(2,1)S(1)} %copy-done.2, bf16[256,128]{1,0:T(8,128)(2,1)S(1)} %copy-done.3, ...), custom_call_target="tpu_custom_call" | custom-call | flops 1000000 | tf_op jit(solution)/shard_map/pallas_call | solution.py:437
  43.4 2.6 %collective-permute-done.6 = bf16[448,128]{1,0:T(8,128)(2,1)S(1)} collective-permute-done((bf16[448,128]{1,0:T(8,128)(2,1)S(1)}, bf16[448,128]{1,0:T(8,128)(2,1)S(1)}, u32[]{:S(2)}, u32[]{:S(2)}) %collective-permute-start.6) | collective-permute-done | bytes 114720 | tf_op jit(solution)/shard_map/ppermute | solution.py:452
  46.0 4.7 %collective-permute-start.10 = (bf16[448,128]{1,0:T(8,128)(2,1)S(1)}, bf16[448,128]{1,0:T(8,128)(2,1)S(1)}, u32[]{:S(2)}, u32[]{:S(2)}) collective-permute-start(bf16[448,128]{1,0:T(8,128)(2,1)S(1)} %add_convert_fusion.2), channel_id=1, source_target_pairs={{0,17},{1,16},{2,19},{3,18},{4,21},{5,20},{6,23},{7,22},{8,25},{9,... | collective-permute-start | bytes 344072 | tf_op jit(solution)/shard_map/ppermute | solution.py:452
  50.8 0.6 %collective-permute-start.8 = (bf16[448,128]{1,0:T(8,128)(2,1)S(1)}, bf16[448,128]{1,0:T(8,128)(2,1)S(1)}, u32[]{:S(2)}, u32[]{:S(2)}) collective-permute-start(bf16[448,128]{1,0:T(8,128)(2,1)S(1)} %add_convert_fusion.2), channel_id=1, source_target_pairs={{0,1},{1,0},{2,3},{3,2},{4,5},{5,4},{6,7},{7,6},{8,9},{9,8},{10,11... | collective-permute-start | bytes 344072 | tf_op jit(solution)/shard_map/ppermute | solution.py:452
  51.4 0.9 %convert_add_fusion = f32[1024,128]{1,0:T(8,128)} fusion(bf16[1024,128]{1,0:T(8,128)(2,1)S(1)} %collective-permute-done.12, f32[1024,128]{1,0:T(8,128)S(1)} %get-tuple-element.59, bf16[1024,128]{1,0:T(8,128)(2,1)S(1)} %collective-permute-done.11), kind=kLoop, calls=%fused_computation | loop fusion | flops 524288 | bytes 1572864 | tf_op jit(solution)/shard_map/add | solution.py:580
  52.3 1.9 %collective-permute-done.10 = bf16[448,128]{1,0:T(8,128)(2,1)S(1)} collective-permute-done((bf16[448,128]{1,0:T(8,128)(2,1)S(1)}, bf16[448,128]{1,0:T(8,128)(2,1)S(1)}, u32[]{:S(2)}, u32[]{:S(2)}) %collective-permute-start.10) | collective-permute-done | bytes 114720 | tf_op jit(solution)/shard_map/ppermute | solution.py:452
  54.3 1.9 %collective-permute-done.9 = bf16[448,128]{1,0:T(8,128)(2,1)S(1)} collective-permute-done((bf16[448,128]{1,0:T(8,128)(2,1)S(1)}, bf16[448,128]{1,0:T(8,128)(2,1)S(1)}, u32[]{:S(2)}, u32[]{:S(2)}) %collective-permute-start.9) | collective-permute-done | bytes 114720 | tf_op jit(solution)/shard_map/ppermute | solution.py:452
  56.3 1.3 %collective-permute-done.13.theirs = bf16[448,128]{1,0:T(8,128)(2,1)S(1)} collective-permute-done((bf16[448,128]{1,0:T(8,128)(2,1)S(1)}, bf16[448,128]{1,0:T(8,128)(2,1)S(1)}, u32[]{:S(2)}, u32[]{:S(2)}) %collective-permute-start.13) | collective-permute-done | bytes 114720 | tf_op jit(solution)/shard_map/ppermute | solution.py:452
  57.6 0.8 %shard_map.159 = (f32[384,128]{1,0:T(8,128)}, f32[128,128]{1,0:T(8,128)}, f32[256,128]{1,0:T(8,128)}, f32[128,128]{1,0:T(8,128)}) custom-call(s32[1]{0:T(128)} %bitcast.8.me, bf16[448,128]{1,0:T(8,128)(2,1)S(1)} %add_convert_fusion.1.mine, bf16[448,128]{1,0:T(8,128)(2,1)S(1)} %collective-permute-done.13.theirs), custom_call_target="tpu_custom_call" | custom-call | flops 1000000 | tf_op jit(solution)/shard_map/pallas_call | solution.py:437
  (37 shorter events, 0.3 us)
Async XLA Ops:
  0.6 12.0 %collective-permute-start.2 = (bf16[1024,128]{1,0:T(8,128)(2,1)}, bf16[1024,128]{1,0:T(8,128)(2,1)S(1)}, u32[]{:S(2)}, u32[]{:S(2)}) collective-permute-start(bf16[1024,128]{1,0:T(8,128)(2,1)} %bitcast.24), channel_id=1, source_target_pairs={{0,7},{1,0},{2,1},{3,2},{4,3},{5,4},{6,5},{7,6},{8,15},{9,8},{10,9... | collective-permute-start | bytes 786440 | tf_op jit(solution)/shard_map/ppermute | solution.py:25
  6.7 10.7 %collective-permute-start.1 = (bf16[1024,128]{1,0:T(8,128)(2,1)}, bf16[1024,128]{1,0:T(8,128)(2,1)S(1)}, u32[]{:S(2)}, u32[]{:S(2)}) collective-permute-start(bf16[1024,128]{1,0:T(8,128)(2,1)} %bitcast.25), channel_id=1, source_target_pairs={{0,1},{1,2},{2,3},{3,4},{4,5},{5,6},{6,7},{7,0},{8,9},{9,10},{10,1... | collective-permute-start | bytes 786440 | tf_op jit(solution)/shard_map/ppermute | solution.py:25
  6.7 4.5 %collective-permute-start = (bf16[1024,128]{1,0:T(8,128)(2,1)}, bf16[1024,128]{1,0:T(8,128)(2,1)S(1)}, u32[]{:S(2)}, u32[]{:S(2)}) collective-permute-start(bf16[1024,128]{1,0:T(8,128)(2,1)} %bitcast.26), channel_id=1, source_target_pairs={{0,8},{8,16},{16,24},{1,9},{9,17},{17,25},{2,10},{10,18},{18,26},{... | collective-permute-start | bytes 786440 | tf_op jit(solution)/shard_map/ppermute | solution.py:25
  8.1 3.0 %copy-start.2 = (bf16[384,128]{1,0:T(8,128)(2,1)S(1)}, bf16[384,128]{1,0:T(8,128)(2,1)}, u32[]{:S(2)}) copy-start(bf16[384,128]{1,0:T(8,128)(2,1)} %w_in.7) | copy-start | bytes 294916
  8.1 3.0 %copy-start.4 = (s32[1,1,4]{2,1,0:T(1,128)S(1)}, s32[1,1,4]{2,1,0:T(1,128)}, u32[]{:S(2)}) copy-start(s32[1,1,4]{2,1,0:T(1,128)} %param.15) | copy-start | bytes 52
  8.2 3.0 %copy-start.9 = (s32[1,1,4,1024]{3,2,1,0:T(4,128)S(1)}, s32[1,1,4,1024]{3,2,1,0:T(4,128)}, u32[]{:S(2)}) copy-start(s32[1,1,4,1024]{3,2,1,0:T(4,128)} %param.13) | copy-start | bytes 49156
  11.1 6.3 %copy-start = (bf16[1,1,4,1024,128]{4,3,2,1,0:T(8,128)(2,1)S(1)}, bf16[1,1,4,1024,128]{4,3,2,1,0:T(8,128)(2,1)}, u32[]{:S(2)}) copy-start(bf16[1,1,4,1024,128]{4,3,2,1,0:T(8,128)(2,1)} %param.17) | copy-start | bytes 3145732
  11.1 6.2 %copy-start.1 = (bf16[1,1,1024,128]{3,2,1,0:T(8,128)(2,1)S(1)}, bf16[1,1,1024,128]{3,2,1,0:T(8,128)(2,1)}, u32[]{:S(2)}) copy-start(bf16[1,1,1024,128]{3,2,1,0:T(8,128)(2,1)} %param.16) | copy-start | bytes 786436
  11.1 6.2 %copy-start.3 = (bf16[256,128]{1,0:T(8,128)(2,1)S(1)}, bf16[256,128]{1,0:T(8,128)(2,1)}, u32[]{:S(2)}) copy-start(bf16[256,128]{1,0:T(8,128)(2,1)} %wn_in.3) | copy-start | bytes 196612
  11.1 6.2 %copy-start.5 = (bf16[1,1,4,1024,128]{4,3,2,1,0:T(8,128)(2,1)S(1)}, bf16[1,1,4,1024,128]{4,3,2,1,0:T(8,128)(2,1)}, u32[]{:S(2)}) copy-start(bf16[1,1,4,1024,128]{4,3,2,1,0:T(8,128)(2,1)} %param.12) | copy-start | bytes 3145732
  11.1 6.2 %copy-start.6 = (bf16[1,1,1024,128]{3,2,1,0:T(8,128)(2,1)S(1)}, bf16[1,1,1024,128]{3,2,1,0:T(8,128)(2,1)}, u32[]{:S(2)}) copy-start(bf16[1,1,1024,128]{3,2,1,0:T(8,128)(2,1)} %param.11) | copy-start | bytes 786436
  11.1 6.2 %copy-start.7 = (bf16[128,128]{1,0:T(8,128)(2,1)S(1)}, bf16[128,128]{1,0:T(8,128)(2,1)}, u32[]{:S(2)}) copy-start(bf16[128,128]{1,0:T(8,128)(2,1)} %wn_out.1) | copy-start | bytes 98308
  11.2 6.2 %copy-start.8 = (bf16[128,128]{1,0:T(8,128)(2,1)S(1)}, bf16[128,128]{1,0:T(8,128)(2,1)}, u32[]{:S(2)}) copy-start(bf16[128,128]{1,0:T(8,128)(2,1)} %w_out.3) | copy-start | bytes 98308
  22.6 8.0 %collective-permute-start.3 = (bf16[1024,128]{1,0:T(8,128)(2,1)S(1)}, bf16[1024,128]{1,0:T(8,128)(2,1)S(1)}, u32[]{:S(2)}, u32[]{:S(2)}) collective-permute-start(bf16[1024,128]{1,0:T(8,128)(2,1)S(1)} %get-tuple-element.51), channel_id=1, source_target_pairs={{0,6},{1,3},{2,0},{3,5},{4,2},{5,7},{6,4},{7,1},{8,14},{9,11},{10,... | collective-permute-start | bytes 786440 | tf_op jit(solution)/shard_map/ppermute | solution.py:546
  30.6 1.3 %collective-permute-start.4 = (bf16[448,128]{1,0:T(8,128)(2,1)S(1)}, bf16[448,128]{1,0:T(8,128)(2,1)S(1)}, u32[]{:S(2)}, u32[]{:S(2)}) collective-permute-start(bf16[448,128]{1,0:T(8,128)(2,1)S(1)} %get-tuple-element.52), channel_id=1, source_target_pairs={{0,8},{8,0},{16,24},{24,16},{1,9},{9,1},{17,25},{25,17},{2,10},{10... | collective-permute-start | bytes 344072 | tf_op jit(solution)/shard_map/ppermute | solution.py:569
  31.9 11.5 %collective-permute-start.7 = (bf16[448,128]{1,0:T(8,128)(2,1)S(1)}, bf16[448,128]{1,0:T(8,128)(2,1)S(1)}, u32[]{:S(2)}, u32[]{:S(2)}) collective-permute-start(bf16[448,128]{1,0:T(8,128)(2,1)S(1)} %add_convert_fusion.3), channel_id=1, source_target_pairs={{0,6},{1,7},{2,4},{3,5},{4,2},{5,3},{6,0},{7,1},{8,14},{9,15},{10,... | collective-permute-start | bytes 344072 | tf_op jit(solution)/shard_map/ppermute | solution.py:452
  36.3 9.7 %collective-permute-start.6 = (bf16[448,128]{1,0:T(8,128)(2,1)S(1)}, bf16[448,128]{1,0:T(8,128)(2,1)S(1)}, u32[]{:S(2)}, u32[]{:S(2)}) collective-permute-start(bf16[448,128]{1,0:T(8,128)(2,1)S(1)} %add_convert_fusion.3), channel_id=1, source_target_pairs={{0,4},{1,5},{2,6},{3,7},{4,0},{5,1},{6,2},{7,3},{8,12},{9,13},{10,... | collective-permute-start | bytes 344072 | tf_op jit(solution)/shard_map/ppermute | solution.py:452
  36.3 9.7 %collective-permute-start.5 = (bf16[448,128]{1,0:T(8,128)(2,1)S(1)}, bf16[448,128]{1,0:T(8,128)(2,1)S(1)}, u32[]{:S(2)}, u32[]{:S(2)}) collective-permute-start(bf16[448,128]{1,0:T(8,128)(2,1)S(1)} %add_convert_fusion.3), channel_id=1, source_target_pairs={{0,2},{1,3},{2,0},{3,1},{4,6},{5,7},{6,4},{7,5},{8,10},{9,11},{10,... | collective-permute-start | bytes 344072 | tf_op jit(solution)/shard_map/ppermute | solution.py:452
  37.0 14.4 %collective-permute-start.11 = (bf16[1024,128]{1,0:T(8,128)(2,1)S(1)}, bf16[1024,128]{1,0:T(8,128)(2,1)S(1)}, u32[]{:S(2)}, u32[]{:S(2)}) collective-permute-start(bf16[1024,128]{1,0:T(8,128)(2,1)S(1)} %get-tuple-element.63), channel_id=1, source_target_pairs={{8,0},{16,8},{24,16},{9,1},{17,9},{25,17},{10,2},{18,10},{26,18},{... | collective-permute-start | bytes 786440 | tf_op jit(solution)/shard_map/ppermute | solution.py:25
  38.3 13.1 %collective-permute-start.12 = (bf16[1024,128]{1,0:T(8,128)(2,1)S(1)}, bf16[1024,128]{1,0:T(8,128)(2,1)S(1)}, u32[]{:S(2)}, u32[]{:S(2)}) collective-permute-start(bf16[1024,128]{1,0:T(8,128)(2,1)S(1)} %add_convert_fusion), channel_id=1, source_target_pairs={{0,1},{1,0},{2,3},{3,2},{4,5},{5,4},{6,7},{7,6},{8,9},{9,8},{10,11... | collective-permute-start | bytes 786440 | tf_op jit(solution)/shard_map/ppermute | solution.py:567
  46.0 8.2 %collective-permute-start.10 = (bf16[448,128]{1,0:T(8,128)(2,1)S(1)}, bf16[448,128]{1,0:T(8,128)(2,1)S(1)}, u32[]{:S(2)}, u32[]{:S(2)}) collective-permute-start(bf16[448,128]{1,0:T(8,128)(2,1)S(1)} %add_convert_fusion.2), channel_id=1, source_target_pairs={{0,17},{1,16},{2,19},{3,18},{4,21},{5,20},{6,23},{7,22},{8,25},{9,... | collective-permute-start | bytes 344072 | tf_op jit(solution)/shard_map/ppermute | solution.py:452
  50.8 5.4 %collective-permute-start.9 = (bf16[448,128]{1,0:T(8,128)(2,1)S(1)}, bf16[448,128]{1,0:T(8,128)(2,1)S(1)}, u32[]{:S(2)}, u32[]{:S(2)}) collective-permute-start(bf16[448,128]{1,0:T(8,128)(2,1)S(1)} %add_convert_fusion.2), channel_id=1, source_target_pairs={{0,16},{1,17},{2,18},{3,19},{4,20},{5,21},{6,22},{7,23},{8,24},{9,... | collective-permute-start | bytes 344072 | tf_op jit(solution)/shard_map/ppermute | solution.py:452
  50.8 5.4 %collective-permute-start.8 = (bf16[448,128]{1,0:T(8,128)(2,1)S(1)}, bf16[448,128]{1,0:T(8,128)(2,1)S(1)}, u32[]{:S(2)}, u32[]{:S(2)}) collective-permute-start(bf16[448,128]{1,0:T(8,128)(2,1)S(1)} %add_convert_fusion.2), channel_id=1, source_target_pairs={{0,1},{1,0},{2,3},{3,2},{4,5},{5,4},{6,7},{7,6},{8,9},{9,8},{10,11... | collective-permute-start | bytes 344072 | tf_op jit(solution)/shard_map/ppermute | solution.py:452
  56.2 1.4 %collective-permute-start.13 = (bf16[448,128]{1,0:T(8,128)(2,1)S(1)}, bf16[448,128]{1,0:T(8,128)(2,1)S(1)}, u32[]{:S(2)}, u32[]{:S(2)}) collective-permute-start(bf16[448,128]{1,0:T(8,128)(2,1)S(1)} %add_convert_fusion.1.mine), channel_id=1, source_target_pairs={{0,8},{1,9},{2,10},{3,11},{4,12},{5,13},{6,14},{7,15},{8,0},{9,1},... | collective-permute-start | bytes 344072 | tf_op jit(solution)/shard_map/ppermute | solution.py:452
  (1 other events, 3.0 us)

commit v6 on v5

--- a/solution.py
+++ b/solution.py
@@ -11,8 +11,7 @@
 bf16, f32 = jnp.bfloat16, jnp.float32
 SPAN = 256
 FOLD = 4
-FORWARD = 2
-BACKWARD = 2
+GROUP = 4
 VMEM_BYTES = 16 * 1024 * 1024
 
 
@@ -122,22 +121,26 @@
         store = jnp.where(real, row - self.first * self.cap, self.held * self.cap)
         return Place(kind, at, offset, rest, row, row - self.first * self.cap, store)
 
-    def pipelined(self, front, back, held, group):
-        steps = (self.ends[-1] + group - 1) // group
-
-        def places(i):
-            return [self.place(group * i + j) for j in range(group)]
-
-        def looped(i, carry):
-            back(places(i - 1), held[...])
-            held[...] = front(places(i))
-            return carry
-
-        @pl.when(steps > 0)
-        def _():
-            held[...] = front(places(0))
-            lax.fori_loop(1, steps, looped, 0)
-            back(places(steps - 1), held[...])
+    def pipelined(self, front, back, held):
+        even = self.ends[-1] % GROUP == 0
+        choices = ((GROUP, even), (2, ~even)) if held.shape[1] == GROUP * SPAN else ((2, True),)
+        for group, wanted in choices:
+            steps = jnp.where(wanted, (self.ends[-1] + group - 1) // group, 0)
+            now = held.at[:, : group * SPAN]
+
+            def places(i, group=group):
+                return [self.place(group * i + j) for j in range(group)]
+
+            def looped(i, carry, now=now, places=places):
+                back(places(i - 1), now[...])
+                now[...] = front(places(i))
+                return carry
+
+            @pl.when(steps > 0)
+            def _(steps=steps, now=now, places=places, looped=looped):
+                now[...] = front(places(0))
+                lax.fori_loop(1, steps, looped, 0)
+                back(places(steps - 1), now[...])
 
     def run(self, step, group=2):
         def looped(i, carry):
@@ -218,7 +221,7 @@
     def back(places, hidden):
         total[...] += Slots(slots_of(recv, places), nodes).sums(hidden)
 
-    tiles.pipelined(front, back, held, FORWARD)
+    tiles.pipelined(front, back, held)
 
 
 def local_kernel(
@@ -290,7 +293,7 @@
             part_grad = pre_grad[:, i * SPAN : (i + 1) * SPAN]
             send_sum[p.at] += Slots(p.slots(send), nodes).sums(part_grad)
 
-    tiles.pipelined(front, back, held, BACKWARD)
+    tiles.pipelined(front, back, held)
 
 
 def senders_back(send_sum, w_in):
@@ -519,7 +522,7 @@
         2 * 10**9,
         scratch=[
             pltpu.VMEM((1, nodes // FOLD, FOLD * d), bf16),
-            pltpu.VMEM((d, FORWARD * SPAN), f32),
+            pltpu.VMEM((d, 2 * SPAN), f32),
         ],
     )
     partial = shape(7 * d, d)
@@ -537,8 +540,8 @@
             pltpu.VMEM((2, nodes // FOLD, FOLD * d), bf16),
             pltpu.VMEM((1, *turned.shape), f32),
             pltpu.VMEM(turned.shape, f32),
-            pltpu.VMEM((d, FORWARD * SPAN), f32),
-            pltpu.VMEM((d, BACKWARD * SPAN), f32),
+            pltpu.VMEM((d, GROUP * SPAN), f32),
+            pltpu.VMEM((d, GROUP * SPAN), f32),
         ],
         scalars=(0, 15),
     )
@@ -557,7 +560,7 @@
         scratch=[
             pltpu.VMEM((3, *turned.shape), f32),
             pltpu.VMEM((7 * d, d), f32),
-            pltpu.VMEM((d, BACKWARD * SPAN), f32),
+            pltpu.VMEM((d, 2 * SPAN), f32),
         ],
         scalars=(0, 20, 21),
     )

time: 59.1 us -> 59.9 us (1.014); the launches traced: 58.4 us -> 60.3 us
  starting transfers between devices: 25.4 us -> 27.4 us
  waiting for transfers between devices: 14 us -> 12.2 us
  Pallas kernels: 16.9 us -> 18.6 us
    ppermute x7, waiting for transfers between devices: 7.75 us -> 5.19 us  [swap(): return lax.ppermute(value, axes, [(i, i ^ mask) for i in range(total)])]
    pallas_call x6, Pallas kernels: 16.9 us -> 18.6 us  [on_device(): pl.pallas_call(kernel, out_shape=outs, in_specs=in_specs, out_specs=[vmem...]
    ppermute x7, starting transfers between devices: 10.4 us -> 12.1 us  [swap(): return lax.ppermute(value, axes, [(i, i ^ mask) for i in range(total)])]
    ppermute x1, starting transfers between devices: 2.93 us -> 4.53 us  [body(): lax.ppermute(near_back, 'phi', [(i, i ^ 1) for i in range(sectors)])]
    ppermute x1, waiting for transfers between devices: 0.19 us -> 1.65 us  [body(): relayed = lax.ppermute(far_back, 'phi', route)]
    ppermute x1, starting transfers between devices: 3.27 us -> 1.99 us  [body(): relayed = lax.ppermute(far_back, 'phi', route)]
    ppermute x4, waiting for transfers between devices: 4.73 us -> 4 us  [shifted(): return lax.ppermute(value, axis, route)]
  transfers between devices with their start and end apart: 14 -> 14, of which waited for: 7 -> 6; matrix products, arithmetic and copies ran while one was open for 2% -> 2% of each run, Pallas kernels for 19% -> 19%
where the time goes in v6:
time: 59.9 us; the launch traced here: 60.3 us
  starting transfers between devices  27.4 us (46%)
  Pallas kernels  18.6 us (31%)
  waiting for transfers between devices  12.2 us (20%)
  other arithmetic  1.12 us (2%)
  between operations  0.91 us (2%)
    pallas_call x6, Pallas kernels, on_device(): pl.pallas_call(kernel, out_shape=outs, in_specs=in_specs, out_specs=[vmem...  18.6 us
    ppermute x7, starting transfers between devices, swap(): return lax.ppermute(value, axes, [(i, i ^ mask) for i in range(total)])  12.1 us
    ppermute x4, starting transfers between devices, shifted(): return lax.ppermute(value, axis, route)  8.79 us
    ppermute x7, waiting for transfers between devices, swap(): return lax.ppermute(value, axes, [(i, i ^ mask) for i in range(total)])  5.19 us
    ppermute x1, starting transfers between devices, body(): lax.ppermute(near_back, 'phi', [(i, i ^ 1) for i in range(sectors)])  4.53 us
    ppermute x4, waiting for transfers between devices, shifted(): return lax.ppermute(value, axis, route)  4 us
    ppermute x1, starting transfers between devices, body(): relayed = lax.ppermute(far_back, 'phi', route)  1.99 us
    ppermute x1, waiting for transfers between devices, body(): relayed = lax.ppermute(far_back, 'phi', route)  1.65 us
  transfers between devices with their start and end apart: 14, of which 6 were waited for; matrix products, arithmetic and copies ran while one was open for 2% of the time, Pallas kernels for 19%

profile of v6, /device:TPU:0, one launch (start us, length us, event | category | flops | bytes accessed | tf_op | source)
XLA Modules:
  0.0 60.3 jit_solution(1096595590577349563)
XLA Ops:
  0.6 6.0 %collective-permute-start.2 = (bf16[1024,128]{1,0:T(8,128)(2,1)}, bf16[1024,128]{1,0:T(8,128)(2,1)S(1)}, u32[]{:S(2)}, u32[]{:S(2)}) collective-permute-start(bf16[1024,128]{1,0:T(8,128)(2,1)} %bitcast.24), channel_id=1, source_target_pairs={{0,7},{1,0},{2,1},{3,2},{4,3},{5,4},{6,5},{7,6},{8,15},{9,8},{10,9... | collective-permute-start | bytes 786440 | tf_op jit(solution)/shard_map/ppermute | solution.py:24
  6.7 1.5 %collective-permute-start = (bf16[1024,128]{1,0:T(8,128)(2,1)}, bf16[1024,128]{1,0:T(8,128)(2,1)S(1)}, u32[]{:S(2)}, u32[]{:S(2)}) collective-permute-start(bf16[1024,128]{1,0:T(8,128)(2,1)} %bitcast.26), channel_id=1, source_target_pairs={{0,8},{8,16},{16,24},{1,9},{9,17},{17,25},{2,10},{10,18},{18,26},{... | collective-permute-start | bytes 786440 | tf_op jit(solution)/shard_map/ppermute | solution.py:24
  8.2 3.6 %shard_map.154.part = f32[4352,128]{1,0:T(8,128)S(1)} custom-call(s32[4]{0:T(128)} %bitcast.16, s32[4,1024]{1,0:T(4,128)} %bitcast.30, s32[4,1024]{1,0:T(4,128)} %bitcast.34, bf16[1024,128]{1,0:T(8,128)(2,1)} %bitcast.27, bf16[4096,128]{1,0:T(8,128)(2,1)} %bitcast.21, bf16[384,128]{1,0:T(8,128)(2,1)} %w_in.7), custom_call_target="tpu_custom_call" | custom-call | flops 4000000000 | tf_op jit(solution)/shard_map/pallas_call | solution.py:440
  11.9 1.4 %shard_map.155 = (f32[2304,128]{1,0:T(8,128)S(1)}, f32[2304,128]{1,0:T(8,128)S(1)}, bf16[9,128,256]{2,1,0:T(8,128)(2,1)S(1)}, f32[512,256]{1,0:T(8,128)S(1)}) custom-call(s32[4]{0:T(128)S(1)} %bitcast.17, s32[4,1024]{1,0:T(4,128)S(1)} %bitcast.31, s32[4,1024]{1,0:T(4,128)S(1)} %bitcast.35, bf16[1024,128]{1,0:T(8,128)(2,1)S(1)} %collective-permute-done.src1, ...), custom_call_target="tpu_custom_call" | custom-call | flops 2000000000 | tf_op jit(solution)/shard_map/pallas_call | solution.py:440
  13.3 4.0 %collective-permute-done.1.src2 = bf16[1024,128]{1,0:T(8,128)(2,1)S(1)} collective-permute-done((bf16[1024,128]{1,0:T(8,128)(2,1)}, bf16[1024,128]{1,0:T(8,128)(2,1)S(1)}, u32[]{:S(2)}, u32[]{:S(2)}) %collective-permute-start.1) | collective-permute-done | bytes 262176 | tf_op jit(solution)/shard_map/ppermute | solution.py:24
  17.4 6.4 %shard_map.156 = (bf16[1024,128]{1,0:T(8,128)(2,1)S(1)}, bf16[2304,128]{1,0:T(8,128)(2,1)S(1)}, f32[512,256]{1,0:T(8,128)S(1)}, bf16[1024,128]{1,0:T(8,128)(2,1)...) custom-call(s32[4]{0:T(128)S(1)} %bitcast.18, ...), custom_call_target="tpu_custom_call" | custom-call | flops 8000000000 | tf_op jit(solution)/shard_map/pallas_call | solution.py:440
  23.8 2.0 %collective-permute-start.3 = (bf16[1024,128]{1,0:T(8,128)(2,1)S(1)}, bf16[1024,128]{1,0:T(8,128)(2,1)S(1)}, u32[]{:S(2)}, u32[]{:S(2)}) collective-permute-start(bf16[1024,128]{1,0:T(8,128)(2,1)S(1)} %get-tuple-element.51), channel_id=1, source_target_pairs={{0,6},{1,3},{2,0},{3,5},{4,2},{5,7},{6,4},{7,1},{8,14},{9,11},{10,... | collective-permute-start | bytes 786440 | tf_op jit(solution)/shard_map/ppermute | solution.py:549
  25.8 4.3 %shard_map.157 = (bf16[1024,128]{1,0:T(8,128)(2,1)S(1)}, bf16[1024,128]{1,0:T(8,128)(2,1)S(1)}, bf16[2304,128]{1,0:T(8,128)(2,1)S(1)}, bf16[2304,128]{1,0:T(8,12...) custom-call(s32[4]{0:T(128)S(1)} %bitcast.19, ...), custom_call_target="tpu_custom_call" | custom-call | flops 8000000000 | tf_op jit(solution)/shard_map/pallas_call | solution.py:440
  30.1 1.7 %collective-permute-done.3 = bf16[1024,128]{1,0:T(8,128)(2,1)S(1)} collective-permute-done((bf16[1024,128]{1,0:T(8,128)(2,1)S(1)}, bf16[1024,128]{1,0:T(8,128)(2,1)S(1)}, u32[]{:S(2)}, u32[]{:S(2)}) %collective-permute-start.3) | collective-permute-done | bytes 262176 | tf_op jit(solution)/shard_map/ppermute | solution.py:549
  31.7 1.3 %collective-permute-done.4 = bf16[448,128]{1,0:T(8,128)(2,1)S(1)} collective-permute-done((bf16[448,128]{1,0:T(8,128)(2,1)S(1)}, bf16[448,128]{1,0:T(8,128)(2,1)S(1)}, u32[]{:S(2)}, u32[]{:S(2)}) %collective-permute-start.4) | collective-permute-done | bytes 114720 | tf_op jit(solution)/shard_map/ppermute | solution.py:572
  33.1 4.3 %collective-permute-start.7 = (bf16[448,128]{1,0:T(8,128)(2,1)S(1)}, bf16[448,128]{1,0:T(8,128)(2,1)S(1)}, u32[]{:S(2)}, u32[]{:S(2)}) collective-permute-start(bf16[448,128]{1,0:T(8,128)(2,1)S(1)} %add_convert_fusion.3), channel_id=1, source_target_pairs={{0,6},{1,7},{2,4},{3,5},{4,2},{5,3},{6,0},{7,1},{8,14},{9,15},{10,... | collective-permute-start | bytes 344072 | tf_op jit(solution)/shard_map/ppermute | solution.py:455
  37.4 0.6 %collective-permute-start.5 = (bf16[448,128]{1,0:T(8,128)(2,1)S(1)}, bf16[448,128]{1,0:T(8,128)(2,1)S(1)}, u32[]{:S(2)}, u32[]{:S(2)}) collective-permute-start(bf16[448,128]{1,0:T(8,128)(2,1)S(1)} %add_convert_fusion.3), channel_id=1, source_target_pairs={{0,2},{1,3},{2,0},{3,1},{4,6},{5,7},{6,4},{7,5},{8,10},{9,11},{10,... | collective-permute-start | bytes 344072 | tf_op jit(solution)/shard_map/ppermute | solution.py:455
  38.1 0.1 add_convert_fusion
  38.2 1.3 %collective-permute-start.11 = (bf16[1024,128]{1,0:T(8,128)(2,1)S(1)}, bf16[1024,128]{1,0:T(8,128)(2,1)S(1)}, u32[]{:S(2)}, u32[]{:S(2)}) collective-permute-start(bf16[1024,128]{1,0:T(8,128)(2,1)S(1)} %get-tuple-element.63), channel_id=1, source_target_pairs={{8,0},{16,8},{24,16},{9,1},{17,9},{25,17},{10,2},{18,10},{26,18},{... | collective-permute-start | bytes 786440 | tf_op jit(solution)/shard_map/ppermute | solution.py:24
  39.5 4.5 %collective-permute-start.12 = (bf16[1024,128]{1,0:T(8,128)(2,1)S(1)}, bf16[1024,128]{1,0:T(8,128)(2,1)S(1)}, u32[]{:S(2)}, u32[]{:S(2)}) collective-permute-start(bf16[1024,128]{1,0:T(8,128)(2,1)S(1)} %add_convert_fusion), channel_id=1, source_target_pairs={{0,1},{1,0},{2,3},{3,2},{4,5},{5,4},{6,7},{7,6},{8,9},{9,8},{10,11... | collective-permute-start | bytes 786440 | tf_op jit(solution)/shard_map/ppermute | solution.py:570
  44.0 2.2 %shard_map.158 = (bf16[4,1024,128]{2,1,0:T(8,128)(2,1)}, f32[1024,128]{1,0:T(8,128)S(1)}) custom-call(s32[4]{0:T(128)S(1)} %bitcast.20, bf16[1024,128]{1,0:T(8,128)(2,1)S(1)} %bitcast.15, bf16[4096,128]{1,0:T(8,128)(2,1)S(1)} %bitcast.13, bf16[384,128]{1,0:T(8,128)(2,1)S(1)} %copy-done.2, bf16[256,128]{1,0:T(8,128)(2,1)S(1)} %copy-done.3, ...), custom_call_target="tpu_custom_call" | custom-call | flops 1000000 | tf_op jit(solution)/shard_map/pallas_call | solution.py:440
  46.2 6.4 %collective-permute-start.10 = (bf16[448,128]{1,0:T(8,128)(2,1)S(1)}, bf16[448,128]{1,0:T(8,128)(2,1)S(1)}, u32[]{:S(2)}, u32[]{:S(2)}) collective-permute-start(bf16[448,128]{1,0:T(8,128)(2,1)S(1)} %add_convert_fusion.2), channel_id=1, source_target_pairs={{0,17},{1,16},{2,19},{3,18},{4,21},{5,20},{6,23},{7,22},{8,25},{9,... | collective-permute-start | bytes 344072 | tf_op jit(solution)/shard_map/ppermute | solution.py:455
  52.6 0.6 %collective-permute-start.8 = (bf16[448,128]{1,0:T(8,128)(2,1)S(1)}, bf16[448,128]{1,0:T(8,128)(2,1)S(1)}, u32[]{:S(2)}, u32[]{:S(2)}) collective-permute-start(bf16[448,128]{1,0:T(8,128)(2,1)S(1)} %add_convert_fusion.2), channel_id=1, source_target_pairs={{0,1},{1,0},{2,3},{3,2},{4,5},{5,4},{6,7},{7,6},{8,9},{9,8},{10,11... | collective-permute-start | bytes 344072 | tf_op jit(solution)/shard_map/ppermute | solution.py:455
  53.3 0.9 %convert_add_fusion = f32[1024,128]{1,0:T(8,128)} fusion(bf16[1024,128]{1,0:T(8,128)(2,1)S(1)} %collective-permute-done.12, f32[1024,128]{1,0:T(8,128)S(1)} %get-tuple-element.59, bf16[1024,128]{1,0:T(8,128)(2,1)S(1)} %collective-permute-done.11), kind=kLoop, calls=%fused_computation | loop fusion | flops 524288 | bytes 1572864 | tf_op jit(solution)/shard_map/add | solution.py:583
  54.2 1.9 %collective-permute-done.10 = bf16[448,128]{1,0:T(8,128)(2,1)S(1)} collective-permute-done((bf16[448,128]{1,0:T(8,128)(2,1)S(1)}, bf16[448,128]{1,0:T(8,128)(2,1)S(1)}, u32[]{:S(2)}, u32[]{:S(2)}) %collective-permute-start.10) | collective-permute-done | bytes 114720 | tf_op jit(solution)/shard_map/ppermute | solution.py:455
  56.1 1.9 %collective-permute-done.9 = bf16[448,128]{1,0:T(8,128)(2,1)S(1)} collective-permute-done((bf16[448,128]{1,0:T(8,128)(2,1)S(1)}, bf16[448,128]{1,0:T(8,128)(2,1)S(1)}, u32[]{:S(2)}, u32[]{:S(2)}) %collective-permute-start.9) | collective-permute-done | bytes 114720 | tf_op jit(solution)/shard_map/ppermute | solution.py:455
  58.1 0.1 collective-permute-start.13
  58.2 1.3 %collective-permute-done.13.theirs = bf16[448,128]{1,0:T(8,128)(2,1)S(1)} collective-permute-done((bf16[448,128]{1,0:T(8,128)(2,1)S(1)}, bf16[448,128]{1,0:T(8,128)(2,1)S(1)}, u32[]{:S(2)}, u32[]{:S(2)}) %collective-permute-start.13) | collective-permute-done | bytes 114720 | tf_op jit(solution)/shard_map/ppermute | solution.py:455
  59.5 0.8 %shard_map.159 = (f32[384,128]{1,0:T(8,128)}, f32[128,128]{1,0:T(8,128)}, f32[256,128]{1,0:T(8,128)}, f32[128,128]{1,0:T(8,128)}) custom-call(s32[1]{0:T(128)} %bitcast.8.me, bf16[448,128]{1,0:T(8,128)(2,1)S(1)} %add_convert_fusion.1.mine, bf16[448,128]{1,0:T(8,128)(2,1)S(1)} %collective-permute-done.13.theirs), custom_call_target="tpu_custom_call" | custom-call | flops 1000000 | tf_op jit(solution)/shard_map/pallas_call | solution.py:440
  (37 shorter events, 0.3 us)
Async XLA Ops:
  0.6 12.7 %collective-permute-start.2 = (bf16[1024,128]{1,0:T(8,128)(2,1)}, bf16[1024,128]{1,0:T(8,128)(2,1)S(1)}, u32[]{:S(2)}, u32[]{:S(2)}) collective-permute-start(bf16[1024,128]{1,0:T(8,128)(2,1)} %bitcast.24), channel_id=1, source_target_pairs={{0,7},{1,0},{2,1},{3,2},{4,3},{5,4},{6,5},{7,6},{8,15},{9,8},{10,9... | collective-permute-start | bytes 786440 | tf_op jit(solution)/shard_map/ppermute | solution.py:24
  6.7 10.7 %collective-permute-start.1 = (bf16[1024,128]{1,0:T(8,128)(2,1)}, bf16[1024,128]{1,0:T(8,128)(2,1)S(1)}, u32[]{:S(2)}, u32[]{:S(2)}) collective-permute-start(bf16[1024,128]{1,0:T(8,128)(2,1)} %bitcast.25), channel_id=1, source_target_pairs={{0,1},{1,2},{2,3},{3,4},{4,5},{5,6},{6,7},{7,0},{8,9},{9,10},{10,1... | collective-permute-start | bytes 786440 | tf_op jit(solution)/shard_map/ppermute | solution.py:24
  6.7 5.2 %collective-permute-start = (bf16[1024,128]{1,0:T(8,128)(2,1)}, bf16[1024,128]{1,0:T(8,128)(2,1)S(1)}, u32[]{:S(2)}, u32[]{:S(2)}) collective-permute-start(bf16[1024,128]{1,0:T(8,128)(2,1)} %bitcast.26), channel_id=1, source_target_pairs={{0,8},{8,16},{16,24},{1,9},{9,17},{17,25},{2,10},{10,18},{18,26},{... | collective-permute-start | bytes 786440 | tf_op jit(solution)/shard_map/ppermute | solution.py:24
  8.1 3.8 %copy-start.2 = (bf16[384,128]{1,0:T(8,128)(2,1)S(1)}, bf16[384,128]{1,0:T(8,128)(2,1)}, u32[]{:S(2)}) copy-start(bf16[384,128]{1,0:T(8,128)(2,1)} %w_in.7) | copy-start | bytes 294916
  8.1 3.8 %copy-start.4 = (s32[1,1,4]{2,1,0:T(1,128)S(1)}, s32[1,1,4]{2,1,0:T(1,128)}, u32[]{:S(2)}) copy-start(s32[1,1,4]{2,1,0:T(1,128)} %param.15) | copy-start | bytes 52
  8.2 3.8 %copy-start.9 = (s32[1,1,4,1024]{3,2,1,0:T(4,128)S(1)}, s32[1,1,4,1024]{3,2,1,0:T(4,128)}, u32[]{:S(2)}) copy-start(s32[1,1,4,1024]{3,2,1,0:T(4,128)} %param.13) | copy-start | bytes 49156
  11.8 5.5 %copy-start = (bf16[1,1,4,1024,128]{4,3,2,1,0:T(8,128)(2,1)S(1)}, bf16[1,1,4,1024,128]{4,3,2,1,0:T(8,128)(2,1)}, u32[]{:S(2)}) copy-start(bf16[1,1,4,1024,128]{4,3,2,1,0:T(8,128)(2,1)} %param.17) | copy-start | bytes 3145732
  11.8 5.5 %copy-start.1 = (bf16[1,1,1024,128]{3,2,1,0:T(8,128)(2,1)S(1)}, bf16[1,1,1024,128]{3,2,1,0:T(8,128)(2,1)}, u32[]{:S(2)}) copy-start(bf16[1,1,1024,128]{3,2,1,0:T(8,128)(2,1)} %param.16) | copy-start | bytes 786436
  11.8 5.5 %copy-start.3 = (bf16[256,128]{1,0:T(8,128)(2,1)S(1)}, bf16[256,128]{1,0:T(8,128)(2,1)}, u32[]{:S(2)}) copy-start(bf16[256,128]{1,0:T(8,128)(2,1)} %wn_in.3) | copy-start | bytes 196612
  11.8 5.5 %copy-start.5 = (bf16[1,1,4,1024,128]{4,3,2,1,0:T(8,128)(2,1)S(1)}, bf16[1,1,4,1024,128]{4,3,2,1,0:T(8,128)(2,1)}, u32[]{:S(2)}) copy-start(bf16[1,1,4,1024,128]{4,3,2,1,0:T(8,128)(2,1)} %param.12) | copy-start | bytes 3145732
  11.9 5.5 %copy-start.6 = (bf16[1,1,1024,128]{3,2,1,0:T(8,128)(2,1)S(1)}, bf16[1,1,1024,128]{3,2,1,0:T(8,128)(2,1)}, u32[]{:S(2)}) copy-start(bf16[1,1,1024,128]{3,2,1,0:T(8,128)(2,1)} %param.11) | copy-start | bytes 786436
  11.9 5.5 %copy-start.7 = (bf16[128,128]{1,0:T(8,128)(2,1)S(1)}, bf16[128,128]{1,0:T(8,128)(2,1)}, u32[]{:S(2)}) copy-start(bf16[128,128]{1,0:T(8,128)(2,1)} %wn_out.1) | copy-start | bytes 98308
  11.9 5.5 %copy-start.8 = (bf16[128,128]{1,0:T(8,128)(2,1)S(1)}, bf16[128,128]{1,0:T(8,128)(2,1)}, u32[]{:S(2)}) copy-start(bf16[128,128]{1,0:T(8,128)(2,1)} %w_out.3) | copy-start | bytes 98308
  23.8 8.0 %collective-permute-start.3 = (bf16[1024,128]{1,0:T(8,128)(2,1)S(1)}, bf16[1024,128]{1,0:T(8,128)(2,1)S(1)}, u32[]{:S(2)}, u32[]{:S(2)}) collective-permute-start(bf16[1024,128]{1,0:T(8,128)(2,1)S(1)} %get-tuple-element.51), channel_id=1, source_target_pairs={{0,6},{1,3},{2,0},{3,5},{4,2},{5,7},{6,4},{7,1},{8,14},{9,11},{10,... | collective-permute-start | bytes 786440 | tf_op jit(solution)/shard_map/ppermute | solution.py:549
  31.7 1.3 %collective-permute-start.4 = (bf16[448,128]{1,0:T(8,128)(2,1)S(1)}, bf16[448,128]{1,0:T(8,128)(2,1)S(1)}, u32[]{:S(2)}, u32[]{:S(2)}) collective-permute-start(bf16[448,128]{1,0:T(8,128)(2,1)S(1)} %get-tuple-element.52), channel_id=1, source_target_pairs={{0,8},{8,0},{16,24},{24,16},{1,9},{9,1},{17,25},{25,17},{2,10},{10... | collective-permute-start | bytes 344072 | tf_op jit(solution)/shard_map/ppermute | solution.py:572
  33.1 13.1 %collective-permute-start.7 = (bf16[448,128]{1,0:T(8,128)(2,1)S(1)}, bf16[448,128]{1,0:T(8,128)(2,1)S(1)}, u32[]{:S(2)}, u32[]{:S(2)}) collective-permute-start(bf16[448,128]{1,0:T(8,128)(2,1)S(1)} %add_convert_fusion.3), channel_id=1, source_target_pairs={{0,6},{1,7},{2,4},{3,5},{4,2},{5,3},{6,0},{7,1},{8,14},{9,15},{10,... | collective-permute-start | bytes 344072 | tf_op jit(solution)/shard_map/ppermute | solution.py:455
  37.4 8.7 %collective-permute-start.6 = (bf16[448,128]{1,0:T(8,128)(2,1)S(1)}, bf16[448,128]{1,0:T(8,128)(2,1)S(1)}, u32[]{:S(2)}, u32[]{:S(2)}) collective-permute-start(bf16[448,128]{1,0:T(8,128)(2,1)S(1)} %add_convert_fusion.3), channel_id=1, source_target_pairs={{0,4},{1,5},{2,6},{3,7},{4,0},{5,1},{6,2},{7,3},{8,12},{9,13},{10,... | collective-permute-start | bytes 344072 | tf_op jit(solution)/shard_map/ppermute | solution.py:455
  37.4 8.7 %collective-permute-start.5 = (bf16[448,128]{1,0:T(8,128)(2,1)S(1)}, bf16[448,128]{1,0:T(8,128)(2,1)S(1)}, u32[]{:S(2)}, u32[]{:S(2)}) collective-permute-start(bf16[448,128]{1,0:T(8,128)(2,1)S(1)} %add_convert_fusion.3), channel_id=1, source_target_pairs={{0,2},{1,3},{2,0},{3,1},{4,6},{5,7},{6,4},{7,5},{8,10},{9,11},{10,... | collective-permute-start | bytes 344072 | tf_op jit(solution)/shard_map/ppermute | solution.py:455
  38.2 15.1 %collective-permute-start.11 = (bf16[1024,128]{1,0:T(8,128)(2,1)S(1)}, bf16[1024,128]{1,0:T(8,128)(2,1)S(1)}, u32[]{:S(2)}, u32[]{:S(2)}) collective-permute-start(bf16[1024,128]{1,0:T(8,128)(2,1)S(1)} %get-tuple-element.63), channel_id=1, source_target_pairs={{8,0},{16,8},{24,16},{9,1},{17,9},{25,17},{10,2},{18,10},{26,18},{... | collective-permute-start | bytes 786440 | tf_op jit(solution)/shard_map/ppermute | solution.py:24
  39.5 13.8 %collective-permute-start.12 = (bf16[1024,128]{1,0:T(8,128)(2,1)S(1)}, bf16[1024,128]{1,0:T(8,128)(2,1)S(1)}, u32[]{:S(2)}, u32[]{:S(2)}) collective-permute-start(bf16[1024,128]{1,0:T(8,128)(2,1)S(1)} %add_convert_fusion), channel_id=1, source_target_pairs={{0,1},{1,0},{2,3},{3,2},{4,5},{5,4},{6,7},{7,6},{8,9},{9,8},{10,11... | collective-permute-start | bytes 786440 | tf_op jit(solution)/shard_map/ppermute | solution.py:570
  46.2 9.9 %collective-permute-start.10 = (bf16[448,128]{1,0:T(8,128)(2,1)S(1)}, bf16[448,128]{1,0:T(8,128)(2,1)S(1)}, u32[]{:S(2)}, u32[]{:S(2)}) collective-permute-start(bf16[448,128]{1,0:T(8,128)(2,1)S(1)} %add_convert_fusion.2), channel_id=1, source_target_pairs={{0,17},{1,16},{2,19},{3,18},{4,21},{5,20},{6,23},{7,22},{8,25},{9,... | collective-permute-start | bytes 344072 | tf_op jit(solution)/shard_map/ppermute | solution.py:455
  52.6 5.4 %collective-permute-start.9 = (bf16[448,128]{1,0:T(8,128)(2,1)S(1)}, bf16[448,128]{1,0:T(8,128)(2,1)S(1)}, u32[]{:S(2)}, u32[]{:S(2)}) collective-permute-start(bf16[448,128]{1,0:T(8,128)(2,1)S(1)} %add_convert_fusion.2), channel_id=1, source_target_pairs={{0,16},{1,17},{2,18},{3,19},{4,20},{5,21},{6,22},{7,23},{8,24},{9,... | collective-permute-start | bytes 344072 | tf_op jit(solution)/shard_map/ppermute | solution.py:455
  52.6 5.4 %collective-permute-start.8 = (bf16[448,128]{1,0:T(8,128)(2,1)S(1)}, bf16[448,128]{1,0:T(8,128)(2,1)S(1)}, u32[]{:S(2)}, u32[]{:S(2)}) collective-permute-start(bf16[448,128]{1,0:T(8,128)(2,1)S(1)} %add_convert_fusion.2), channel_id=1, source_target_pairs={{0,1},{1,0},{2,3},{3,2},{4,5},{5,4},{6,7},{7,6},{8,9},{9,8},{10,11... | collective-permute-start | bytes 344072 | tf_op jit(solution)/shard_map/ppermute | solution.py:455
  58.1 1.4 %collective-permute-start.13 = (bf16[448,128]{1,0:T(8,128)(2,1)S(1)}, bf16[448,128]{1,0:T(8,128)(2,1)S(1)}, u32[]{:S(2)}, u32[]{:S(2)}) collective-permute-start(bf16[448,128]{1,0:T(8,128)(2,1)S(1)} %add_convert_fusion.1.mine), channel_id=1, source_target_pairs={{0,8},{1,9},{2,10},{3,11},{4,12},{5,13},{6,14},{7,15},{8,0},{9,1},... | collective-permute-start | bytes 344072 | tf_op jit(solution)/shard_map/ppermute | solution.py:455
  (1 other events, 3.8 us)
